TPU v7x, 512 devices: a whole 4x4x16 slice. The times are simulated.
512 devices in a mesh: seq: 128 (over y, z, core), fsdp: 4 (over x).
Axes of the slice: x: 4, y: 4, z: 16, core: 2. Of those that a mesh axis runs over, the one named last changes fastest.
Arguments:
- queries: bfloat16 [16384, 4096], P('seq', 'fsdp'), may hold values from -6 to 6
- keys: bfloat16 [16384, 4096], P('seq', 'fsdp'), may hold values from -6 to 6
- values: bfloat16 [16384, 4096], P('seq', 'fsdp'), may hold values from -6 to 6
- grad_out: bfloat16 [16384, 4096], P('seq', 'fsdp'), may hold values from -16 to 16
- norm_gain: float32 [4096], P('fsdp'), may hold values from 0.3 to 20
- norm_bias: float32 [4096], P('fsdp'), may hold values from -8 to 8
- first_moment: float32 [2, 4096], P(None, 'fsdp'), may hold values from -500 to 500
- second_moment: float32 [2, 4096], P(None, 'fsdp'), may hold values from 10000 to 1000000
Outputs:
- grad_queries: bfloat16 [16384, 4096], P('seq', 'fsdp')
- grad_keys: bfloat16 [16384, 4096], P('seq', 'fsdp')
- grad_values: bfloat16 [16384, 4096], P('seq', 'fsdp')
- new_gain: float32 [4096], P('fsdp')
- new_bias: float32 [4096], P('fsdp')
All inputs are finite; a program needn't handle non-finite values.
Results may differ from a plain program's by a relative error of at most 0.0075.
Values sent between devices are 32-bit elements; how exact they have to be, the bound alone decides.
No kernel may reach another device: no remote copies, remote signals or barrier semaphores. Data moves between devices by JAX's collectives and lax.ppermute only.
A program may use at most 192 MiB of HBM per device.

v0:
```python
import jax
import jax.numpy as jnp
from jax import lax
from jax.sharding import PartitionSpec as P

HEAD_DIM = 128
SPAN = 128


BETA_ONE = 0.9
BETA_TWO = 0.999
ADAM_EPS = 1e-06
DECAY_RATE = 0.01
LEARN_RATE = 0.2
NORM_EPS = 1e-05
TRUST_EPS = 1e-06
CORRECT_ONE = 1.0 - 0.9**10
CORRECT_TWO = 1.0 - 0.999**10


def group_norm_grads(output, grad_f, gain):
    center = output - jnp.mean(output, axis=-1, keepdims=True)
    inv_std = lax.rsqrt(jnp.mean(center * center, axis=-1, keepdims=True) + NORM_EPS)
    normed = center * inv_std
    scaled = grad_f * gain
    d_out = inv_std * (
        scaled
        - jnp.mean(scaled, axis=-1, keepdims=True)
        - normed * jnp.mean(scaled * normed, axis=-1, keepdims=True)
    )
    return (normed, d_out)


def lamb_direction(weight, grad, first, second):
    first_new = BETA_ONE * first + (1.0 - BETA_ONE) * grad
    second_new = BETA_TWO * second + (1.0 - BETA_TWO) * grad * grad
    return (
        first_new / CORRECT_ONE / (jnp.sqrt(second_new / CORRECT_TWO) + ADAM_EPS)
        + DECAY_RATE * weight
    )


def as_slices(state, members):
    return state.reshape(members, state.size // members)


def per_device(queries, keys, values, grad_out, norm_gain, norm_bias, first_moment, second_moment):
    tok_rows, col_width = queries.shape
    heads_here = col_width // HEAD_DIM
    blocks = tok_rows // SPAN
    members = lax.axis_size("seq")
    shape_four = (blocks, SPAN, heads_here, HEAD_DIM)
    query_b = queries.reshape(shape_four)
    key_b = keys.reshape(shape_four)
    value_b = values.reshape(shape_four)
    causal = jnp.arange(SPAN)[:, None] >= jnp.arange(SPAN)[None, :]
    pair_terms = jnp.einsum("cjhd,cjhe->chde", key_b, value_b, preferred_element_type=jnp.float32)
    pair_total = jnp.sum(pair_terms, axis=0)
    landed = lax.all_to_all(
        as_slices(pair_total, members), "seq", split_axis=0, concat_axis=0, tiled=True
    )
    before_slices = jnp.cumsum(landed, axis=0) - landed
    earlier = lax.all_to_all(before_slices, "seq", split_axis=0, concat_axis=0, tiled=True).reshape(
        pair_total.shape
    )
    states = earlier[None] + jnp.cumsum(pair_terms, axis=0) - pair_terms
    state_b = states.astype(jnp.bfloat16)
    scores = jnp.einsum("cihd,cjhd->chij", query_b, key_b, preferred_element_type=jnp.float32)
    weights = jnp.where(causal, scores, 0.0).astype(jnp.bfloat16)
    output = jnp.einsum(
        "chij,cjhe->cihe", weights, value_b, preferred_element_type=jnp.float32
    ) + jnp.einsum("cihd,chde->cihe", query_b, state_b, preferred_element_type=jnp.float32)
    gain = norm_gain.reshape(heads_here, HEAD_DIM)
    grad_f = grad_out.reshape(shape_four).astype(jnp.float32)
    normed, d_out = group_norm_grads(output, grad_f, gain)
    grad_gain = jnp.sum(grad_f * normed, axis=(0, 1)).reshape(-1)
    grad_bias = jnp.sum(grad_f, axis=(0, 1)).reshape(-1)
    dout_b = d_out.astype(jnp.bfloat16)
    later_terms = jnp.einsum("cihd,cihe->chde", query_b, dout_b, preferred_element_type=jnp.float32)
    own_total = jnp.sum(later_terms, axis=0)
    arrived = lax.all_to_all(
        as_slices(own_total, members), "seq", split_axis=0, concat_axis=0, tiled=True
    )
    after_slices = jnp.sum(arrived, axis=0, keepdims=True) - jnp.cumsum(arrived, axis=0)
    after = lax.all_to_all(after_slices, "seq", split_axis=0, concat_axis=0, tiled=True).reshape(
        own_total.shape
    )
    later_states = after[None] + own_total[None] - jnp.cumsum(later_terms, axis=0)
    later_b = later_states.astype(jnp.bfloat16)
    grad_w = jnp.where(
        causal,
        jnp.einsum("cihe,cjhe->chij", dout_b, value_b, preferred_element_type=jnp.float32),
        0.0,
    ).astype(jnp.bfloat16)
    grad_q = jnp.einsum(
        "chij,cjhd->cihd", grad_w, key_b, preferred_element_type=jnp.float32
    ) + jnp.einsum("cihe,chde->cihd", dout_b, state_b, preferred_element_type=jnp.float32)
    grad_k = jnp.einsum(
        "chij,cihd->cjhd", grad_w, query_b, preferred_element_type=jnp.float32
    ) + jnp.einsum("cjhe,chde->cjhd", value_b, later_b, preferred_element_type=jnp.float32)
    grad_v = jnp.einsum(
        "chij,cihe->cjhe", weights, dout_b, preferred_element_type=jnp.float32
    ) + jnp.einsum("cjhd,chde->cjhe", key_b, later_b, preferred_element_type=jnp.float32)
    summed = lax.psum((grad_gain, grad_bias), "seq")
    gain_step = lamb_direction(norm_gain, summed[0], first_moment[0], second_moment[0])
    bias_step = lamb_direction(norm_bias, summed[1], first_moment[1], second_moment[1])
    totals = lax.psum(
        (
            jnp.sum(norm_gain * norm_gain),
            jnp.sum(gain_step * gain_step),
            jnp.sum(norm_bias * norm_bias),
            jnp.sum(bias_step * bias_step),
        ),
        "fsdp",
    )
    new_gain = (
        norm_gain - LEARN_RATE * jnp.sqrt(totals[0]) / jnp.sqrt(totals[1] + TRUST_EPS) * gain_step
    )
    new_bias = (
        norm_bias - LEARN_RATE * jnp.sqrt(totals[2]) / jnp.sqrt(totals[3] + TRUST_EPS) * bias_step
    )
    return (
        grad_q.reshape(tok_rows, col_width).astype(jnp.bfloat16),
        grad_k.reshape(tok_rows, col_width).astype(jnp.bfloat16),
        grad_v.reshape(tok_rows, col_width).astype(jnp.bfloat16),
        new_gain,
        new_bias,
    )


def solution(mesh):
    return jax.shard_map(
        per_device,
        mesh=mesh,
        in_specs=(
            P("seq", "fsdp"),
            P("seq", "fsdp"),
            P("seq", "fsdp"),
            P("seq", "fsdp"),
            P("fsdp"),
            P("fsdp"),
            P(None, "fsdp"),
            P(None, "fsdp"),
        ),
        out_specs=(P("seq", "fsdp"), P("seq", "fsdp"), P("seq", "fsdp"), P("fsdp"), P("fsdp")),
        check_vma=False,
    )
```

profile of v0, /device:TPU:1, one launch (start us, length us, event | category | flops | bytes accessed | tf_op | source)
XLA Modules:
  0.0 438.1 jit_solution(6779706149331185834)
XLA Ops:
  0.6 1.0 copy.89
  2.1 53.6 %all_to_all.30 = f32[128,1,1024]{2,1,0:T(1,128)S(1)} all-to-all(f32[128,1,1024]{2,1,0:T(1,128)S(1)} %bitcast.131), channel_id=1, replica_groups=mesh['seq'=128,'fsdp'=4] {'seq'}, dimensions={0} | all-to-all | bytes 1048576 | tf_op jit(solution)/shard_map/all_to_all | solution.py:59
  55.7 0.4 fusion.50
  56.1 1.3 sub.60
  57.4 7.3 %all-to-all-start.1 = ((f32[128,1,1024]{2,1,0:T(1,128)}), f32[128,1,1024]{2,1,0:T(1,128)S(1)}, u32[]{:S(2)}, u32[]{:S(2)}) async-start(f32[128,1,1024]{2,1,0:T(1,128)} %sub.60), calls=%async_computation.1 | async-start | bytes 1048576 | tf_op jit(solution)/shard_map/all_to_all | solution.py:63
  64.9 0.8 copy-done.1
  65.8 0.3 fusion.4
  66.1 31.9 %all-to-all-done.1 = f32[128,1,1024]{2,1,0:T(1,128)S(1)} async-done(((f32[128,1,1024]{2,1,0:T(1,128)}), f32[128,1,1024]{2,1,0:T(1,128)S(1)}, u32[]{:S(2)}, u32[]{:S(2)}) %all-to-all-start.1) | async-done | bytes 524320 | tf_op jit(solution)/shard_map/all_to_all | solution.py:63
  98.0 0.3 fusion.23
  98.3 0.3 fusion.49
  98.8 0.7 copy-done.6
  99.5 0.4 multiply_reduce_fusion
  100.3 1.0 copy.73
  101.3 7.2 %all-to-all-start.2 = ((f32[128,1,1024]{2,1,0:T(1,128)}), f32[128,1,1024]{2,1,0:T(1,128)S(1)}, u32[]{:S(2)}, u32[]{:S(2)}) async-start(f32[128,1,1024]{2,1,0:T(1,128)} %bitcast.15), calls=%async_computation.2 | async-start | bytes 1048576 | tf_op jit(solution)/shard_map/all_to_all | solution.py:81
  108.5 33.2 %all-to-all-done.2 = f32[128,1,1024]{2,1,0:T(1,128)S(1)} async-done(((f32[128,1,1024]{2,1,0:T(1,128)}), f32[128,1,1024]{2,1,0:T(1,128)S(1)}, u32[]{:S(2)}, u32[]{:S(2)}) %all-to-all-start.2) | async-done | bytes 524320 | tf_op jit(solution)/shard_map/all_to_all | solution.py:81
  141.7 0.3 reduce_sum.111
  142.0 1.2 broadcast_subtract_fusion
  143.3 7.3 %all-to-all-start.3 = ((f32[128,1,1024]{2,1,0:T(1,128)}), f32[128,1,1024]{2,1,0:T(1,128)S(1)}, u32[]{:S(2)}, u32[]{:S(2)}) async-start(f32[128,1,1024]{2,1,0:T(1,128)} %broadcast_subtract_fusion), calls=%async_computation.3 | async-start | bytes 1048576 | tf_op jit(solution)/shard_map/all_to_all | solution.py:85
  150.6 0.7 copy-done.9
  151.3 267.5 %all-reduce = (f32[1024]{0:T(1024)S(1)}, f32[1024]{0:T(1024)S(1)}) all-reduce(f32[1024]{0:T(1024)S(1)} %bitcast.142, f32[1024]{0:T(1024)S(1)} %convert_reduce_fusion), channel_id=1, replica_groups=mesh['seq'=128,'fsdp'=4] {'seq'}, use_global_device_ids=true, to_apply=%region_10.11 | all-reduce | flops 2048 | bytes 16384 | tf_op jit(solution)/shard_map/psum | solution.py:104
  418.8 0.7 copy-done.7
  419.4 0.6 multiply_reduce_fusion.4
  420.1 9.2 %all-reduce.1 = (f32[]{:T(128)}, f32[]{:T(128)}, f32[]{:T(128)}, f32[]{:T(128)}) all-reduce(f32[]{:T(128)} %get-tuple-element.43, f32[]{:T(128)} %get-tuple-element.44, f32[]{:T(128)} %get-tuple-element.37, f32[]{:T(128)} %get-tuple-element.29), channel_id=1, replica_groups=mesh['seq'=128,'fsdp'=4] {'fsdp'}, use_global_device_ids=true, to_apply=%region_8.9 | all-reduce | flops 4 | bytes 32 | tf_op jit(solution)/shard_map/psum | solution.py:107
  429.2 0.3 fusion.5
  429.8 0.3 fusion.8
  430.1 0.9 copy.79
  433.8 0.6 multiply_subtract_fusion.1
  434.4 0.6 multiply_subtract_fusion
  435.4 0.3 fusion.13
  436.1 0.9 copy.80
  436.9 0.3 fusion.6
  437.2 0.9 copy.81
  (36 shorter events, 2.3 us)
Async XLA Ops:
  0.6 1.3 copy-start
  57.4 7.3 %copy-start.2 = (bf16[128,1024]{1,0:T(8,128)(2,1)S(1)}, bf16[128,1024]{1,0:T(8,128)(2,1)}, u32[]{:S(2)}) copy-start(bf16[128,1024]{1,0:T(8,128)(2,1)} %param.11) | copy-start | bytes 786436
  57.4 40.5 %all-to-all-start.1 = ((f32[128,1,1024]{2,1,0:T(1,128)}), f32[128,1,1024]{2,1,0:T(1,128)S(1)}, u32[]{:S(2)}, u32[]{:S(2)}) async-start(f32[128,1,1024]{2,1,0:T(1,128)} %sub.60), calls=%async_computation.1 | async-start | bytes 1048576 | tf_op jit(solution)/shard_map/all_to_all | solution.py:63
  64.7 1.0 copy-start.1
  64.8 1.0 copy-start.3
  66.1 32.3 %copy-start.4 = (bf16[8,128,128]{2,1,0:T(8,128)(2,1)}, bf16[8,128,128]{2,1,0:T(8,128)(2,1)S(1)}, u32[]{:S(2)}) copy-start(bf16[8,128,128]{2,1,0:T(8,128)(2,1)S(1)} %fusion.4) | copy-start | bytes 786436
  98.8 0.7 copy-start.6
  101.3 40.4 %all-to-all-start.2 = ((f32[128,1,1024]{2,1,0:T(1,128)}), f32[128,1,1024]{2,1,0:T(1,128)S(1)}, u32[]{:S(2)}, u32[]{:S(2)}) async-start(f32[128,1,1024]{2,1,0:T(1,128)} %bitcast.15), calls=%async_computation.2 | async-start | bytes 1048576 | tf_op jit(solution)/shard_map/all_to_all | solution.py:81
  143.2 7.3 %copy-start.8 = (f32[2,1024]{1,0:T(2,128)S(1)}, f32[2,1024]{1,0:T(2,128)}, u32[]{:S(2)}) copy-start(f32[2,1024]{1,0:T(2,128)} %param.15) | copy-start | bytes 24580
  143.3 291.9 %all-to-all-start.3 = ((f32[128,1,1024]{2,1,0:T(1,128)}), f32[128,1,1024]{2,1,0:T(1,128)S(1)}, u32[]{:S(2)}, u32[]{:S(2)}) async-start(f32[128,1,1024]{2,1,0:T(1,128)} %broadcast_subtract_fusion), calls=%async_computation.3 | async-start | bytes 1048576 | tf_op jit(solution)/shard_map/all_to_all | solution.py:85
  150.6 0.7 copy-start.9
  418.7 0.7 copy-start.7
  430.1 4.9 %copy-start.5 = (bf16[8,128,128]{2,1,0:T(8,128)(2,1)S(1)}, bf16[8,128,128]{2,1,0:T(8,128)(2,1)}, u32[]{:S(2)}) copy-start(bf16[8,128,128]{2,1,0:T(8,128)(2,1)} %copy-done.4) | copy-start | bytes 786436
where the time goes:
time: 439 us; the launch traced here: 438 us
  blocking collectives  330 us (75%)
  waiting for transfers between devices  65 us (15%)
  starting transfers between devices  21.7 us (5%)
  local copies, waits for them, and re-layouts  8.05 us (2%)
  other arithmetic  6.02 us (1%)
    psum x1, blocking collectives, per_device(): summed = lax.psum((grad_gain, grad_bias), 'seq')  267 us
    all_to_all x1, blocking collectives, per_device(): lax.all_to_all(as_slices(pair_total, members), 'seq', split_axis=0, conca...  53.6 us
    all_to_all x1, waiting for transfers between devices, per_device(): lax.all_to_all(as_slices(own_total, members), 'seq', split_axis=0, concat...  33.2 us
    all_to_all x1, waiting for transfers between devices, per_device(): lax.all_to_all(before_slices, 'seq', split_axis=0, concat_axis=0, tiled=T...  31.9 us
    psum x1, blocking collectives, per_device(): lax.psum((jnp.sum(norm_gain * norm_gain), jnp.sum(gain_step * gain_step),...  9.16 us
  transfers between devices with their start and end apart: 3, of which 2 were waited for; matrix products, arithmetic and copies ran while one was open for 1% of the time, Pallas kernels for 0%

commit v1 on v0

v1 whole, which is shorter than its diff:
```python
import functools

import jax
import jax.numpy as jnp
from jax import lax
from jax.experimental import pallas as pl
from jax.experimental.pallas import tpu as pltpu
from jax.sharding import Mesh
from jax.sharding import PartitionSpec as P

HEAD_DIM = 128
HEADS_HERE = 8
HALF = HEADS_HERE // 2
CORES = 2

BETA_ONE = 0.9
BETA_TWO = 0.999
ADAM_EPS = 1e-06
DECAY_RATE = 0.01
LEARN_RATE = 0.2
NORM_EPS = 1e-05
TRUST_EPS = 1e-06
CORRECT_ONE = 1.0 - 0.9**10
CORRECT_TWO = 1.0 - 0.999**10

F32 = jnp.float32
BF16 = jnp.bfloat16


def dot(a, b, da, db):
    return lax.dot_general(a, b, (((da,), (db,)), ((), ())), preferred_element_type=F32)


def cols(head):
    return pl.ds(pl.multiple_of(head * HEAD_DIM, HEAD_DIM), HEAD_DIM)


def causal_mask():
    row = lax.broadcasted_iota(jnp.int32, (HEAD_DIM, HEAD_DIM), 0)
    col = lax.broadcasted_iota(jnp.int32, (HEAD_DIM, HEAD_DIM), 1)
    return row >= col


def pair_kernel(core_ref, k_ref, v_ref, mine_ref, send_ref):
    core = core_ref[0]
    for out, half in ((send_ref, 1 - core), (mine_ref, core)):
        for j in range(HALF):
            at = cols(half * HALF + j)
            out[j] = dot(k_ref[:, at], v_ref[:, at], 0, 0)


def local_kernel(q_ref, k_ref, v_ref, w_ref, loc_ref):
    causal = causal_mask()
    for h in range(HEADS_HERE):
        at = slice(h * HEAD_DIM, (h + 1) * HEAD_DIM)
        scores = dot(q_ref[:, at], k_ref[:, at], 1, 1)
        w = jnp.where(causal, scores, 0.0).astype(BF16)
        w_ref[h] = w
        loc_ref[:, at] = dot(w, v_ref[:, at], 1, 0)


def scan_kernel(reverse, x_ref, o_ref):
    n = x_ref.shape[0]
    total = jnp.zeros(x_ref.shape[1:], F32)
    for i in reversed(range(n)) if reverse else range(n):
        o_ref[i] = total
        total = total + x_ref[i]


def norm_kernel(core_ref, q_ref, g_ref, gain_ref, loc_ref, own_ref, far_ref, state_ref, dout_ref, mine_ref, send_ref, grads_ref):
    core = core_ref[0]
    for half, source, out in ((core, own_ref, mine_ref), (1 - core, far_ref, send_ref)):
        for j in range(HALF):
            head = half * HALF + j
            at = cols(head)
            state = source[j].astype(BF16)
            state_ref[head] = state
            q = q_ref[:, at]
            output = loc_ref[:, at] + dot(q, state, 1, 0)
            center = output - jnp.mean(output, axis=-1, keepdims=True)
            inv_std = lax.rsqrt(jnp.mean(center * center, axis=-1, keepdims=True) + NORM_EPS)
            normed = center * inv_std
            grad_f = g_ref[:, at].astype(F32)
            scaled = grad_f * gain_ref[:, at]
            d_out = inv_std * (
                scaled
                - jnp.mean(scaled, axis=-1, keepdims=True)
                - normed * jnp.mean(scaled * normed, axis=-1, keepdims=True)
            )
            dout = d_out.astype(BF16)
            dout_ref[:, at] = dout
            out[j] = dot(q, dout, 0, 0)
            grads_ref[0:1, at] = jnp.sum(grad_f * normed, axis=0, keepdims=True)
            grads_ref[1:2, at] = jnp.sum(grad_f, axis=0, keepdims=True)


def near_kernel(q_ref, k_ref, v_ref, dout_ref, w_ref, state_ref, gq_ref, gk_ref, gv_ref):
    causal = causal_mask()
    for h in range(HEADS_HERE):
        at = slice(h * HEAD_DIM, (h + 1) * HEAD_DIM)
        dout = dout_ref[:, at]
        gw = jnp.where(causal, dot(dout, v_ref[:, at], 1, 1), 0.0).astype(BF16)
        gq_ref[:, at] = (dot(gw, k_ref[:, at], 1, 0) + dot(dout, state_ref[h], 1, 1)).astype(BF16)
        gk_ref[:, at] = dot(gw, q_ref[:, at], 0, 0)
        gv_ref[:, at] = dot(w_ref[h], dout, 0, 0)


def far_kernel(core_ref, k_ref, v_ref, gk_loc_ref, gv_loc_ref, own_ref, far_ref, gk_ref, gv_ref):
    core = core_ref[0]
    for half, source in ((core, own_ref), (1 - core, far_ref)):
        for j in range(HALF):
            at = cols(half * HALF + j)
            later = source[j].astype(BF16)
            gk_ref[:, at] = (gk_loc_ref[:, at] + dot(v_ref[:, at], later, 1, 1)).astype(BF16)
            gv_ref[:, at] = (gv_loc_ref[:, at] + dot(k_ref[:, at], later, 1, 0)).astype(BF16)


def call(kernel, outs, *args, scalar=False):
    vmem = pl.BlockSpec(memory_space=pltpu.VMEM)
    specs = [vmem] * len(args)
    if scalar:
        specs[0] = pl.BlockSpec(memory_space=pltpu.SMEM)
    return pl.pallas_call(
        kernel,
        out_shape=[jax.ShapeDtypeStruct(s, d) for s, d in outs],
        in_specs=specs,
        out_specs=[vmem] * len(outs),
        compiler_params=pltpu.CompilerParams(vmem_limit_bytes=32 * 1024 * 1024),
    )(*args)


def lamb_direction(weight, grad, first, second):
    first_new = BETA_ONE * first + (1.0 - BETA_ONE) * grad
    second_new = BETA_TWO * second + (1.0 - BETA_TWO) * grad * grad
    return (
        first_new / CORRECT_ONE / (jnp.sqrt(second_new / CORRECT_TWO) + ADAM_EPS)
        + DECAY_RATE * weight
    )


HALF_STATE = (HALF, HEAD_DIM, HEAD_DIM)


def swap(array):
    return lax.ppermute(array, "core", [(0, 1), (1, 0)])


def chip_scan(mine, arrived, reverse):
    chips = lax.axis_size("y") * lax.axis_size("z")
    pair = (mine + arrived).reshape(chips, -1, HEAD_DIM)
    landed = lax.all_to_all(pair, ("y", "z"), 0, 0, tiled=True)
    (sums,) = call(functools.partial(scan_kernel, reverse), [(landed.shape, F32)], landed)
    return lax.all_to_all(sums, ("y", "z"), 0, 0, tiled=True).reshape(HALF_STATE)


def per_device(queries, keys, values, grad_out, norm_gain, norm_bias, first_moment, second_moment):
    rows, width = queries.shape
    wide = (rows, width)
    states = (HEADS_HERE, HEAD_DIM, HEAD_DIM)
    core = lax.axis_index("core")
    core_s = core.astype(jnp.int32).reshape(1)

    mine, send = call(pair_kernel, [(HALF_STATE, F32)] * 2, core_s, keys, values, scalar=True)
    arrived = swap(send)
    weights, local = call(local_kernel, [(states, BF16), (wide, F32)], queries, keys, values)
    before = chip_scan(mine, arrived, False)
    far = swap(jnp.where(core == 0, before + mine, before))
    own = jnp.where(core == 1, before + arrived, before)

    state_b, dout, mine, send, grads = call(
        norm_kernel,
        [(states, BF16), (wide, BF16), (HALF_STATE, F32), (HALF_STATE, F32), ((2, width), F32)],
        core_s, queries, grad_out, norm_gain.reshape(1, width), local, own, far, scalar=True,
    )
    arrived = swap(send)
    grad_q, gk_loc, gv_loc = call(
        near_kernel, [(wide, BF16), (wide, F32), (wide, F32)], queries, keys, values, dout, weights, state_b
    )
    summed = lax.psum(lax.psum(lax.psum(grads, "core"), "z"), "y")
    after = chip_scan(mine, arrived, True)
    far = swap(jnp.where(core == 1, after + mine, after))
    own = jnp.where(core == 0, after + arrived, after)
    grad_k, grad_v = call(
        far_kernel, [(wide, BF16)] * 2, core_s, keys, values, gk_loc, gv_loc, own, far, scalar=True
    )

    weight = jnp.stack([norm_gain, norm_bias])
    step = lamb_direction(weight, summed, first_moment, second_moment)
    totals = jnp.stack([jnp.sum(weight * weight, axis=1), jnp.sum(step * step, axis=1)])
    totals = jnp.sum(lax.all_gather(totals, "fsdp"), axis=0)
    ratio = jnp.sqrt(totals[0]) / jnp.sqrt(totals[1] + TRUST_EPS)
    new = weight - LEARN_RATE * ratio[:, None] * step
    return grad_q, grad_k, grad_v, new[0], new[1]


def solution(mesh):
    seq, fsdp = mesh.devices.shape
    fine = Mesh(mesh.devices.reshape(4, seq // (4 * CORES), CORES, fsdp), ("y", "z", "core", "fsdp"))
    rows = ("y", "z", "core")
    big = P(rows, "fsdp")
    return jax.shard_map(
        per_device,
        mesh=fine,
        in_specs=(big, big, big, big, P("fsdp"), P("fsdp"), P(None, "fsdp"), P(None, "fsdp")),
        out_specs=(big, big, big, P("fsdp"), P("fsdp")),
        check_vma=False,
    )
```

time: 439 us -> 183 us (0.42)
  blocking collectives: 330 us -> 106 us
  waiting for transfers between devices: 65 us -> 20.8 us
  starting transfers between devices: 21.7 us -> 44.2 us
  Pallas kernels: 0 us -> 7.41 us
  other arithmetic: 6.02 us -> 0.49 us
  local copies, waits for them, and re-layouts: 8.05 us -> 3.19 us
    psum x2 -> x3, blocking collectives: 277 us -> 39.1 us  [per_device(): summed = lax.psum(lax.psum(lax.psum(grads, 'core'), 'z'), 'y')]
    all_to_all x3 -> x2, waiting for transfers between devices: 65 us -> 18.2 us  [chip_scan(): lax.all_to_all(sums, ('y', 'z'), 0, 0, tiled=True).reshape(HALF_STATE)]
    ppermute x0 -> x4, starting transfers between devices: none -> 30.4 us  [swap(): return lax.ppermute(array, 'core', [(0, 1), (1, 0)])]
    all_to_all x3 -> x2, starting transfers between devices: 21.7 us -> 13.8 us  [chip_scan(): lax.all_to_all(sums, ('y', 'z'), 0, 0, tiled=True).reshape(HALF_STATE)]
    all_gather x0 -> x1, blocking collectives: none -> 7.71 us  [per_device(): totals = jnp.sum(lax.all_gather(totals, 'fsdp'), axis=0)]
    pallas_call x0 -> x7, Pallas kernels: none -> 7.41 us  [call(): pl.pallas_call(kernel, out_shape=[jax.ShapeDtypeStruct(s, d) for s, d in...]
    all_to_all x1 -> x2, blocking collectives: 53.6 us -> 58.8 us  [chip_scan(): landed = lax.all_to_all(pair, ('y', 'z'), 0, 0, tiled=True)]
  transfers between devices with their start and end apart: 3 -> 6, of which waited for: 2 -> 3; matrix products, arithmetic and copies ran while one was open for 1% -> 0% of each run, Pallas kernels for 0% -> 2%
where the time goes in v1:
time: 183 us
  blocking collectives  106 us (58%)
  starting transfers between devices  44.2 us (24%)
  waiting for transfers between devices  20.8 us (11%)
  Pallas kernels  7.41 us (4%)
  local copies, waits for them, and re-layouts  3.19 us (2%)
    all_to_all x2, blocking collectives, chip_scan(): landed = lax.all_to_all(pair, ('y', 'z'), 0, 0, tiled=True)  58.8 us
    psum x3, blocking collectives, per_device(): summed = lax.psum(lax.psum(lax.psum(grads, 'core'), 'z'), 'y')  39.1 us
    ppermute x4, starting transfers between devices, swap(): return lax.ppermute(array, 'core', [(0, 1), (1, 0)])  30.4 us
    all_to_all x2, waiting for transfers between devices, chip_scan(): lax.all_to_all(sums, ('y', 'z'), 0, 0, tiled=True).reshape(HALF_STATE)  18.2 us
    all_to_all x2, starting transfers between devices, chip_scan(): lax.all_to_all(sums, ('y', 'z'), 0, 0, tiled=True).reshape(HALF_STATE)  13.8 us
    all_gather x1, blocking collectives, per_device(): totals = jnp.sum(lax.all_gather(totals, 'fsdp'), axis=0)  7.71 us
    pallas_call x7, Pallas kernels, call(): pl.pallas_call(kernel, out_shape=[jax.ShapeDtypeStruct(s, d) for s, d in...  7.41 us
  transfers between devices with their start and end apart: 6, of which 3 were waited for; matrix products, arithmetic and copies ran while one was open for 0% of the time, Pallas kernels for 2%

profile of v1, /device:TPU:1, one launch (start us, length us, event | category | flops | bytes accessed | tf_op | source)
XLA Modules:
  0.0 182.6 jit_solution(1088532828887185359)
XLA Ops:
  0.6 0.0 copy-start
  0.6 0.9 copy-done
  1.6 0.9 copy-done.2
  2.5 0.3 shard_map.120
  2.8 8.8 %collective-permute-start = (f32[4,128,128]{2,1,0:T(8,128)S(1)}, f32[4,128,128]{2,1,0:T(8,128)S(1)}, u32[]{:S(2)}, u32[]{:S(2)}) collective-permute-start(f32[4,128,128]{2,1,0:T(8,128)S(1)} %get-tuple-element.21), channel_id=1, source_target_pairs={{0,4},{4,0},{1,5},{5,1},{2,6},{6,2},{3,7},{7,3},{8,12},{12,8},{9,1... | collective-permute-start | bytes 786440 | tf_op jit(solution)/shard_map/ppermute | solution.py:145
  11.6 1.1 collective-permute-done
  12.8 32.7 %all_to_all.20.x_ref = f32[64,8,128]{2,1,0:T(8,128)S(1)} all-to-all(f32[64,8,128]{2,1,0:T(8,128)S(1)} %bitcast.24), channel_id=1, replica_groups=mesh['y'=4,'z'=16,'core'=2,'fsdp'=4] {'y','z'}, dimensions={0} | all-to-all | bytes 524288 | tf_op jit(solution)/shard_map/all_to_all | solution.py:151
  45.5 0.8 shard_map.121
  46.2 7.0 %all-to-all-start.1 = ((f32[64,8,128]{2,1,0:T(8,128)}), f32[64,8,128]{2,1,0:T(8,128)S(1)}, u32[]{:S(2)}, u32[]{:S(2)}) async-start(f32[64,8,128]{2,1,0:T(8,128)} %shard_map.121), calls=%async_computation.1 | async-start | bytes 524288 | tf_op jit(solution)/shard_map/all_to_all | solution.py:153
  53.2 18.2 %all-to-all-done.1 = f32[64,8,128]{2,1,0:T(8,128)S(1)} async-done(((f32[64,8,128]{2,1,0:T(8,128)}), f32[64,8,128]{2,1,0:T(8,128)S(1)}, u32[]{:S(2)}, u32[]{:S(2)}) %all-to-all-start.1) | async-done | bytes 262176 | tf_op jit(solution)/shard_map/all_to_all | solution.py:153
  71.5 0.0 copy-start.5
  71.5 5.8 %collective-permute-start.1 = (f32[4,128,128]{2,1,0:T(8,128)S(1)}, f32[4,128,128]{2,1,0:T(8,128)S(1)}, u32[]{:S(2)}, u32[]{:S(2)}) collective-permute-start(f32[4,128,128]{2,1,0:T(8,128)S(1)} %get-tuple-element.37), channel_id=1, source_target_pairs={{0,4},{4,0},{1,5},{5,1},{2,6},{6,2},{3,7},{7,3},{8,12},{12,8},{9,1... | collective-permute-start | bytes 786440 | tf_op jit(solution)/shard_map/ppermute | solution.py:145
  77.4 1.3 shard_map.119
  78.7 0.0 copy-start.6
  78.7 0.7 copy-done.6
  79.4 1.0 shard_map.122
  80.4 1.9 %collective-permute-start.2 = (f32[4,128,128]{2,1,0:T(8,128)S(1)}, f32[4,128,128]{2,1,0:T(8,128)S(1)}, u32[]{:S(2)}, u32[]{:S(2)}) collective-permute-start(f32[4,128,128]{2,1,0:T(8,128)S(1)} %get-tuple-element.29), channel_id=1, source_target_pairs={{0,4},{4,0},{1,5},{5,1},{2,6},{6,2},{3,7},{7,3},{8,12},{12,8},{9,1... | collective-permute-start | bytes 786440 | tf_op jit(solution)/shard_map/ppermute | solution.py:145
  82.3 1.5 collective-permute-done.2
  83.9 26.1 %all_to_all.21.x_ref = f32[64,8,128]{2,1,0:T(8,128)S(1)} all-to-all(f32[64,8,128]{2,1,0:T(8,128)S(1)} %bitcast.25), channel_id=1, replica_groups=mesh['y'=4,'z'=16,'core'=2,'fsdp'=4] {'y','z'}, dimensions={0} | all-to-all | bytes 524288 | tf_op jit(solution)/shard_map/all_to_all | solution.py:151
  110.0 0.8 shard_map.124
  110.8 6.8 %all-to-all-start.3 = ((f32[64,8,128]{2,1,0:T(8,128)}), f32[64,8,128]{2,1,0:T(8,128)S(1)}, u32[]{:S(2)}, u32[]{:S(2)}) async-start(f32[64,8,128]{2,1,0:T(8,128)} %shard_map.124), calls=%async_computation.3 | async-start | bytes 524288 | tf_op jit(solution)/shard_map/all_to_all | solution.py:153
  117.6 3.7 %psum.21 = f32[2,1024]{1,0:T(2,128)S(1)} all-reduce(f32[2,1024]{1,0:T(2,128)S(1)} %get-tuple-element.32), channel_id=1, replica_groups=mesh['y'=4,'z'=16,'core'=2,'fsdp'=4] {'core'}, use_global_device_ids=true, to_apply=%region_1.2 | all-reduce | flops 2048 | bytes 16384 | tf_op jit(solution)/shard_map/psum | solution.py:179
  121.3 26.8 %psum.22 = f32[2,1024]{1,0:T(2,128)S(1)} all-reduce(f32[2,1024]{1,0:T(2,128)S(1)} %psum.21), channel_id=1, replica_groups=mesh['y'=4,'z'=16,'core'=2,'fsdp'=4] {'z'}, use_global_device_ids=true, to_apply=%region_2.3 | all-reduce | flops 2048 | bytes 16384 | tf_op jit(solution)/shard_map/psum | solution.py:179
  148.0 8.7 %psum.23 = f32[2,1024]{1,0:T(2,128)S(1)} all-reduce(f32[2,1024]{1,0:T(2,128)S(1)} %psum.22), channel_id=1, replica_groups=mesh['y'=4,'z'=16,'core'=2,'fsdp'=4] {'y'}, use_global_device_ids=true, to_apply=%region_3.4 | all-reduce | flops 2048 | bytes 16384 | tf_op jit(solution)/shard_map/psum | solution.py:179
  156.8 0.2 multiply_reduce_fusion
  157.0 7.7 %all-gather.1 = f32[4,2,2]{2,1,0:T(2,128)S(1)} all-gather(f32[1,2,2]{2,1,0:T(2,128)S(1)} %maximum_bitcast_fusion), channel_id=2, replica_groups=mesh['y'=4,'z'=16,'core'=2,'fsdp'=4] {'fsdp'}, dimensions={0}, use_global_device_ids=true | all-gather | bytes 80 | tf_op jit(solution)/shard_map/all_gather | solution.py:190
  164.7 0.1 add_select_fusion
  164.8 13.9 %collective-permute-start.3 = (f32[4,128,128]{2,1,0:T(8,128)S(1)}, f32[4,128,128]{2,1,0:T(8,128)S(1)}, u32[]{:S(2)}, u32[]{:S(2)}) collective-permute-start(f32[4,128,128]{2,1,0:T(8,128)S(1)} %get-tuple-element.35), channel_id=1, source_target_pairs={{0,4},{4,0},{1,5},{5,1},{2,6},{6,2},{3,7},{7,3},{8,12},{12,8},{9,1... | collective-permute-start | bytes 786440 | tf_op jit(solution)/shard_map/ppermute | solution.py:145
  178.6 0.1 multiply_subtract_fusion
  178.7 2.1 %shard_map.123 = (bf16[128,1024]{1,0:T(8,128)(2,1)}, f32[128,1024]{1,0:T(8,128)S(1)}, f32[128,1024]{1,0:T(8,128)S(1)}) custom-call(bf16[128,1024]{1,0:T(8,128)(2,1)S(1)} %copy-done.4, bf16[128,1024]{1,0:T(8,128)(2,1)S(1)} %copy-done.1, bf16[128,1024]{1,0:T(8,128)(2,1)S(1)} %copy-done.3, bf16[128,1024]{1,0:T(8,128)(2,1)S(1)} %get-tuple-element.22.dout_ref, ...), custom_call_target="tpu_custom_call" | custom-call | tf_op jit(solution)/shard_map/pallas_call | solution.py:123
  180.8 0.6 fusion.3
  181.4 1.2 shard_map.125
  (23 shorter events, 0.2 us)
Async XLA Ops:
  0.6 1.0 copy-start
  1.6 0.9 copy-start.2
  2.8 9.9 %collective-permute-start = (f32[4,128,128]{2,1,0:T(8,128)S(1)}, f32[4,128,128]{2,1,0:T(8,128)S(1)}, u32[]{:S(2)}, u32[]{:S(2)}) collective-permute-start(f32[4,128,128]{2,1,0:T(8,128)S(1)} %get-tuple-element.21), channel_id=1, source_target_pairs={{0,4},{4,0},{1,5},{5,1},{2,6},{6,2},{3,7},{7,3},{8,12},{12,8},{9,1... | collective-permute-start | bytes 786440 | tf_op jit(solution)/shard_map/ppermute | solution.py:145
  46.2 25.2 %all-to-all-start.1 = ((f32[64,8,128]{2,1,0:T(8,128)}), f32[64,8,128]{2,1,0:T(8,128)S(1)}, u32[]{:S(2)}, u32[]{:S(2)}) async-start(f32[64,8,128]{2,1,0:T(8,128)} %shard_map.121), calls=%async_computation.1 | async-start | bytes 524288 | tf_op jit(solution)/shard_map/all_to_all | solution.py:153
  71.4 5.9 %copy-start.1 = (bf16[128,1024]{1,0:T(8,128)(2,1)S(1)}, bf16[128,1024]{1,0:T(8,128)(2,1)}, u32[]{:S(2)}) copy-start(bf16[128,1024]{1,0:T(8,128)(2,1)} %k_ref.7) | copy-start | bytes 786436
  71.4 5.9 %copy-start.3 = (bf16[128,1024]{1,0:T(8,128)(2,1)S(1)}, bf16[128,1024]{1,0:T(8,128)(2,1)}, u32[]{:S(2)}) copy-start(bf16[128,1024]{1,0:T(8,128)(2,1)} %v_ref.7) | copy-start | bytes 786436
  71.4 5.9 %copy-start.4 = (bf16[128,1024]{1,0:T(8,128)(2,1)S(1)}, bf16[128,1024]{1,0:T(8,128)(2,1)}, u32[]{:S(2)}) copy-start(bf16[128,1024]{1,0:T(8,128)(2,1)} %q_ref.5) | copy-start | bytes 786436
  71.5 7.2 %copy-start.5 = (bf16[128,1024]{1,0:T(8,128)(2,1)S(1)}, bf16[128,1024]{1,0:T(8,128)(2,1)}, u32[]{:S(2)}) copy-start(bf16[128,1024]{1,0:T(8,128)(2,1)} %g_ref.1) | copy-start | bytes 786436
  71.5 7.2 %collective-permute-start.1 = (f32[4,128,128]{2,1,0:T(8,128)S(1)}, f32[4,128,128]{2,1,0:T(8,128)S(1)}, u32[]{:S(2)}, u32[]{:S(2)}) collective-permute-start(f32[4,128,128]{2,1,0:T(8,128)S(1)} %get-tuple-element.37), channel_id=1, source_target_pairs={{0,4},{4,0},{1,5},{5,1},{2,6},{6,2},{3,7},{7,3},{8,12},{12,8},{9,1... | collective-permute-start | bytes 786440 | tf_op jit(solution)/shard_map/ppermute | solution.py:145
  78.7 0.7 copy-start.6
  80.4 3.4 %collective-permute-start.2 = (f32[4,128,128]{2,1,0:T(8,128)S(1)}, f32[4,128,128]{2,1,0:T(8,128)S(1)}, u32[]{:S(2)}, u32[]{:S(2)}) collective-permute-start(f32[4,128,128]{2,1,0:T(8,128)S(1)} %get-tuple-element.29), channel_id=1, source_target_pairs={{0,4},{4,0},{1,5},{5,1},{2,6},{6,2},{3,7},{7,3},{8,12},{12,8},{9,1... | collective-permute-start | bytes 786440 | tf_op jit(solution)/shard_map/ppermute | solution.py:145
  110.8 45.9 %copy-start.7 = (f32[1024]{0:T(1024)S(1)}, f32[1024]{0:T(1024)}, u32[]{:S(2)}) copy-start(f32[1024]{0:T(1024)} %param.13) | copy-start | bytes 12292
  110.8 53.9 %all-to-all-start.3 = ((f32[64,8,128]{2,1,0:T(8,128)}), f32[64,8,128]{2,1,0:T(8,128)S(1)}, u32[]{:S(2)}, u32[]{:S(2)}) async-start(f32[64,8,128]{2,1,0:T(8,128)} %shard_map.124), calls=%async_computation.3 | async-start | bytes 524288 | tf_op jit(solution)/shard_map/all_to_all | solution.py:153
  148.0 8.7 %copy-start.8 = (f32[2,1024]{1,0:T(2,128)S(1)}, f32[2,1024]{1,0:T(2,128)}, u32[]{:S(2)}) copy-start(f32[2,1024]{1,0:T(2,128)} %param.15) | copy-start | bytes 24580
  148.0 8.7 %copy-start.9 = (f32[2,1024]{1,0:T(2,128)S(1)}, f32[2,1024]{1,0:T(2,128)}, u32[]{:S(2)}) copy-start(f32[2,1024]{1,0:T(2,128)} %param.14) | copy-start | bytes 24580
  164.8 16.6 %collective-permute-start.3 = (f32[4,128,128]{2,1,0:T(8,128)S(1)}, f32[4,128,128]{2,1,0:T(8,128)S(1)}, u32[]{:S(2)}, u32[]{:S(2)}) collective-permute-start(f32[4,128,128]{2,1,0:T(8,128)S(1)} %get-tuple-element.35), channel_id=1, source_target_pairs={{0,4},{4,0},{1,5},{5,1},{2,6},{6,2},{3,7},{7,3},{8,12},{12,8},{9,1... | collective-permute-start | bytes 786440 | tf_op jit(solution)/shard_map/ppermute | solution.py:145

commit v2 on v1

v2 whole, which is shorter than its diff:
```python
import functools

import jax
import jax.numpy as jnp
from jax import lax
from jax.experimental import pallas as pl
from jax.experimental.pallas import tpu as pltpu
from jax.sharding import Mesh
from jax.sharding import PartitionSpec as P

HEAD_DIM = 128
HEADS_HERE = 8
HALF = HEADS_HERE // 2
HALF_WIDTH = HALF * HEAD_DIM
CORES = 2
GROUP = 4
GRAD_ROWS = 8
VMEM_LIMIT = 12 * 1024 * 1024

BETA_ONE = 0.9
BETA_TWO = 0.999
ADAM_EPS = 1e-06
DECAY_RATE = 0.01
LEARN_RATE = 0.2
NORM_EPS = 1e-05
TRUST_EPS = 1e-06
CORRECT_ONE = 1.0 - 0.9**10
CORRECT_TWO = 1.0 - 0.999**10

F32 = jnp.float32
BF16 = jnp.bfloat16


def dot(a, b, da, db):
    return lax.dot_general(a, b, (((da,), (db,)), ((), ())), preferred_element_type=F32)


def cols(head):
    return pl.ds(pl.multiple_of(head * HEAD_DIM, HEAD_DIM), HEAD_DIM)


def causal_mask():
    row = lax.broadcasted_iota(jnp.int32, (HEAD_DIM, HEAD_DIM), 0)
    col = lax.broadcasted_iota(jnp.int32, (HEAD_DIM, HEAD_DIM), 1)
    return row >= col


def fixed(j):
    return slice(j * HEAD_DIM, (j + 1) * HEAD_DIM)


def pair_kernel(core_ref, k_hbm, v_hbm, mine_ref, send_ref, k_ref, v_ref, sems):
    copies = [
        pltpu.make_async_copy(src, dst, sems.at[i]) for i, (src, dst) in enumerate(((k_hbm, k_ref), (v_hbm, v_ref)))
    ]
    for copy in copies:
        copy.start()
    for copy in copies:
        copy.wait()
    core = core_ref[0]
    for out, half in ((send_ref, 1 - core), (mine_ref, core)):
        for j in range(HALF):
            at = cols(half * HALF + j)
            out[j] = dot(k_ref[:, at], v_ref[:, at], 0, 0)


def add_kernel(a_ref, b_ref, out_ref):
    rows = out_ref.shape[1]
    per = HEAD_DIM // rows
    for s in range(out_ref.shape[0]):
        at = slice((s % per) * rows, (s % per + 1) * rows)
        out_ref[s] = a_ref[s // per, at] + b_ref[s // per, at]


def widen_kernel(core_ref, q_ref, k_ref, v_ref, g_ref, send_ref):
    half = 1 - core_ref[0]
    at = pl.ds(pl.multiple_of(half * HALF_WIDTH, HALF_WIDTH), HALF_WIDTH)
    for i, ref in enumerate((q_ref, k_ref, v_ref, g_ref)):
        send_ref[i] = ref[:, at].astype(F32)


def local_kernel(core_ref, q_ref, k_ref, v_ref, recv_ref, w_ref, loc_ref):
    core = core_ref[0]
    causal = causal_mask()
    for j in range(HALF):
        at = cols(core * HALF + j)
        there = fixed(j)
        for b in range(CORES):
            if b == 0:
                q, k, v = q_ref[:, at], k_ref[:, at], v_ref[:, at]
            else:
                q, k, v = (recv_ref[i, :, there].astype(BF16) for i in range(3))
            w = jnp.where(causal, dot(q, k, 1, 1), 0.0).astype(BF16)
            w_ref[b, j] = w
            loc_ref[b, :, there] = dot(w, v, 1, 0)


def group_kernel(reverse, rows, h_ref, x_ref, part_ref, send_ref):
    h = h_ref[0]
    order = list(reversed(range(GROUP))) if reverse else list(range(GROUP))
    above = jnp.zeros((rows, HEAD_DIM), F32)
    for y in order:
        total = above
        for l in order:
            part_ref[y * GROUP + l] = total
            total = total + x_ref[y * GROUP + l, :rows]
        at = slice(y * rows, (y + 1) * rows)
        for i in range(GROUP):
            whole = (i < h) if reverse else (i > h)
            send_ref[i, at] = jnp.where(i == h, 0.0, jnp.where(whole, total, above))
        above = total
    if x_ref.shape[1] > rows:
        grads = x_ref[0, rows:]
        for i in range(1, x_ref.shape[0]):
            grads = grads + x_ref[i, rows:]
        for i in range(GROUP):
            send_ref[i, GROUP * rows :] = grads


def offset_kernel(rows, sent_ref, part_ref, out_ref, *grads_ref):
    for y in range(GROUP):
        at = slice(y * rows, (y + 1) * rows)
        offset = (sent_ref[0, at] + sent_ref[1, at]) + (sent_ref[2, at] + sent_ref[3, at])
        for l in range(GROUP):
            out_ref[y * GROUP + l] = part_ref[y * GROUP + l] + offset
    if grads_ref:
        at = slice(GROUP * rows, GROUP * rows + GRAD_ROWS)
        grads_ref[0][...] = (sent_ref[0, at] + sent_ref[1, at]) + (sent_ref[2, at] + sent_ref[3, at])


def norm_kernel(
    core_ref, q_ref, g_ref, gain_ref, recv_ref, loc_ref, before_ref, mine_ref, arrived_ref,
    state_ref, dout_ref, own_ref, other_ref, pay_ref,
):
    core = core_ref[0]
    slices, rows = pay_ref.shape[0] // HALF, pay_ref.shape[1] - GRAD_ROWS
    gain_rows, bias_rows = [], []
    for j in range(HALF):
        at = cols(core * HALF + j)
        there = fixed(j)
        gain = gain_ref[pl.ds(core * HALF + j, 1), :]
        before = before_ref[j]
        gain_row = jnp.zeros((1, HEAD_DIM), F32)
        bias_row = jnp.zeros((1, HEAD_DIM), F32)
        pair = None
        for b in range(CORES):
            if b == 0:
                q, grad_f = q_ref[:, at], g_ref[:, at].astype(F32)
                state = jnp.where(core == 1, before + arrived_ref[j], before).astype(BF16)
            else:
                q, grad_f = recv_ref[0, :, there].astype(BF16), recv_ref[3, :, there]
                state = jnp.where(core == 0, before + mine_ref[j], before).astype(BF16)
            state_ref[b, j] = state
            output = loc_ref[b, :, there] + dot(q, state, 1, 0)
            center = output - jnp.mean(output, axis=-1, keepdims=True)
            inv_std = lax.rsqrt(jnp.mean(center * center, axis=-1, keepdims=True) + NORM_EPS)
            normed = center * inv_std
            scaled = grad_f * gain
            d_out = inv_std * (
                scaled
                - jnp.mean(scaled, axis=-1, keepdims=True)
                - normed * jnp.mean(scaled * normed, axis=-1, keepdims=True)
            )
            dout = d_out.astype(BF16)
            dout_ref[b, :, there] = dout
            term = dot(q, dout, 0, 0)
            (own_ref, other_ref)[b][j] = term
            pair = term if pair is None else pair + term
            gain_row = gain_row + jnp.sum(grad_f * normed, axis=0, keepdims=True)
            bias_row = bias_row + jnp.sum(grad_f, axis=0, keepdims=True)
        for i in range(slices):
            pay_ref[j * slices + i, :rows] = pair[i * rows : (i + 1) * rows]
        gain_rows.append(gain_row)
        bias_rows.append(bias_row)
    grads = jnp.concatenate(gain_rows + bias_rows, axis=0)
    for s in range(pay_ref.shape[0]):
        pay_ref[s, rows:] = grads


def near_kernel(
    core_ref, q_ref, k_ref, v_ref, recv_ref, dout_ref, w_ref, state_ref, gq_ref, gk_ref, gv_ref, send_ref
):
    core = core_ref[0]
    causal = causal_mask()
    for j in range(HALF):
        at = cols(core * HALF + j)
        there = fixed(j)
        for b in range(CORES):
            if b == 0:
                q, k, v = q_ref[:, at], k_ref[:, at], v_ref[:, at]
            else:
                q, k, v = (recv_ref[i, :, there].astype(BF16) for i in range(3))
            dout = dout_ref[b, :, there]
            gw = jnp.where(causal, dot(dout, v, 1, 1), 0.0).astype(BF16)
            gq = dot(gw, k, 1, 0) + dot(dout, state_ref[b, j], 1, 1)
            gk = dot(gw, q, 0, 0)
            gv = dot(w_ref[b, j], dout, 0, 0)
            if b == 0:
                gq_ref[:, there], gk_ref[:, there], gv_ref[:, there] = gq.astype(BF16), gk, gv
            else:
                send_ref[0, :, there], send_ref[1, :, there], send_ref[2, :, there] = gq, gk, gv


def half_at(half):
    return pl.ds(pl.multiple_of(half * HALF_WIDTH, HALF_WIDTH), HALF_WIDTH)


def join_kernel(core_ref, own_ref, recv_ref, out_ref):
    core = core_ref[0]
    out_ref[:, half_at(core)] = own_ref[...]
    out_ref[:, half_at(1 - core)] = recv_ref[0].astype(BF16)


def far_kernel(
    core_ref, k_ref, v_ref, gk_own_ref, gv_own_ref, recv_ref, after_ref, other_ref, far_ref, gk_ref, gv_ref
):
    core = core_ref[0]
    for j in range(HALF):
        there = fixed(j)
        for b in range(CORES):
            if b == 0:
                at = cols(core * HALF + j)
                after = after_ref[j]
                later = jnp.where(core == 0, after + other_ref[j], after).astype(BF16)
                gk, gv = gk_own_ref[:, there], gv_own_ref[:, there]
            else:
                at = cols((1 - core) * HALF + j)
                later = far_ref[j].astype(BF16)
                gk, gv = recv_ref[1, :, there], recv_ref[2, :, there]
            gk_ref[:, at] = (gk + dot(v_ref[:, at], later, 1, 1)).astype(BF16)
            gv_ref[:, at] = (gv + dot(k_ref[:, at], later, 1, 0)).astype(BF16)


def lamb_direction(weight, grad, first, second):
    first_new = BETA_ONE * first + (1.0 - BETA_ONE) * grad
    second_new = BETA_TWO * second + (1.0 - BETA_TWO) * grad * grad
    return (
        first_new / CORRECT_ONE / (jnp.sqrt(second_new / CORRECT_TWO) + ADAM_EPS)
        + DECAY_RATE * weight
    )


def whole_sum(x):
    return jnp.sum(jnp.sum(x, axis=1, keepdims=True), axis=0, keepdims=True)


def step_kernel(core_ref, grads_ref, weight_ref, first_ref, second_ref, out_ref):
    at = pl.ds(core_ref[0] * HALF, HALF)
    for i in range(2):
        weight = weight_ref[i, at, :]
        step = lamb_direction(
            weight, grads_ref[i * HALF : (i + 1) * HALF], first_ref[i, at, :], second_ref[i, at, :]
        )
        out_ref[i * HALF : (i + 1) * HALF] = step
        for row, sum_of in ((8 + i, whole_sum(weight * weight)), (10 + i, whole_sum(step * step))):
            out_ref[row : row + 1] = jnp.broadcast_to(sum_of, (1, HEAD_DIM))
    out_ref[12:16] = jnp.zeros((4, HEAD_DIM), F32)


def new_kernel(core_ref, mine_ref, other_ref, sums_ref, weight_ref, out_ref):
    core = core_ref[0]
    for i in range(2):
        ratio = jnp.sqrt(sums_ref[i : i + 1]) / jnp.sqrt(sums_ref[2 + i : 3 + i] + TRUST_EPS)
        for half, ref in ((core, mine_ref), (1 - core, other_ref)):
            at = pl.ds(half * HALF, HALF)
            step = ref[i * HALF : (i + 1) * HALF]
            out_ref[i, at, :] = weight_ref[i, at, :] - LEARN_RATE * ratio * step


def call(kernel, outs, *args, scalar=True, hbm=False, scratch=()):
    vmem = pl.BlockSpec(memory_space=pltpu.VMEM)
    specs = [pl.BlockSpec(memory_space=pltpu.HBM) if hbm else vmem] * len(args)
    if scalar:
        specs[0] = pl.BlockSpec(memory_space=pltpu.SMEM)
    return pl.pallas_call(
        kernel,
        out_shape=[jax.ShapeDtypeStruct(s, d) for s, d in outs],
        in_specs=specs,
        out_specs=[vmem] * len(outs),
        scratch_shapes=scratch,
        compiler_params=pltpu.CompilerParams(vmem_limit_bytes=VMEM_LIMIT),
    )(*args)


STATE = (HALF, HEAD_DIM, HEAD_DIM)


def swap(array, axis="core", step=1):
    n = lax.axis_size(axis)
    return lax.ppermute(array, axis, [(i, i ^ step) for i in range(n)])


def exchange(array, axis):
    return lax.all_to_all(array, axis, 0, 0, tiled=True)


NEAR = ("y", "l")


def chip_scan(pay, reverse, beside):
    members = GROUP * GROUP
    rows = HALF * HEAD_DIM // members
    extra = pay.shape[1] - rows
    part = (members, rows, HEAD_DIM)
    h_s = lax.axis_index("h").astype(jnp.int32).reshape(1)
    landed = exchange(pay, NEAR)
    part_sums, send = call(
        functools.partial(group_kernel, reverse, rows),
        [(part, F32), ((GROUP, GROUP * rows + extra, HEAD_DIM), F32)], h_s, landed,
    )
    sent, beside = lax.optimization_barrier((exchange(send, "h"), beside))
    outs = [(part, F32)] + ([((extra, HEAD_DIM), F32)] if extra else [])
    sums, *rest = call(functools.partial(offset_kernel, rows), outs, sent, part_sums, scalar=False)
    return exchange(sums, NEAR).reshape(STATE), rest, beside


def per_device(queries, keys, values, grad_out, norm_gain, norm_bias, first_moment, second_moment):
    rows, width = queries.shape
    half = (rows, HALF_WIDTH)
    members = GROUP * GROUP
    slice_rows = HALF * HEAD_DIM // members
    core = lax.axis_index("core")
    core_s = core.astype(jnp.int32).reshape(1)
    by_head = (HEADS_HERE, HEAD_DIM)
    weight = jnp.stack([norm_gain.reshape(by_head), norm_bias.reshape(by_head)])
    first = first_moment.reshape((2,) + by_head)
    second = second_moment.reshape((2,) + by_head)

    mine, send = call(
        pair_kernel, [(STATE, F32)] * 2, core_s, keys, values, hbm=True,
        scratch=[pltpu.VMEM((rows, width), BF16)] * 2 + [pltpu.SemaphoreType.DMA((2,))],
    )
    arrived = swap(send)
    (pay,) = call(add_kernel, [((members, slice_rows, HEAD_DIM), F32)], mine, arrived, scalar=False)
    (wide,) = call(widen_kernel, [((4,) + half, F32)], core_s, queries, keys, values, grad_out)
    recv = swap(wide)
    weights, local = call(
        local_kernel, [((CORES,) + STATE, BF16), ((CORES,) + half, F32)], core_s, queries, keys, values, recv
    )
    before, _, (recv, weights, local) = chip_scan(pay, False, (recv, weights, local))

    pay_shape = (members, slice_rows + GRAD_ROWS, HEAD_DIM)
    state_b, dout, own, other, pay = call(
        norm_kernel,
        [((CORES,) + STATE, BF16), ((CORES,) + half, BF16), (STATE, F32), (STATE, F32), (pay_shape, F32)],
        core_s, queries, grad_out, weight[0], recv, local, before, mine, arrived,
    )
    gq_own, gk_own, gv_own, send = call(
        near_kernel,
        [(half, BF16), (half, F32), (half, F32), ((3,) + half, F32)],
        core_s, queries, keys, values, recv, dout, weights, state_b,
    )
    near = swap(send)
    (grad_q,) = call(join_kernel, [((rows, width), BF16)], core_s, gq_own, near)
    after, (grads,), (near, grad_q, gk_own, gv_own) = chip_scan(pay, True, (near, grad_q, gk_own, gv_own))

    (step,) = call(step_kernel, [((16, HEAD_DIM), F32)], core_s, grads, weight, first, second)
    step_there = swap(step)
    squares = step[8:] + step_there[8:]
    squares = lax.psum(squares, "fsdp")
    after, squares = lax.optimization_barrier((after, squares))
    (new,) = call(new_kernel, [((2,) + by_head, F32)], core_s, step, step_there, squares, weight)

    far = swap(jnp.where(core == 1, after + own, after))
    grad_k, grad_v = call(
        far_kernel, [((rows, width), BF16)] * 2,
        core_s, keys, values, gk_own, gv_own, near, after, other, far,
    )
    return grad_q, grad_k, grad_v, new[0].reshape(width), new[1].reshape(width)


def solution(mesh):
    seq, fsdp = mesh.devices.shape
    fine = Mesh(
        mesh.devices.reshape(GROUP, seq // (GROUP * GROUP * CORES), GROUP, CORES, fsdp), ("y", "h", "l", "core", "fsdp")
    )
    big = P(("y", "h", "l", "core"), "fsdp")
    return jax.shard_map(
        per_device,
        mesh=fine,
        in_specs=(big, big, big, big, P("fsdp"), P("fsdp"), P(None, "fsdp"), P(None, "fsdp")),
        out_specs=(big, big, big, P("fsdp"), P("fsdp")),
        check_vma=False,
    )
```

time: 183 us -> 140 us (0.77)
  blocking collectives: 106 us -> 34.3 us
  starting transfers between devices: 44.2 us -> 53.9 us
  waiting for transfers between devices: 20.8 us -> 29.4 us
  local copies, waits for them, and re-layouts: 3.19 us -> 9.8 us
  Pallas kernels: 7.41 us -> 10.2 us
    all_to_all x2, blocking collectives: 58.8 us -> 25.7 us  [exchange(): return lax.all_to_all(array, axis, 0, 0, tiled=True)]
    psum x3 -> x1, blocking collectives: 39.1 us -> 8.65 us  [per_device(): squares = lax.psum(squares, 'fsdp')]
    all_to_all x2 -> x4, starting transfers between devices: 13.8 us -> 27.6 us  [exchange(): return lax.all_to_all(array, axis, 0, 0, tiled=True)]
    all_gather x1 -> x0, blocking collectives: 7.71 us -> none  [per_device(): totals = jnp.sum(lax.all_gather(totals, 'fsdp'), axis=0)]
    all_to_all x2 -> x4, waiting for transfers between devices: 18.2 us -> 25.1 us  [exchange(): return lax.all_to_all(array, axis, 0, 0, tiled=True)]
    unnamed x20 -> x40, local copies, waits for them, and re-layouts: 2.59 us -> 9.2 us
    ppermute x4 -> x5, starting transfers between devices: 30.4 us -> 26.3 us  [swap(): return lax.ppermute(array, axis, [(i, i ^ step) for i in range(n)])]
    pallas_call x7 -> x14, Pallas kernels: 7.41 us -> 10.2 us  [call(): pl.pallas_call(kernel, out_shape=[jax.ShapeDtypeStruct(s, d) for s, d in...]
  transfers between devices with their start and end apart: 6 -> 9, of which waited for: 3 -> 7; matrix products, arithmetic and copies ran while one was open for 0% -> 0% of each run, Pallas kernels for 2% -> 4%
where the time goes in v2:
time: 140 us; the launch traced here: 139 us
  starting transfers between devices  53.9 us (38%)
  blocking collectives  34.3 us (24%)
  waiting for transfers between devices  29.4 us (21%)
  Pallas kernels  10.2 us (7%)
  local copies, waits for them, and re-layouts  9.8 us (7%)
    all_to_all x4, starting transfers between devices, exchange(): return lax.all_to_all(array, axis, 0, 0, tiled=True)  27.6 us
    ppermute x5, starting transfers between devices, swap(): return lax.ppermute(array, axis, [(i, i ^ step) for i in range(n)])  26.3 us
    all_to_all x2, blocking collectives, exchange(): return lax.all_to_all(array, axis, 0, 0, tiled=True)  25.7 us
    all_to_all x4, waiting for transfers between devices, exchange(): return lax.all_to_all(array, axis, 0, 0, tiled=True)  25.1 us
    pallas_call x14, Pallas kernels, call(): pl.pallas_call(kernel, out_shape=[jax.ShapeDtypeStruct(s, d) for s, d in...  10.2 us
    unnamed x40, local copies, waits for them, and re-layouts  9.2 us
    psum x1, blocking collectives, per_device(): squares = lax.psum(squares, 'fsdp')  8.65 us
    ppermute x5, waiting for transfers between devices, swap(): return lax.ppermute(array, axis, [(i, i ^ step) for i in range(n)])  4.35 us
  transfers between devices with their start and end apart: 9, of which 7 were waited for; matrix products, arithmetic and copies ran while one was open for 0% of the time, Pallas kernels for 4%

profile of v2, /device:TPU:1, one launch (start us, length us, event | category | flops | bytes accessed | tf_op | source)
XLA Modules:
  0.0 138.6 jit_solution(5657514373904596927)
XLA Ops:
  0.6 0.9 copy-done
  1.6 0.9 copy-done.2
  2.9 8.8 %collective-permute-start = (f32[4,128,128]{2,1,0:T(8,128)S(1)}, f32[4,128,128]{2,1,0:T(8,128)S(1)}, u32[]{:S(2)}, u32[]{:S(2)}) collective-permute-start(f32[4,128,128]{2,1,0:T(8,128)S(1)} %get-tuple-element.38), channel_id=1, source_target_pairs={{0,4},{4,0},{1,5},{5,1},{2,6},{6,2},{3,7},{7,3},{8,12},{12,8},{9,1... | collective-permute-start | bytes 786440 | tf_op jit(solution)/shard_map/ppermute | solution.py:290
  11.7 1.1 collective-permute-done.b_ref.arrived_ref
  13.6 3.7 %all-to-all-start = ((f32[16,32,128]{2,1,0:T(8,128)}), f32[16,32,128]{2,1,0:T(8,128)S(1)}, u32[]{:S(2)}, u32[]{:S(2)}) async-start(f32[16,32,128]{2,1,0:T(8,128)} %shard_map.120), calls=%async_computation | async-start | bytes 524288 | tf_op jit(solution)/shard_map/all_to_all | solution.py:294
  17.3 1.1 shard_map.122
  18.3 2.3 %collective-permute-start.1 = (f32[4,128,512]{2,1,0:T(8,128)}, f32[4,128,512]{2,1,0:T(8,128)S(1)}, u32[]{:S(2)}, u32[]{:S(2)}) collective-permute-start(f32[4,128,512]{2,1,0:T(8,128)} %shard_map.122), channel_id=1, source_target_pairs={{0,4},{4,0},{1,5},{5,1},{2,6},{6,2},{3,7},{7,3},{8,12},{12,8},{9,1... | collective-permute-start | bytes 3145736 | tf_op jit(solution)/shard_map/ppermute | solution.py:290
  20.6 6.6 %all-to-all-done.x_ref = f32[16,32,128]{2,1,0:T(8,128)S(1)} async-done(((f32[16,32,128]{2,1,0:T(8,128)}), f32[16,32,128]{2,1,0:T(8,128)S(1)}, u32[]{:S(2)}, u32[]{:S(2)}) %all-to-all-start) | async-done | bytes 262176 | tf_op jit(solution)/shard_map/all_to_all | solution.py:294
  27.2 0.7 shard_map.121
  28.6 11.5 %all-to-all-start.1 = ((f32[4,128,128]{2,1,0:T(8,128)}), f32[4,128,128]{2,1,0:T(8,128)S(1)}, u32[]{:S(2)}, u32[]{:S(2)}) async-start(f32[4,128,128]{2,1,0:T(8,128)} %get-tuple-element.39), calls=%async_computation.1 | async-start | bytes 524288 | tf_op jit(solution)/shard_map/all_to_all | solution.py:294
  40.2 1.4 shard_map.123
  42.2 13.7 %all-to-all-done.1.sent_ref = f32[4,128,128]{2,1,0:T(8,128)S(1)} async-done(((f32[4,128,128]{2,1,0:T(8,128)}), f32[4,128,128]{2,1,0:T(8,128)S(1)}, u32[]{:S(2)}, u32[]{:S(2)}) %all-to-all-start.1) | async-done | bytes 262176 | tf_op jit(solution)/shard_map/all_to_all | solution.py:294
  55.9 0.9 copy-done.7
  56.9 13.9 %all_to_all.30 = f32[16,32,128]{2,1,0:T(8,128)S(1)} all-to-all(f32[16,32,128]{2,1,0:T(8,128)S(1)} %shard_map.124), channel_id=1, replica_groups=mesh['y'=4,'h'=4,'l'=4,'core'=2,'fsdp'=4] {'y','l'}, dimensions={0} | all-to-all | bytes 524288 | tf_op jit(solution)/shard_map/all_to_all | solution.py:294
  70.8 1.0 shard_map.125
  73.2 11.8 %all_to_all.31.x_ref = f32[16,40,128]{2,1,0:T(8,128)S(1)} all-to-all(f32[16,40,128]{2,1,0:T(8,128)S(1)} %get-tuple-element.46), channel_id=1, replica_groups=mesh['y'=4,'h'=4,'l'=4,'core'=2,'fsdp'=4] {'y','l'}, dimensions={0} | all-to-all | bytes 655360 | tf_op jit(solution)/shard_map/all_to_all | solution.py:294
  85.0 0.8 shard_map.126
  85.8 8.5 %all-to-all-start.4 = ((f32[4,136,128]{2,1,0:T(8,128)}), f32[4,136,128]{2,1,0:T(8,128)S(1)}, u32[]{:S(2)}, u32[]{:S(2)}) async-start(f32[4,136,128]{2,1,0:T(8,128)} %get-tuple-element.47), calls=%async_computation.4 | async-start | bytes 557056 | tf_op jit(solution)/shard_map/all_to_all | solution.py:294
  94.3 0.9 copy-done.11
  95.3 0.9 copy-done.13
  96.2 0.9 copy-done.15
  97.2 1.4 %shard_map.127 = (bf16[128,512]{1,0:T(8,128)(2,1)S(1)}, f32[128,512]{1,0:T(8,128)S(1)}, f32[128,512]{1,0:T(8,128)S(1)}, f32[3,128,512]{2,1,0:T(8,128)S(1)}) custom-call(s32[1]{0:T(128)} %bitcast.1.core_ref, bf16[128,1024]{1,0:T(8,128)(2,1)S(1)} %copy-done.4, bf16[128,1024]{1,0:T(8,128)(2,1)S(1)} %copy-done.1, bf16[128,1024]{1,0:T(8,128)(2,1)S(1)} %copy-done.3, ...), custom_call_target="tpu_custom_call" | custom-call | tf_op jit(solution)/shard_map/pallas_call | solution.py:275
  98.6 4.3 %collective-permute-start.2 = (f32[3,128,512]{2,1,0:T(8,128)S(1)}, f32[3,128,512]{2,1,0:T(8,128)S(1)}, u32[]{:S(2)}, u32[]{:S(2)}) collective-permute-start(f32[3,128,512]{2,1,0:T(8,128)S(1)} %get-tuple-element.51), channel_id=1, source_target_pairs={{0,4},{4,0},{1,5},{5,1},{2,6},{6,2},{3,7},{7,3},{8,12},{12,8},{9,1... | collective-permute-start | bytes 2359304 | tf_op jit(solution)/shard_map/ppermute | solution.py:290
  102.9 1.9 %collective-permute-done.2.recv_ref = f32[3,128,512]{2,1,0:T(8,128)S(1)} collective-permute-done((f32[3,128,512]{2,1,0:T(8,128)S(1)}, f32[3,128,512]{2,1,0:T(8,128)S(1)}, u32[]{:S(2)}, u32[]{:S(2)}) %collective-permute-start.2) | collective-permute-done | bytes 786464 | tf_op jit(solution)/shard_map/ppermute | solution.py:290
  105.5 4.8 %all-to-all-done.4.sent_ref = f32[4,136,128]{2,1,0:T(8,128)S(1)} async-done(((f32[4,136,128]{2,1,0:T(8,128)}), f32[4,136,128]{2,1,0:T(8,128)S(1)}, u32[]{:S(2)}, u32[]{:S(2)}) %all-to-all-start.4) | async-done | bytes 278560 | tf_op jit(solution)/shard_map/all_to_all | solution.py:294
  110.3 0.7 shard_map.129
  111.0 3.9 %all-to-all-start.5 = ((f32[16,32,128]{2,1,0:T(8,128)}), f32[16,32,128]{2,1,0:T(8,128)S(1)}, u32[]{:S(2)}, u32[]{:S(2)}) async-start(f32[16,32,128]{2,1,0:T(8,128)} %get-tuple-element.61), calls=%async_computation.5 | async-start | bytes 524288 | tf_op jit(solution)/shard_map/all_to_all | solution.py:294
  115.8 6.7 %collective-permute-start.3 = (f32[16,128]{1,0:T(8,128)S(1)}, f32[16,128]{1,0:T(8,128)S(1)}, u32[]{:S(2)}, u32[]{:S(2)}) collective-permute-start(f32[16,128]{1,0:T(8,128)S(1)} %shard_map.130.mine_ref), channel_id=1, source_target_pairs={{0,4},{4,0},{1,5},{5,1},{2,6},{6,2},{3,7},{7,3},{8,12},{12,8},{9,1... | collective-permute-start | bytes 24584 | tf_op jit(solution)/shard_map/ppermute | solution.py:290
  122.5 0.8 collective-permute-done.3.other_ref
  123.3 8.6 %psum.7.sums_ref = f32[8,128]{1,0:T(8,128)S(1)} all-reduce(f32[8,128]{1,0:T(8,128)S(1)} %slice_add_fusion), channel_id=1, replica_groups=mesh['y'=4,'h'=4,'l'=4,'core'=2,'fsdp'=4] {'fsdp'}, use_global_device_ids=true, to_apply=%region_0.0 | all-reduce | flops 1024 | bytes 8192 | tf_op jit(solution)/shard_map/psum | solution.py:360
  132.0 4.2 %collective-permute-start.4 = (f32[4,128,128]{2,1,0:T(8,128)S(1)}, f32[4,128,128]{2,1,0:T(8,128)S(1)}, u32[]{:S(2)}, u32[]{:S(2)}) collective-permute-start(f32[4,128,128]{2,1,0:T(8,128)S(1)} %add_select_fusion), channel_id=1, source_target_pairs={{0,4},{4,0},{1,5},{5,1},{2,6},{6,2},{3,7},{7,3},{8,12},{12,8},{9,1... | collective-permute-start | bytes 786440 | tf_op jit(solution)/shard_map/ppermute | solution.py:290
  137.4 1.2 shard_map.131
  (48 shorter events, 6.6 us)
Async XLA Ops:
  0.6 1.0 copy-start
  1.6 0.9 copy-start.2
  2.9 9.9 %collective-permute-start = (f32[4,128,128]{2,1,0:T(8,128)S(1)}, f32[4,128,128]{2,1,0:T(8,128)S(1)}, u32[]{:S(2)}, u32[]{:S(2)}) collective-permute-start(f32[4,128,128]{2,1,0:T(8,128)S(1)} %get-tuple-element.38), channel_id=1, source_target_pairs={{0,4},{4,0},{1,5},{5,1},{2,6},{6,2},{3,7},{7,3},{8,12},{12,8},{9,1... | collective-permute-start | bytes 786440 | tf_op jit(solution)/shard_map/ppermute | solution.py:290
  12.8 4.4 %copy-start.4 = (bf16[128,1024]{1,0:T(8,128)(2,1)S(1)}, bf16[128,1024]{1,0:T(8,128)(2,1)}, u32[]{:S(2)}) copy-start(bf16[128,1024]{1,0:T(8,128)(2,1)} %q_ref.7) | copy-start | bytes 786436
  12.8 4.4 %copy-start.5 = (bf16[128,1024]{1,0:T(8,128)(2,1)S(1)}, bf16[128,1024]{1,0:T(8,128)(2,1)}, u32[]{:S(2)}) copy-start(bf16[128,1024]{1,0:T(8,128)(2,1)} %g_ref.3) | copy-start | bytes 786436
  13.6 3.7 %copy-start.1 = (bf16[128,1024]{1,0:T(8,128)(2,1)S(1)}, bf16[128,1024]{1,0:T(8,128)(2,1)}, u32[]{:S(2)}) copy-start(bf16[128,1024]{1,0:T(8,128)(2,1)} %k_ref.7) | copy-start | bytes 786436
  13.6 3.7 %copy-start.3 = (bf16[128,1024]{1,0:T(8,128)(2,1)S(1)}, bf16[128,1024]{1,0:T(8,128)(2,1)}, u32[]{:S(2)}) copy-start(bf16[128,1024]{1,0:T(8,128)(2,1)} %v_ref.7) | copy-start | bytes 786436
  13.6 13.6 %all-to-all-start = ((f32[16,32,128]{2,1,0:T(8,128)}), f32[16,32,128]{2,1,0:T(8,128)S(1)}, u32[]{:S(2)}, u32[]{:S(2)}) async-start(f32[16,32,128]{2,1,0:T(8,128)} %shard_map.120), calls=%async_computation | async-start | bytes 524288 | tf_op jit(solution)/shard_map/all_to_all | solution.py:294
  18.3 21.8 %collective-permute-start.1 = (f32[4,128,512]{2,1,0:T(8,128)}, f32[4,128,512]{2,1,0:T(8,128)S(1)}, u32[]{:S(2)}, u32[]{:S(2)}) collective-permute-start(f32[4,128,512]{2,1,0:T(8,128)} %shard_map.122), channel_id=1, source_target_pairs={{0,4},{4,0},{1,5},{5,1},{2,6},{6,2},{3,7},{7,3},{8,12},{12,8},{9,1... | collective-permute-start | bytes 3145736 | tf_op jit(solution)/shard_map/ppermute | solution.py:290
  27.9 0.7 copy-start.6
  28.6 27.3 %all-to-all-start.1 = ((f32[4,128,128]{2,1,0:T(8,128)}), f32[4,128,128]{2,1,0:T(8,128)S(1)}, u32[]{:S(2)}, u32[]{:S(2)}) async-start(f32[4,128,128]{2,1,0:T(8,128)} %get-tuple-element.39), calls=%async_computation.1 | async-start | bytes 524288 | tf_op jit(solution)/shard_map/all_to_all | solution.py:294
  41.5 0.7 copy-start.10
  55.9 1.0 copy-start.7
  56.9 13.9 %copy-start.16 = (f32[1024]{0:T(1024)S(1)}, f32[1024]{0:T(1024)}, u32[]{:S(2)}) copy-start(f32[1024]{0:T(1024)} %param.12) | copy-start | bytes 12292
  71.8 0.7 copy-start.8
  72.5 0.7 copy-start.14
  73.2 11.8 %copy-start.12 = (bf16[2,4,128,128]{3,2,1,0:T(8,128)(2,1)}, bf16[2,4,128,128]{3,2,1,0:T(8,128)(2,1)S(1)}, u32[]{:S(2)}) copy-start(bf16[2,4,128,128]{3,2,1,0:T(8,128)(2,1)S(1)} %get-tuple-element.50.state_ref) | copy-start | bytes 786436
  85.8 24.5 %all-to-all-start.4 = ((f32[4,136,128]{2,1,0:T(8,128)}), f32[4,136,128]{2,1,0:T(8,128)S(1)}, u32[]{:S(2)}, u32[]{:S(2)}) async-start(f32[4,136,128]{2,1,0:T(8,128)} %get-tuple-element.47), calls=%async_computation.4 | async-start | bytes 557056 | tf_op jit(solution)/shard_map/all_to_all | solution.py:294
  94.3 0.9 copy-start.11
  95.3 0.9 copy-start.13
  96.2 0.9 copy-start.15
  98.6 6.2 %collective-permute-start.2 = (f32[3,128,512]{2,1,0:T(8,128)S(1)}, f32[3,128,512]{2,1,0:T(8,128)S(1)}, u32[]{:S(2)}, u32[]{:S(2)}) collective-permute-start(f32[3,128,512]{2,1,0:T(8,128)S(1)} %get-tuple-element.51), channel_id=1, source_target_pairs={{0,4},{4,0},{1,5},{5,1},{2,6},{6,2},{3,7},{7,3},{8,12},{12,8},{9,1... | collective-permute-start | bytes 2359304 | tf_op jit(solution)/shard_map/ppermute | solution.py:290
  111.0 3.9 %copy-start.19 = (f32[1024]{0:T(1024)S(1)}, f32[1024]{0:T(1024)}, u32[]{:S(2)}) copy-start(f32[1024]{0:T(1024)} %param.13) | copy-start | bytes 12292
  111.0 21.0 %all-to-all-start.5 = ((f32[16,32,128]{2,1,0:T(8,128)}), f32[16,32,128]{2,1,0:T(8,128)S(1)}, u32[]{:S(2)}, u32[]{:S(2)}) async-start(f32[16,32,128]{2,1,0:T(8,128)} %get-tuple-element.61), calls=%async_computation.5 | async-start | bytes 524288 | tf_op jit(solution)/shard_map/all_to_all | solution.py:294
  115.0 0.7 copy-start.17
  115.0 0.7 copy-start.18
  115.8 7.5 %collective-permute-start.3 = (f32[16,128]{1,0:T(8,128)S(1)}, f32[16,128]{1,0:T(8,128)S(1)}, u32[]{:S(2)}, u32[]{:S(2)}) collective-permute-start(f32[16,128]{1,0:T(8,128)S(1)} %shard_map.130.mine_ref), channel_id=1, source_target_pairs={{0,4},{4,0},{1,5},{5,1},{2,6},{6,2},{3,7},{7,3},{8,12},{12,8},{9,1... | collective-permute-start | bytes 24584 | tf_op jit(solution)/shard_map/ppermute | solution.py:290
  132.0 5.4 %copy-start.9 = (f32[4,128,128]{2,1,0:T(8,128)S(1)}, f32[4,128,128]{2,1,0:T(8,128)}, u32[]{:S(2)}) copy-start(f32[4,128,128]{2,1,0:T(8,128)} %copy-done.8) | copy-start | bytes 786436
  132.0 5.4 %collective-permute-start.4 = (f32[4,128,128]{2,1,0:T(8,128)S(1)}, f32[4,128,128]{2,1,0:T(8,128)S(1)}, u32[]{:S(2)}, u32[]{:S(2)}) collective-permute-start(f32[4,128,128]{2,1,0:T(8,128)S(1)} %add_select_fusion), channel_id=1, source_target_pairs={{0,4},{4,0},{1,5},{5,1},{2,6},{6,2},{3,7},{7,3},{8,12},{12,8},{9,1... | collective-permute-start | bytes 786440 | tf_op jit(solution)/shard_map/ppermute | solution.py:290

commit v3 on v2

v3 whole, which is shorter than its diff:
```python
import functools

import jax
import jax.numpy as jnp
from jax import lax
from jax.experimental import pallas as pl
from jax.experimental.pallas import tpu as pltpu
from jax.sharding import Mesh
from jax.sharding import PartitionSpec as P

HEAD_DIM = 128
HEADS_HERE = 8
HALF = HEADS_HERE // 2
HALF_WIDTH = HALF * HEAD_DIM
CORES = 2
GROUP = 4
GRAD_ROWS = 8
STEP_ROW = HALF * HEAD_DIM
VMEM_LIMIT = 12 * 1024 * 1024

BETA_ONE = 0.9
BETA_TWO = 0.999
ADAM_EPS = 1e-06
DECAY_RATE = 0.01
LEARN_RATE = 0.2
NORM_EPS = 1e-05
TRUST_EPS = 1e-06
CORRECT_ONE = 1.0 - 0.9**10
CORRECT_TWO = 1.0 - 0.999**10

F32 = jnp.float32
BF16 = jnp.bfloat16


def dot(a, b, da, db):
    return lax.dot_general(a, b, (((da,), (db,)), ((), ())), preferred_element_type=F32)


def cols(head):
    return pl.ds(pl.multiple_of(head * HEAD_DIM, HEAD_DIM), HEAD_DIM)


def causal_mask():
    row = lax.broadcasted_iota(jnp.int32, (HEAD_DIM, HEAD_DIM), 0)
    col = lax.broadcasted_iota(jnp.int32, (HEAD_DIM, HEAD_DIM), 1)
    return row >= col


def fixed(j):
    return slice(j * HEAD_DIM, (j + 1) * HEAD_DIM)


def pair_kernel(core_ref, kv_ref, mine_ref, send_ref):
    core = core_ref[0]
    k_ref, v_ref = kv_ref.at[0], kv_ref.at[1]
    for out, half in ((send_ref, 1 - core), (mine_ref, core)):
        for j in range(HALF):
            at = cols(half * HALF + j)
            out[j] = dot(k_ref[:, at], v_ref[:, at], 0, 0)


def add_kernel(core_ref, a_ref, b_ref, out_ref, first_ref):
    core = core_ref[0]
    for j in range(HALF):
        first_ref[j] = jnp.where(core == 0, a_ref[j], b_ref[j])
    rows = out_ref.shape[1]
    per = HEAD_DIM // rows
    for s in range(out_ref.shape[0]):
        at = slice((s % per) * rows, (s % per + 1) * rows)
        out_ref[s] = a_ref[s // per, at] + b_ref[s // per, at]


def widen_kernel(core_ref, q_ref, k_ref, v_ref, g_ref, send_ref):
    half = 1 - core_ref[0]
    at = pl.ds(pl.multiple_of(half * HALF_WIDTH, HALF_WIDTH), HALF_WIDTH)
    for i, ref in enumerate((q_ref, k_ref, v_ref, g_ref)):
        send_ref[i] = ref[:, at].astype(F32)


def local_kernel(core_ref, q_ref, k_ref, v_ref, g_ref, recv_ref, in_ref, loc_ref):
    core = core_ref[0]
    causal = causal_mask()
    at = half_at(core)
    for i, ref in enumerate((q_ref, k_ref, v_ref, g_ref)):
        in_ref[0, i] = ref[:, at]
        in_ref[1, i] = recv_ref[i].astype(BF16)
    for j in range(HALF):
        there = fixed(j)
        for b in range(CORES):
            q, k, v = (in_ref[b, i, :, there] for i in range(3))
            w = jnp.where(causal, dot(q, k, 1, 1), 0.0).astype(BF16)
            loc_ref[b, :, there] = dot(w, v, 1, 0)


def group_kernel(reverse, rows, x_ref, part_ref, send_ref):
    order = list(reversed(range(GROUP))) if reverse else list(range(GROUP))
    total = jnp.zeros((rows, HEAD_DIM), F32)
    for i, y in enumerate(order):
        for l in order:
            part_ref[y * GROUP + l] = total
            total = total + x_ref[y * GROUP + l, :rows]
        send_ref[i * rows : (i + 1) * rows] = total
    if x_ref.shape[1] > rows:
        grads = x_ref[0, rows:]
        for i in range(1, x_ref.shape[0]):
            grads = grads + x_ref[i, rows:]
        send_ref[GROUP * rows :] = grads


def sum_kernel(a_ref, b_ref, out_ref):
    out_ref[...] = a_ref[...] + b_ref[...]


def offset_kernel(reverse, rows, h_ref, near_ref, far_ref, mine_ref, part_ref, out_ref, *grads_ref):
    h = h_ref[0]
    order = list(reversed(range(GROUP))) if reverse else list(range(GROUP))
    near_first = ((h ^ 1) > h) if reverse else ((h ^ 1) < h)
    far_first = ((h ^ 3) > h) if reverse else ((h ^ 3) < h)
    zero = jnp.zeros((rows, HEAD_DIM), F32)
    for i, y in enumerate(order):
        offset = zero
        for ref, first in ((near_ref, near_first), (far_ref, far_first)):
            up_to = ref[i * rows : (i + 1) * rows]
            above = ref[(i - 1) * rows : i * rows] if i else zero
            offset = offset + jnp.where(first, up_to, above)
        for l in range(GROUP):
            out_ref[y * GROUP + l] = part_ref[y * GROUP + l] + offset
    if grads_ref:
        grads_ref[0][...] = mine_ref[GROUP * rows :] + far_ref[GROUP * rows :]


def norm_kernel(core_ref, in_ref, gain_ref, loc_ref, before_ref, first_ref, state_ref, dout_ref, pay_ref):
    core = core_ref[0]
    slices, rows = pay_ref.shape[0] // HALF, pay_ref.shape[1] - GRAD_ROWS
    gain_rows, bias_rows = [], []
    for j in range(HALF):
        there = fixed(j)
        gain = gain_ref[pl.ds(core * HALF + j, 1), :]
        before = before_ref[j]
        pair, gain_row, bias_row = 0.0, 0.0, 0.0
        for b in range(CORES):
            state = jnp.where(core != b, before + first_ref[j], before).astype(BF16)
            state_ref[b, j] = state
            q, grad_f = in_ref[b, 0, :, there], in_ref[b, 3, :, there].astype(F32)
            output = loc_ref[b, :, there] + dot(q, state, 1, 0)
            center = output - jnp.mean(output, axis=-1, keepdims=True)
            inv_std = lax.rsqrt(jnp.mean(center * center, axis=-1, keepdims=True) + NORM_EPS)
            normed = center * inv_std
            scaled = grad_f * gain
            d_out = inv_std * (
                scaled
                - jnp.mean(scaled, axis=-1, keepdims=True)
                - normed * jnp.mean(scaled * normed, axis=-1, keepdims=True)
            )
            dout = d_out.astype(BF16)
            dout_ref[b, :, there] = dout
            pair = pair + dot(q, dout, 0, 0)
            gain_row = gain_row + jnp.sum(grad_f * normed, axis=0, keepdims=True)
            bias_row = bias_row + jnp.sum(grad_f, axis=0, keepdims=True)
        for i in range(slices):
            pay_ref[j * slices + i, :rows] = pair[i * rows : (i + 1) * rows]
        gain_rows.append(gain_row)
        bias_rows.append(bias_row)
    grads = jnp.concatenate(gain_rows + bias_rows, axis=0)
    for s in range(pay_ref.shape[0]):
        pay_ref[s, rows:] = grads


def near_kernel(
    core_ref, in_ref, dout_ref, state_ref, gain_ref, bias_ref, first_ref, second_ref,
    gq_ref, gk_ref, gv_ref, send_ref, own_ref, other_ref, pack_ref,
):
    core = core_ref[0]
    for p, ref in enumerate((gain_ref, bias_ref)):
        pack_ref[0, p * HALF : (p + 1) * HALF] = ref[pl.ds(core * HALF, HALF), :]
        for j in range(HALF):
            at, row = cols(core * HALF + j), p * HALF + j
            pack_ref[1, row : row + 1] = first_ref[p : p + 1, at]
            pack_ref[2, row : row + 1] = second_ref[p : p + 1, at]
    causal = causal_mask()
    for j in range(HALF):
        there = fixed(j)
        for b in range(CORES):
            q, k, v = (in_ref[b, i, :, there] for i in range(3))
            dout = dout_ref[b, :, there]
            (own_ref, other_ref)[b][j] = dot(q, dout, 0, 0)
            w = jnp.where(causal, dot(q, k, 1, 1), 0.0).astype(BF16)
            gw = jnp.where(causal, dot(dout, v, 1, 1), 0.0).astype(BF16)
            gq = dot(gw, k, 1, 0) + dot(dout, state_ref[b, j], 1, 1)
            gk = dot(gw, q, 0, 0)
            gv = dot(w, dout, 0, 0)
            if b == 0:
                gq_ref[:, there], gk_ref[:, there], gv_ref[:, there] = gq.astype(BF16), gk, gv
            else:
                send_ref[0, :, there], send_ref[1, :, there], send_ref[2, :, there] = gq, gk, gv


def half_at(half):
    return pl.ds(pl.multiple_of(half * HALF_WIDTH, HALF_WIDTH), HALF_WIDTH)


def join_kernel(core_ref, own_ref, recv_ref, out_ref):
    core = core_ref[0]
    out_ref[:, half_at(core)] = own_ref[...]
    out_ref[:, half_at(1 - core)] = recv_ref[0].astype(BF16)


def lamb_direction(weight, grad, first, second):
    first_new = BETA_ONE * first + (1.0 - BETA_ONE) * grad
    second_new = BETA_TWO * second + (1.0 - BETA_TWO) * grad * grad
    return (
        first_new / CORRECT_ONE / (jnp.sqrt(second_new / CORRECT_TWO) + ADAM_EPS)
        + DECAY_RATE * weight
    )


def whole_sum(x):
    return jnp.sum(jnp.sum(x, axis=1, keepdims=True), axis=0, keepdims=True)


def step_kernel(grads_ref, pack_ref, step_ref, squares_ref):
    for i in range(2):
        at = slice(i * HALF, (i + 1) * HALF)
        weight = pack_ref[0, at]
        step = lamb_direction(weight, grads_ref[at], pack_ref[1, at], pack_ref[2, at])
        step_ref[at] = step
        for row, sum_of in ((i, whole_sum(weight * weight)), (2 + i, whole_sum(step * step))):
            squares_ref[row : row + 1] = jnp.broadcast_to(sum_of, (1, HEAD_DIM))
    squares_ref[4:8] = jnp.zeros((4, HEAD_DIM), F32)


def pack_kernel(core_ref, after_ref, own_ref, step_ref, squares_ref, out_ref):
    core = core_ref[0]
    for j in range(HALF):
        after = after_ref[j]
        out_ref[j * HEAD_DIM : (j + 1) * HEAD_DIM] = jnp.where(core == 1, after + own_ref[j], after)
    out_ref[STEP_ROW : STEP_ROW + 8] = step_ref[...]
    out_ref[STEP_ROW + 8 :] = squares_ref[...]


def far_kernel(
    core_ref, k_ref, v_ref, gk_own_ref, gv_own_ref, recv_ref, after_ref, other_ref, far_ref, step_ref, squares_ref,
    gain_ref, bias_ref, gk_ref, gv_ref, new_gain_ref, new_bias_ref,
):
    core = core_ref[0]
    for j in range(HALF):
        there = fixed(j)
        for b in range(CORES):
            if b == 0:
                at = cols(core * HALF + j)
                after = after_ref[j]
                later = jnp.where(core == 0, after + other_ref[j], after).astype(BF16)
                gk, gv = gk_own_ref[:, there], gv_own_ref[:, there]
            else:
                at = cols((1 - core) * HALF + j)
                later = far_ref[there].astype(BF16)
                gk, gv = recv_ref[1, :, there], recv_ref[2, :, there]
            gk_ref[:, at] = (gk + dot(v_ref[:, at], later, 1, 1)).astype(BF16)
            gv_ref[:, at] = (gv + dot(k_ref[:, at], later, 1, 0)).astype(BF16)
    squares = squares_ref[...] + far_ref[STEP_ROW + 8 :]
    for i, (weight_ref, out) in enumerate(((gain_ref, new_gain_ref), (bias_ref, new_bias_ref))):
        ratio = jnp.sqrt(squares[i : i + 1]) / jnp.sqrt(squares[2 + i : 3 + i] + TRUST_EPS)
        steps = (step_ref[i * HALF : (i + 1) * HALF], far_ref[STEP_ROW + i * HALF : STEP_ROW + (i + 1) * HALF])
        for half, step in zip((core, 1 - core), steps):
            at = pl.ds(half * HALF, HALF)
            out[at, :] = weight_ref[at, :] - LEARN_RATE * ratio * step


def call(kernel, outs, *args, scalar=True):
    vmem = pl.BlockSpec(memory_space=pltpu.VMEM)
    specs = [vmem] * len(args)
    if scalar:
        specs[0] = pl.BlockSpec(memory_space=pltpu.SMEM)
    return pl.pallas_call(
        kernel,
        out_shape=[jax.ShapeDtypeStruct(s, d) for s, d in outs],
        in_specs=specs,
        out_specs=[vmem] * len(outs),
        compiler_params=pltpu.CompilerParams(vmem_limit_bytes=VMEM_LIMIT),
    )(*args)


STATE = (HALF, HEAD_DIM, HEAD_DIM)


def swap(array, axis="core", step=1):
    n = lax.axis_size(axis)
    return lax.ppermute(array, axis, [(i, i ^ step) for i in range(n)])


def exchange(array, axis):
    return lax.all_to_all(array, axis, 0, 0, tiled=True)


NEAR = ("y", "l")


def chip_scan(pay, reverse, beside_one, beside_two, given):
    members = GROUP * GROUP
    rows = HALF * HEAD_DIM // members
    extra = pay.shape[1] - rows
    part = (members, rows, HEAD_DIM)
    h_s = lax.axis_index("h").astype(jnp.int32).reshape(1)
    landed = exchange(pay, NEAR)
    if reverse:
        landed, given = lax.optimization_barrier((landed, given))
    sums_shape = (GROUP * rows + extra, HEAD_DIM)
    part_sums, send = call(
        functools.partial(group_kernel, reverse, rows), [(part, F32), (sums_shape, F32)], landed, scalar=False
    )
    near, given = lax.optimization_barrier((swap(send, "h", 1), beside_one(given)))
    (both,) = call(sum_kernel, [(sums_shape, F32)], send, near, scalar=False)
    far, made = lax.optimization_barrier((swap(both, "h", 3), beside_two(given)))
    outs = [(part, F32)] + ([((extra, HEAD_DIM), F32)] if extra else [])
    sums, *rest = call(functools.partial(offset_kernel, reverse, rows), outs, h_s, near, far, both, part_sums)
    return exchange(sums, NEAR).reshape(STATE), rest, made


def per_device(queries, keys, values, grad_out, norm_gain, norm_bias, first_moment, second_moment):
    rows, width = queries.shape
    half = (rows, HALF_WIDTH)
    members = GROUP * GROUP
    slice_rows = HALF * HEAD_DIM // members
    core_s = lax.axis_index("core").astype(jnp.int32).reshape(1)
    by_head = (HEADS_HERE, HEAD_DIM)
    gain, bias = norm_gain.reshape(by_head), norm_bias.reshape(by_head)

    def share_inputs():
        (wide,) = call(widen_kernel, [((4,) + half, F32)], core_s, queries, keys, values, grad_out)
        return swap(wide)

    def local_part(recv):
        return call(
            local_kernel, [((CORES, 4) + half, BF16), ((CORES,) + half, F32)],
            core_s, queries, keys, values, grad_out, recv,
        )

    def near_grads(both, dout, state):
        return call(
            near_kernel,
            [(half, BF16), (half, F32), (half, F32), ((3,) + half, F32), (STATE, F32), (STATE, F32), ((3,) + by_head, F32)],
            core_s, both, dout, state, gain, bias, first_moment, second_moment,
        )

    def share_grads(gq_own, gk_own, gv_own, send, own, other, pack):
        near = swap(send)
        (grad_q,) = call(join_kernel, [((rows, width), BF16)], core_s, gq_own, near)
        return grad_q, gk_own, gv_own, near, own, other, pack

    mine, send = call(pair_kernel, [(STATE, F32)] * 2, core_s, jnp.stack([keys, values]))
    pay, first_state = call(
        add_kernel, [((members, slice_rows, HEAD_DIM), F32), (STATE, F32)], core_s, mine, swap(send)
    )
    before, _, (both, local) = chip_scan(pay, False, lambda recv: recv, local_part, share_inputs())

    pay_shape = (members, slice_rows + GRAD_ROWS, HEAD_DIM)
    state, dout, pay = call(
        norm_kernel,
        [((CORES,) + STATE, BF16), ((CORES,) + half, BF16), (pay_shape, F32)],
        core_s, both, gain, local, before, first_state,
    )
    after, (grads,), (grad_q, gk_own, gv_own, near, own, other, pack) = chip_scan(
        pay, True, lambda tied: near_grads(*tied), lambda tied: share_grads(*tied), (both, dout, state)
    )

    step, squares = call(step_kernel, [(by_head, F32)] * 2, grads, pack, scalar=False)
    after, squares = lax.optimization_barrier((after, lax.psum(squares, "fsdp")))
    (send,) = call(pack_kernel, [((STEP_ROW + 16, HEAD_DIM), F32)], core_s, after, own, step, squares)
    far = swap(send)
    grad_k, grad_v, new_gain, new_bias = call(
        far_kernel, [((rows, width), BF16)] * 2 + [(by_head, F32)] * 2,
        core_s, keys, values, gk_own, gv_own, near, after, other, far, step, squares, gain, bias,
    )
    return grad_q, grad_k, grad_v, new_gain.reshape(width), new_bias.reshape(width)


def solution(mesh):
    seq, fsdp = mesh.devices.shape
    fine = Mesh(
        mesh.devices.reshape(GROUP, seq // (GROUP * GROUP * CORES), GROUP, CORES, fsdp), ("y", "h", "l", "core", "fsdp")
    )
    big = P(("y", "h", "l", "core"), "fsdp")
    return jax.shard_map(
        per_device,
        mesh=fine,
        in_specs=(big, big, big, big, P("fsdp"), P("fsdp"), P(None, "fsdp"), P(None, "fsdp")),
        out_specs=(big, big, big, P("fsdp"), P("fsdp")),
        check_vma=False,
    )
```

time: 140 us -> 133 us (0.950)
  local copies, waits for them, and re-layouts: 9.8 us -> 2.12 us
  starting transfers between devices: 53.9 us -> 47.6 us
  blocking collectives: 34.3 us -> 40.3 us
  waiting for transfers between devices: 29.4 us -> 32.1 us
  Pallas kernels: 10.2 us -> 8.51 us
    all_to_all x4 -> x2, starting transfers between devices: 27.6 us -> 7.2 us  [exchange(): return lax.all_to_all(array, axis, 0, 0, tiled=True)]
    ppermute x5 -> x8, waiting for transfers between devices: 4.35 us -> 24.6 us  [swap(): return lax.ppermute(array, axis, [(i, i ^ step) for i in range(n)])]
    all_to_all x4 -> x2, waiting for transfers between devices: 25.1 us -> 7.54 us  [exchange(): return lax.all_to_all(array, axis, 0, 0, tiled=True)]
    ppermute x5 -> x8, starting transfers between devices: 26.3 us -> 40.4 us  [swap(): return lax.ppermute(array, axis, [(i, i ^ step) for i in range(n)])]
    unnamed x40 -> x24, local copies, waits for them, and re-layouts: 9.2 us -> 2.12 us
    all_to_all x2, blocking collectives: 25.7 us -> 31.6 us  [exchange(): return lax.all_to_all(array, axis, 0, 0, tiled=True)]
    pallas_call x14 -> x16, Pallas kernels: 10.2 us -> 8.51 us  [call(): pl.pallas_call(kernel, out_shape=[jax.ShapeDtypeStruct(s, d) for s, d in...]
  transfers between devices with their start and end apart: 9 -> 10, of which waited for: 7 -> 7; matrix products, arithmetic and copies ran while one was open for 0% -> 0% of each run, Pallas kernels for 4% -> 3%
where the time goes in v3:
time: 133 us
  starting transfers between devices  47.6 us (36%)
  blocking collectives  40.3 us (30%)
  waiting for transfers between devices  32.1 us (24%)
  Pallas kernels  8.51 us (6%)
  local copies, waits for them, and re-layouts  2.12 us (2%)
    ppermute x8, starting transfers between devices, swap(): return lax.ppermute(array, axis, [(i, i ^ step) for i in range(n)])  40.4 us
    all_to_all x2, blocking collectives, exchange(): return lax.all_to_all(array, axis, 0, 0, tiled=True)  31.6 us
    ppermute x8, waiting for transfers between devices, swap(): return lax.ppermute(array, axis, [(i, i ^ step) for i in range(n)])  24.6 us
    psum x1, blocking collectives, per_device(): lax.psum(squares, 'fsdp')  8.77 us
    pallas_call x16, Pallas kernels, call(): pl.pallas_call(kernel, out_shape=[jax.ShapeDtypeStruct(s, d) for s, d in...  8.51 us
    all_to_all x2, waiting for transfers between devices, exchange(): return lax.all_to_all(array, axis, 0, 0, tiled=True)  7.54 us
    all_to_all x2, starting transfers between devices, exchange(): return lax.all_to_all(array, axis, 0, 0, tiled=True)  7.2 us
  transfers between devices with their start and end apart: 10, of which 7 were waited for; matrix products, arithmetic and copies ran while one was open for 0% of the time, Pallas kernels for 3%

profile of v3, /device:TPU:1, one launch (start us, length us, event | category | flops | bytes accessed | tf_op | source)
XLA Modules:
  0.0 132.6 jit_solution(2467920115398571751)
XLA Ops:
  0.6 1.1 pad_maximum_fusion.kv_ref
  1.7 0.3 shard_map.119
  2.0 8.8 %collective-permute-start = (f32[4,128,128]{2,1,0:T(8,128)S(1)}, f32[4,128,128]{2,1,0:T(8,128)S(1)}, u32[]{:S(2)}, u32[]{:S(2)}) collective-permute-start(f32[4,128,128]{2,1,0:T(8,128)S(1)} %get-tuple-element.61), channel_id=1, source_target_pairs={{0,4},{4,0},{1,5},{5,1},{2,6},{6,2},{3,7},{7,3},{8,12},{12,8},{9,1... | collective-permute-start | bytes 786440 | tf_op jit(solution)/shard_map/ppermute | solution.py:288
  10.8 1.1 collective-permute-done.b_ref
  12.0 0.7 shard_map.120
  12.7 0.7 copy-done.4
  13.4 3.7 %all-to-all-start = ((f32[16,32,128]{2,1,0:T(8,128)}), f32[16,32,128]{2,1,0:T(8,128)S(1)}, u32[]{:S(2)}, u32[]{:S(2)}) async-start(f32[16,32,128]{2,1,0:T(8,128)} %get-tuple-element.62), calls=%async_computation | async-start | bytes 524288 | tf_op jit(solution)/shard_map/all_to_all | solution.py:292
  17.2 2.3 %collective-permute-start.2 = (f32[4,128,512]{2,1,0:T(8,128)S(1)}, f32[4,128,512]{2,1,0:T(8,128)S(1)}, u32[]{:S(2)}, u32[]{:S(2)}) collective-permute-start(f32[4,128,512]{2,1,0:T(8,128)S(1)} %shard_map.122), channel_id=1, source_target_pairs={{0,4},{4,0},{1,5},{5,1},{2,6},{6,2},{3,7},{7,3},{8,12},{12,8},{9,1... | collective-permute-start | bytes 3145736 | tf_op jit(solution)/shard_map/ppermute | solution.py:288
  19.5 7.5 %all-to-all-done.x_ref = f32[16,32,128]{2,1,0:T(8,128)S(1)} async-done(((f32[16,32,128]{2,1,0:T(8,128)}), f32[16,32,128]{2,1,0:T(8,128)S(1)}, u32[]{:S(2)}, u32[]{:S(2)}) %all-to-all-start) | async-done | bytes 262176 | tf_op jit(solution)/shard_map/all_to_all | solution.py:292
  27.1 0.7 copy-done.6
  27.8 8.2 %collective-permute-start.1 = (f32[128,128]{1,0:T(8,128)S(1)}, f32[128,128]{1,0:T(8,128)S(1)}, u32[]{:S(2)}, u32[]{:S(2)}) collective-permute-start(f32[128,128]{1,0:T(8,128)S(1)} %get-tuple-element.63.a_ref), channel_id=1, source_target_pairs={{0,32},{32,0},{64,96},{96,64},{1,33},{33,1},{65,97},{97,65},{2,34}... | collective-permute-start | bytes 196616 | tf_op jit(solution)/shard_map/ppermute | solution.py:288
  36.0 6.3 %collective-permute-done.1.b_ref.near_ref = f32[128,128]{1,0:T(8,128)S(1)} collective-permute-done((f32[128,128]{1,0:T(8,128)S(1)}, f32[128,128]{1,0:T(8,128)S(1)}, u32[]{:S(2)}, u32[]{:S(2)}) %collective-permute-start.1) | collective-permute-done | bytes 65568 | tf_op jit(solution)/shard_map/ppermute | solution.py:288
  42.3 5.2 %collective-permute-start.3 = (f32[128,128]{1,0:T(8,128)S(1)}, f32[128,128]{1,0:T(8,128)S(1)}, u32[]{:S(2)}, u32[]{:S(2)}) collective-permute-start(f32[128,128]{1,0:T(8,128)S(1)} %shard_map.123.mine_ref), channel_id=1, source_target_pairs={{0,96},{32,64},{64,32},{96,0},{1,97},{33,65},{65,33},{97,1},{2,98}... | collective-permute-start | bytes 196616 | tf_op jit(solution)/shard_map/ppermute | solution.py:288
  47.6 1.4 %shard_map.124 = (bf16[2,4,128,512]{3,2,1,0:T(8,128)(2,1)S(1)}, f32[2,128,512]{2,1,0:T(8,128)S(1)}) custom-call(s32[1]{0:T(128)} %bitcast.core_ref, bf16[128,1024]{1,0:T(8,128)(2,1)S(1)} %copy-done.2, bf16[128,1024]{1,0:T(8,128)(2,1)S(1)} %copy-done, bf16[128,1024]{1,0:T(8,128)(2,1)S(1)} %copy-done.1, bf16[128,1024]{1,0:T(8,128)(2,1)S(1)} %copy-done.3, ...), custom_call_target="tpu_custom_call" | custom-call | tf_op jit(solution)/shard_map/pallas_call | solution.py:274
  49.0 2.4 %collective-permute-done.3.far_ref = f32[128,128]{1,0:T(8,128)S(1)} collective-permute-done((f32[128,128]{1,0:T(8,128)S(1)}, f32[128,128]{1,0:T(8,128)S(1)}, u32[]{:S(2)}, u32[]{:S(2)}) %collective-permute-start.3) | collective-permute-done | bytes 65568 | tf_op jit(solution)/shard_map/ppermute | solution.py:288
  51.5 16.8 %all_to_all.20 = f32[16,32,128]{2,1,0:T(8,128)S(1)} all-to-all(f32[16,32,128]{2,1,0:T(8,128)S(1)} %shard_map.125), channel_id=1, replica_groups=mesh['y'=4,'h'=4,'l'=4,'core'=2,'fsdp'=4] {'y','l'}, dimensions={0} | all-to-all | bytes 524288 | tf_op jit(solution)/shard_map/all_to_all | solution.py:292
  68.2 0.7 copy-done.8
  68.9 1.0 shard_map.126
  69.9 14.8 %all_to_all.21.x_ref = f32[16,40,128]{2,1,0:T(8,128)S(1)} all-to-all(f32[16,40,128]{2,1,0:T(8,128)S(1)} %get-tuple-element.73), channel_id=1, replica_groups=mesh['y'=4,'h'=4,'l'=4,'core'=2,'fsdp'=4] {'y','l'}, dimensions={0} | all-to-all | bytes 655360 | tf_op jit(solution)/shard_map/all_to_all | solution.py:292
  84.7 3.3 %collective-permute-start.4 = (f32[136,128]{1,0:T(8,128)S(1)}, f32[136,128]{1,0:T(8,128)S(1)}, u32[]{:S(2)}, u32[]{:S(2)}) collective-permute-start(f32[136,128]{1,0:T(8,128)S(1)} %get-tuple-element.77.a_ref), channel_id=1, source_target_pairs={{0,32},{32,0},{64,96},{96,64},{1,33},{33,1},{65,97},{97,65},{2,34}... | collective-permute-start | bytes 208904 | tf_op jit(solution)/shard_map/ppermute | solution.py:288
  88.0 2.2 %shard_map.128 = (bf16[128,512]{1,0:T(8,128)(2,1)S(1)}, f32[128,512]{1,0:T(8,128)S(1)}, f32[128,512]{1,0:T(8,128)S(1)}, f32[3,128,512]{2,1,0:T(8,128)S(1)}, f32[...) custom-call(s32[1]{0:T(128)} %bitcast.core_ref, ...), custom_call_target="tpu_custom_call" | custom-call | tf_op jit(solution)/shard_map/pallas_call | solution.py:274
  90.2 7.0 %collective-permute-done.4.b_ref.near_ref = f32[136,128]{1,0:T(8,128)S(1)} collective-permute-done((f32[136,128]{1,0:T(8,128)S(1)}, f32[136,128]{1,0:T(8,128)S(1)}, u32[]{:S(2)}, u32[]{:S(2)}) %collective-permute-start.4) | collective-permute-done | bytes 69664 | tf_op jit(solution)/shard_map/ppermute | solution.py:288
  97.2 2.8 %collective-permute-start.6 = (f32[3,128,512]{2,1,0:T(8,128)S(1)}, f32[3,128,512]{2,1,0:T(8,128)S(1)}, u32[]{:S(2)}, u32[]{:S(2)}) collective-permute-start(f32[3,128,512]{2,1,0:T(8,128)S(1)} %get-tuple-element.90), channel_id=1, source_target_pairs={{0,4},{4,0},{1,5},{5,1},{2,6},{6,2},{3,7},{7,3},{8,12},{12,8},{9,1... | collective-permute-start | bytes 2359304 | tf_op jit(solution)/shard_map/ppermute | solution.py:288
  100.1 2.4 %collective-permute-start.5 = (f32[136,128]{1,0:T(8,128)S(1)}, f32[136,128]{1,0:T(8,128)S(1)}, u32[]{:S(2)}, u32[]{:S(2)}) collective-permute-start(f32[136,128]{1,0:T(8,128)S(1)} %shard_map.129.mine_ref), channel_id=1, source_target_pairs={{0,96},{32,64},{64,32},{96,0},{1,97},{33,65},{65,33},{97,1},{2,98}... | collective-permute-start | bytes 208904 | tf_op jit(solution)/shard_map/ppermute | solution.py:288
  102.6 0.7 shard_map.130
  103.3 6.4 %collective-permute-done.5.far_ref = f32[136,128]{1,0:T(8,128)S(1)} collective-permute-done((f32[136,128]{1,0:T(8,128)S(1)}, f32[136,128]{1,0:T(8,128)S(1)}, u32[]{:S(2)}, u32[]{:S(2)}) %collective-permute-start.5) | collective-permute-done | bytes 69664 | tf_op jit(solution)/shard_map/ppermute | solution.py:288
  109.7 0.7 shard_map.131
  110.5 3.5 %all-to-all-start.3 = ((f32[16,32,128]{2,1,0:T(8,128)}), f32[16,32,128]{2,1,0:T(8,128)S(1)}, u32[]{:S(2)}, u32[]{:S(2)}) async-start(f32[16,32,128]{2,1,0:T(8,128)} %get-tuple-element.102), calls=%async_computation.3 | async-start | bytes 524288 | tf_op jit(solution)/shard_map/all_to_all | solution.py:292
  114.1 8.8 %psum.7.squares_ref = f32[8,128]{1,0:T(8,128)S(1)} all-reduce(f32[8,128]{1,0:T(8,128)S(1)} %get-tuple-element.105), channel_id=1, replica_groups=mesh['y'=4,'h'=4,'l'=4,'core'=2,'fsdp'=4] {'fsdp'}, use_global_device_ids=true, to_apply=%region_0.0 | all-reduce | flops 1024 | bytes 8192 | tf_op jit(solution)/shard_map/psum | solution.py:367
  122.9 7.4 %collective-permute-start.7 = (f32[528,128]{1,0:T(8,128)S(1)}, f32[528,128]{1,0:T(8,128)S(1)}, u32[]{:S(2)}, u32[]{:S(2)}) collective-permute-start(f32[528,128]{1,0:T(8,128)S(1)} %shard_map.133), channel_id=1, source_target_pairs={{0,4},{4,0},{1,5},{5,1},{2,6},{6,2},{3,7},{7,3},{8,12},{12,8},{9,1... | collective-permute-start | bytes 811016 | tf_op jit(solution)/shard_map/ppermute | solution.py:288
  130.3 1.2 collective-permute-done.7.far_ref
  131.4 1.2 shard_map.134
  (32 shorter events, 0.4 us)
Async XLA Ops:
  2.0 9.9 %collective-permute-start = (f32[4,128,128]{2,1,0:T(8,128)S(1)}, f32[4,128,128]{2,1,0:T(8,128)S(1)}, u32[]{:S(2)}, u32[]{:S(2)}) collective-permute-start(f32[4,128,128]{2,1,0:T(8,128)S(1)} %get-tuple-element.61), channel_id=1, source_target_pairs={{0,4},{4,0},{1,5},{5,1},{2,6},{6,2},{3,7},{7,3},{8,12},{12,8},{9,1... | collective-permute-start | bytes 786440 | tf_op jit(solution)/shard_map/ppermute | solution.py:288
  11.9 5.1 %copy-start.2 = (bf16[128,1024]{1,0:T(8,128)(2,1)S(1)}, bf16[128,1024]{1,0:T(8,128)(2,1)}, u32[]{:S(2)}) copy-start(bf16[128,1024]{1,0:T(8,128)(2,1)} %q_ref.3) | copy-start | bytes 786436
  11.9 5.1 %copy-start.3 = (bf16[128,1024]{1,0:T(8,128)(2,1)S(1)}, bf16[128,1024]{1,0:T(8,128)(2,1)}, u32[]{:S(2)}) copy-start(bf16[128,1024]{1,0:T(8,128)(2,1)} %g_ref.3) | copy-start | bytes 786436
  12.7 0.7 copy-start.4
  13.4 3.7 %copy-start = (bf16[128,1024]{1,0:T(8,128)(2,1)S(1)}, bf16[128,1024]{1,0:T(8,128)(2,1)}, u32[]{:S(2)}) copy-start(bf16[128,1024]{1,0:T(8,128)(2,1)} %k_ref.5) | copy-start | bytes 786436
  13.4 3.7 %copy-start.1 = (bf16[128,1024]{1,0:T(8,128)(2,1)S(1)}, bf16[128,1024]{1,0:T(8,128)(2,1)}, u32[]{:S(2)}) copy-start(bf16[128,1024]{1,0:T(8,128)(2,1)} %v_ref.5) | copy-start | bytes 786436
  13.4 13.6 %all-to-all-start = ((f32[16,32,128]{2,1,0:T(8,128)}), f32[16,32,128]{2,1,0:T(8,128)S(1)}, u32[]{:S(2)}, u32[]{:S(2)}) async-start(f32[16,32,128]{2,1,0:T(8,128)} %get-tuple-element.62), calls=%async_computation | async-start | bytes 524288 | tf_op jit(solution)/shard_map/all_to_all | solution.py:292
  17.2 18.8 %collective-permute-start.2 = (f32[4,128,512]{2,1,0:T(8,128)S(1)}, f32[4,128,512]{2,1,0:T(8,128)S(1)}, u32[]{:S(2)}, u32[]{:S(2)}) collective-permute-start(f32[4,128,512]{2,1,0:T(8,128)S(1)} %shard_map.122), channel_id=1, source_target_pairs={{0,4},{4,0},{1,5},{5,1},{2,6},{6,2},{3,7},{7,3},{8,12},{12,8},{9,1... | collective-permute-start | bytes 3145736 | tf_op jit(solution)/shard_map/ppermute | solution.py:288
  27.1 0.7 copy-start.6
  27.8 14.6 %collective-permute-start.1 = (f32[128,128]{1,0:T(8,128)S(1)}, f32[128,128]{1,0:T(8,128)S(1)}, u32[]{:S(2)}, u32[]{:S(2)}) collective-permute-start(f32[128,128]{1,0:T(8,128)S(1)} %get-tuple-element.63.a_ref), channel_id=1, source_target_pairs={{0,32},{32,0},{64,96},{96,64},{1,33},{33,1},{65,97},{97,65},{2,34}... | collective-permute-start | bytes 196616 | tf_op jit(solution)/shard_map/ppermute | solution.py:288
  42.3 9.1 %collective-permute-start.3 = (f32[128,128]{1,0:T(8,128)S(1)}, f32[128,128]{1,0:T(8,128)S(1)}, u32[]{:S(2)}, u32[]{:S(2)}) collective-permute-start(f32[128,128]{1,0:T(8,128)S(1)} %shard_map.123.mine_ref), channel_id=1, source_target_pairs={{0,96},{32,64},{64,32},{96,0},{1,97},{33,65},{65,33},{97,1},{2,98}... | collective-permute-start | bytes 196616 | tf_op jit(solution)/shard_map/ppermute | solution.py:288
  47.6 3.8 %copy-start.7 = (f32[16,32,128]{2,1,0:T(8,128)S(1)}, f32[16,32,128]{2,1,0:T(8,128)}, u32[]{:S(2)}) copy-start(f32[16,32,128]{2,1,0:T(8,128)} %copy-done.6) | copy-start | bytes 786436
  51.5 16.8 %copy-start.5 = (f32[4,128,128]{2,1,0:T(8,128)S(1)}, f32[4,128,128]{2,1,0:T(8,128)}, u32[]{:S(2)}) copy-start(f32[4,128,128]{2,1,0:T(8,128)} %copy-done.4) | copy-start | bytes 786436
  68.2 0.7 copy-start.8
  84.7 3.3 %copy-start.9 = (f32[1024]{0:T(1024)S(1)}, f32[1024]{0:T(1024)}, u32[]{:S(2)}) copy-start(f32[1024]{0:T(1024)} %param.13) | copy-start | bytes 12292
  84.7 3.3 %copy-start.10 = (f32[2,1024]{1,0:T(2,128)S(1)}, f32[2,1024]{1,0:T(2,128)}, u32[]{:S(2)}) copy-start(f32[2,1024]{1,0:T(2,128)} %first_ref.1) | copy-start | bytes 24580
  84.7 3.3 %copy-start.11 = (f32[2,1024]{1,0:T(2,128)S(1)}, f32[2,1024]{1,0:T(2,128)}, u32[]{:S(2)}) copy-start(f32[2,1024]{1,0:T(2,128)} %second_ref.1) | copy-start | bytes 24580
  84.7 12.5 %collective-permute-start.4 = (f32[136,128]{1,0:T(8,128)S(1)}, f32[136,128]{1,0:T(8,128)S(1)}, u32[]{:S(2)}, u32[]{:S(2)}) collective-permute-start(f32[136,128]{1,0:T(8,128)S(1)} %get-tuple-element.77.a_ref), channel_id=1, source_target_pairs={{0,32},{32,0},{64,96},{96,64},{1,33},{33,1},{65,97},{97,65},{2,34}... | collective-permute-start | bytes 208904 | tf_op jit(solution)/shard_map/ppermute | solution.py:288
  97.2 5.3 %collective-permute-start.6 = (f32[3,128,512]{2,1,0:T(8,128)S(1)}, f32[3,128,512]{2,1,0:T(8,128)S(1)}, u32[]{:S(2)}, u32[]{:S(2)}) collective-permute-start(f32[3,128,512]{2,1,0:T(8,128)S(1)} %get-tuple-element.90), channel_id=1, source_target_pairs={{0,4},{4,0},{1,5},{5,1},{2,6},{6,2},{3,7},{7,3},{8,12},{12,8},{9,1... | collective-permute-start | bytes 2359304 | tf_op jit(solution)/shard_map/ppermute | solution.py:288
  100.1 9.6 %collective-permute-start.5 = (f32[136,128]{1,0:T(8,128)S(1)}, f32[136,128]{1,0:T(8,128)S(1)}, u32[]{:S(2)}, u32[]{:S(2)}) collective-permute-start(f32[136,128]{1,0:T(8,128)S(1)} %shard_map.129.mine_ref), channel_id=1, source_target_pairs={{0,96},{32,64},{64,32},{96,0},{1,97},{33,65},{65,33},{97,1},{2,98}... | collective-permute-start | bytes 208904 | tf_op jit(solution)/shard_map/ppermute | solution.py:288
  110.5 12.4 %all-to-all-start.3 = ((f32[16,32,128]{2,1,0:T(8,128)}), f32[16,32,128]{2,1,0:T(8,128)S(1)}, u32[]{:S(2)}, u32[]{:S(2)}) async-start(f32[16,32,128]{2,1,0:T(8,128)} %get-tuple-element.102), calls=%async_computation.3 | async-start | bytes 524288 | tf_op jit(solution)/shard_map/all_to_all | solution.py:292
  122.9 8.5 %collective-permute-start.7 = (f32[528,128]{1,0:T(8,128)S(1)}, f32[528,128]{1,0:T(8,128)S(1)}, u32[]{:S(2)}, u32[]{:S(2)}) collective-permute-start(f32[528,128]{1,0:T(8,128)S(1)} %shard_map.133), channel_id=1, source_target_pairs={{0,4},{4,0},{1,5},{5,1},{2,6},{6,2},{3,7},{7,3},{8,12},{12,8},{9,1... | collective-permute-start | bytes 811016 | tf_op jit(solution)/shard_map/ppermute | solution.py:288

commit v4 on v3

--- a/solution.py
+++ b/solution.py
@@ -59,10 +59,7 @@
             out[j] = dot(k_ref[:, at], v_ref[:, at], 0, 0)
 
 
-def add_kernel(core_ref, a_ref, b_ref, out_ref, first_ref):
-    core = core_ref[0]
-    for j in range(HALF):
-        first_ref[j] = jnp.where(core == 0, a_ref[j], b_ref[j])
+def add_kernel(a_ref, b_ref, out_ref):
     rows = out_ref.shape[1]
     per = HEAD_DIM // rows
     for s in range(out_ref.shape[0]):
@@ -77,7 +74,7 @@
         send_ref[i] = ref[:, at].astype(F32)
 
 
-def local_kernel(core_ref, q_ref, k_ref, v_ref, g_ref, recv_ref, in_ref, loc_ref):
+def local_kernel(core_ref, q_ref, k_ref, v_ref, g_ref, recv_ref, in_ref, loc_ref, first_ref):
     core = core_ref[0]
     causal = causal_mask()
     at = half_at(core)
@@ -86,6 +83,7 @@
         in_ref[1, i] = recv_ref[i].astype(BF16)
     for j in range(HALF):
         there = fixed(j)
+        first_ref[j] = dot(in_ref[core, 1, :, there], in_ref[core, 2, :, there], 0, 0)
         for b in range(CORES):
             q, k, v = (in_ref[b, i, :, there] for i in range(3))
             w = jnp.where(causal, dot(q, k, 1, 1), 0.0).astype(BF16)
@@ -107,22 +105,31 @@
         send_ref[GROUP * rows :] = grads
 
 
-def sum_kernel(a_ref, b_ref, out_ref):
-    out_ref[...] = a_ref[...] + b_ref[...]
-
-
-def offset_kernel(reverse, rows, h_ref, near_ref, far_ref, mine_ref, part_ref, out_ref, *grads_ref):
-    h = h_ref[0]
-    order = list(reversed(range(GROUP))) if reverse else list(range(GROUP))
-    near_first = ((h ^ 1) > h) if reverse else ((h ^ 1) < h)
-    far_first = ((h ^ 3) > h) if reverse else ((h ^ 3) < h)
-    zero = jnp.zeros((rows, HEAD_DIM), F32)
-    for i, y in enumerate(order):
-        offset = zero
-        for ref, first in ((near_ref, near_first), (far_ref, far_first)):
-            up_to = ref[i * rows : (i + 1) * rows]
-            above = ref[(i - 1) * rows : i * rows] if i else zero
-            offset = offset + jnp.where(first, up_to, above)
+def for_group(reverse, rows, ref, i, group, dest):
+    first = (group > dest) if reverse else (group < dest)
+    up_to = ref[i * rows : (i + 1) * rows]
+    above = ref[(i - 1) * rows : i * rows] if i else jnp.zeros((rows, HEAD_DIM), F32)
+    return jnp.where(first, up_to, above)
+
+
+def partners(at_ref):
+    h, core = at_ref[0] // CORES, at_ref[0] % CORES
+    return h, h ^ (1 + 2 * core), h ^ (3 - 2 * core)
+
+
+def sum_kernel(reverse, rows, at_ref, mine_ref, near_ref, out_ref):
+    h, near, far = partners(at_ref)
+    for i in range(GROUP):
+        own = for_group(reverse, rows, mine_ref, i, h, far)
+        out_ref[i * rows : (i + 1) * rows] = own + for_group(reverse, rows, near_ref, i, near, far)
+    if out_ref.shape[0] > GROUP * rows:
+        out_ref[GROUP * rows :] = mine_ref[GROUP * rows :] + near_ref[GROUP * rows :]
+
+
+def offset_kernel(reverse, rows, at_ref, near_ref, far_ref, mine_ref, part_ref, out_ref, *grads_ref):
+    h, near, _ = partners(at_ref)
+    for i, y in enumerate(reversed(range(GROUP)) if reverse else range(GROUP)):
+        offset = for_group(reverse, rows, near_ref, i, near, h) + far_ref[i * rows : (i + 1) * rows]
         for l in range(GROUP):
             out_ref[y * GROUP + l] = part_ref[y * GROUP + l] + offset
     if grads_ref:
@@ -288,6 +295,11 @@
     return lax.ppermute(array, axis, [(i, i ^ step) for i in range(n)])
 
 
+def group_swap(array, steps):
+    pairs = [(h * CORES + c, (h ^ steps[c]) * CORES + c) for h in range(GROUP) for c in range(CORES)]
+    return lax.ppermute(array, ("h", "core"), pairs)
+
+
 def exchange(array, axis):
     return lax.all_to_all(array, axis, 0, 0, tiled=True)
 
@@ -300,7 +312,7 @@
     rows = HALF * HEAD_DIM // members
     extra = pay.shape[1] - rows
     part = (members, rows, HEAD_DIM)
-    h_s = lax.axis_index("h").astype(jnp.int32).reshape(1)
+    at_s = lax.axis_index(("h", "core")).astype(jnp.int32).reshape(1)
     landed = exchange(pay, NEAR)
     if reverse:
         landed, given = lax.optimization_barrier((landed, given))
@@ -308,11 +320,11 @@
     part_sums, send = call(
         functools.partial(group_kernel, reverse, rows), [(part, F32), (sums_shape, F32)], landed, scalar=False
     )
-    near, given = lax.optimization_barrier((swap(send, "h", 1), beside_one(given)))
-    (both,) = call(sum_kernel, [(sums_shape, F32)], send, near, scalar=False)
-    far, made = lax.optimization_barrier((swap(both, "h", 3), beside_two(given)))
+    near, given = lax.optimization_barrier((group_swap(send, (1, 3)), beside_one(given)))
+    (both,) = call(functools.partial(sum_kernel, reverse, rows), [(sums_shape, F32)], at_s, send, near)
+    far, made = lax.optimization_barrier((group_swap(both, (3, 1)), beside_two(given)))
     outs = [(part, F32)] + ([((extra, HEAD_DIM), F32)] if extra else [])
-    sums, *rest = call(functools.partial(offset_kernel, reverse, rows), outs, h_s, near, far, both, part_sums)
+    sums, *rest = call(functools.partial(offset_kernel, reverse, rows), outs, at_s, near, far, both, part_sums)
     return exchange(sums, NEAR).reshape(STATE), rest, made
 
 
@@ -331,7 +343,7 @@
 
     def local_part(recv):
         return call(
-            local_kernel, [((CORES, 4) + half, BF16), ((CORES,) + half, F32)],
+            local_kernel, [((CORES, 4) + half, BF16), ((CORES,) + half, F32), (STATE, F32)],
             core_s, queries, keys, values, grad_out, recv,
         )
 
@@ -348,10 +360,8 @@
         return grad_q, gk_own, gv_own, near, own, other, pack
 
     mine, send = call(pair_kernel, [(STATE, F32)] * 2, core_s, jnp.stack([keys, values]))
-    pay, first_state = call(
-        add_kernel, [((members, slice_rows, HEAD_DIM), F32), (STATE, F32)], core_s, mine, swap(send)
-    )
-    before, _, (both, local) = chip_scan(pay, False, lambda recv: recv, local_part, share_inputs())
+    (pay,) = call(add_kernel, [((members, slice_rows, HEAD_DIM), F32)], mine, swap(send), scalar=False)
+    before, _, (both, local, first_state) = chip_scan(pay, False, lambda recv: recv, local_part, share_inputs())
 
     pay_shape = (members, slice_rows + GRAD_ROWS, HEAD_DIM)
     state, dout, pay = call(

time: 133 us -> 125 us (0.940)
  starting transfers between devices: 47.6 us -> 60.3 us
  waiting for transfers between devices: 32.1 us -> 20.8 us
  blocking collectives: 40.3 us -> 32 us
  local copies, waits for them, and re-layouts: 2.12 us -> 0.74 us
    ppermute x0 -> x4, starting transfers between devices: none -> 27.2 us  [group_swap(): return lax.ppermute(array, ('h', 'core'), pairs)]
    ppermute x8 -> x4, waiting for transfers between devices: 24.6 us -> 2.3 us  [swap(): return lax.ppermute(array, axis, [(i, i ^ step) for i in range(n)])]
    ppermute x8 -> x4, starting transfers between devices: 40.4 us -> 25.9 us  [swap(): return lax.ppermute(array, axis, [(i, i ^ step) for i in range(n)])]
    ppermute x0 -> x4, waiting for transfers between devices: none -> 10.3 us  [group_swap(): return lax.ppermute(array, ('h', 'core'), pairs)]
    all_to_all x2, blocking collectives: 31.6 us -> 23.3 us  [exchange(): return lax.all_to_all(array, axis, 0, 0, tiled=True)]
    unnamed x24 -> x20, local copies, waits for them, and re-layouts: 2.12 us -> 0.74 us
  transfers between devices with their start and end apart: 10 -> 10, of which waited for: 7 -> 8; matrix products, arithmetic and copies ran while one was open for 0% -> 0% of each run, Pallas kernels for 3% -> 3%
where the time goes in v4:
time: 125 us; the launch traced here: 124 us
  starting transfers between devices  60.3 us (48%)
  blocking collectives  32 us (26%)
  waiting for transfers between devices  20.8 us (17%)
  Pallas kernels  8.18 us (7%)
    ppermute x4, starting transfers between devices, group_swap(): return lax.ppermute(array, ('h', 'core'), pairs)  27.2 us
    ppermute x4, starting transfers between devices, swap(): return lax.ppermute(array, axis, [(i, i ^ step) for i in range(n)])  25.9 us
    all_to_all x2, blocking collectives, exchange(): return lax.all_to_all(array, axis, 0, 0, tiled=True)  23.3 us
    ppermute x4, waiting for transfers between devices, group_swap(): return lax.ppermute(array, ('h', 'core'), pairs)  10.3 us
    psum x1, blocking collectives, per_device(): lax.psum(squares, 'fsdp')  8.77 us
    all_to_all x2, waiting for transfers between devices, exchange(): return lax.all_to_all(array, axis, 0, 0, tiled=True)  8.21 us
    pallas_call x16, Pallas kernels, call(): pl.pallas_call(kernel, out_shape=[jax.ShapeDtypeStruct(s, d) for s, d in...  8.18 us
    all_to_all x2, starting transfers between devices, exchange(): return lax.all_to_all(array, axis, 0, 0, tiled=True)  7.2 us
  transfers between devices with their start and end apart: 10, of which 8 were waited for; matrix products, arithmetic and copies ran while one was open for 0% of the time, Pallas kernels for 3%

profile of v4, /device:TPU:1, one launch (start us, length us, event | category | flops | bytes accessed | tf_op | source)
XLA Modules:
  0.0 124.0 jit_solution(10615483602941156957)
XLA Ops:
  0.6 1.1 pad_maximum_fusion.kv_ref
  1.7 0.3 shard_map.119
  2.0 8.8 %collective-permute-start = (f32[4,128,128]{2,1,0:T(8,128)S(1)}, f32[4,128,128]{2,1,0:T(8,128)S(1)}, u32[]{:S(2)}, u32[]{:S(2)}) collective-permute-start(f32[4,128,128]{2,1,0:T(8,128)S(1)} %get-tuple-element.61), channel_id=1, source_target_pairs={{0,4},{4,0},{1,5},{5,1},{2,6},{6,2},{3,7},{7,3},{8,12},{12,8},{9,1... | collective-permute-start | bytes 786440 | tf_op jit(solution)/shard_map/ppermute | solution.py:295
  10.8 1.1 collective-permute-done.b_ref
  12.0 0.7 shard_map.120
  12.7 3.7 %all-to-all-start = ((f32[16,32,128]{2,1,0:T(8,128)}), f32[16,32,128]{2,1,0:T(8,128)S(1)}, u32[]{:S(2)}, u32[]{:S(2)}) async-start(f32[16,32,128]{2,1,0:T(8,128)} %shard_map.120), calls=%async_computation | async-start | bytes 524288 | tf_op jit(solution)/shard_map/all_to_all | solution.py:304
  16.5 2.3 %collective-permute-start.2 = (f32[4,128,512]{2,1,0:T(8,128)S(1)}, f32[4,128,512]{2,1,0:T(8,128)S(1)}, u32[]{:S(2)}, u32[]{:S(2)}) collective-permute-start(f32[4,128,512]{2,1,0:T(8,128)S(1)} %shard_map.122), channel_id=1, source_target_pairs={{0,4},{4,0},{1,5},{5,1},{2,6},{6,2},{3,7},{7,3},{8,12},{12,8},{9,1... | collective-permute-start | bytes 3145736 | tf_op jit(solution)/shard_map/ppermute | solution.py:295
  18.8 7.5 %all-to-all-done.x_ref = f32[16,32,128]{2,1,0:T(8,128)S(1)} async-done(((f32[16,32,128]{2,1,0:T(8,128)}), f32[16,32,128]{2,1,0:T(8,128)S(1)}, u32[]{:S(2)}, u32[]{:S(2)}) %all-to-all-start) | async-done | bytes 262176 | tf_op jit(solution)/shard_map/all_to_all | solution.py:304
  26.4 0.7 copy-done.4
  27.0 9.1 %collective-permute-start.1 = (f32[128,128]{1,0:T(8,128)S(1)}, f32[128,128]{1,0:T(8,128)S(1)}, u32[]{:S(2)}, u32[]{:S(2)}) collective-permute-start(f32[128,128]{1,0:T(8,128)S(1)} %get-tuple-element.62.mine_ref), channel_id=1, source_target_pairs={{0,32},{4,100},{32,0},{36,68},{64,96},{68,36},{96,64},{100,4},{1,3... | collective-permute-start | bytes 196616 | tf_op jit(solution)/shard_map/ppermute | solution.py:300
  36.2 2.9 %collective-permute-done.1.near_ref = f32[128,128]{1,0:T(8,128)S(1)} collective-permute-done((f32[128,128]{1,0:T(8,128)S(1)}, f32[128,128]{1,0:T(8,128)S(1)}, u32[]{:S(2)}, u32[]{:S(2)}) %collective-permute-start.1) | collective-permute-done | bytes 65568 | tf_op jit(solution)/shard_map/ppermute | solution.py:300
  39.1 7.2 %collective-permute-start.3 = (f32[128,128]{1,0:T(8,128)S(1)}, f32[128,128]{1,0:T(8,128)S(1)}, u32[]{:S(2)}, u32[]{:S(2)}) collective-permute-start(f32[128,128]{1,0:T(8,128)S(1)} %shard_map.123.mine_ref), channel_id=1, source_target_pairs={{0,96},{4,36},{32,64},{36,4},{64,32},{68,100},{96,0},{100,68},{1,9... | collective-permute-start | bytes 196616 | tf_op jit(solution)/shard_map/ppermute | solution.py:300
  46.3 1.0 shard_map.124
  47.4 1.6 %collective-permute-done.3.far_ref = f32[128,128]{1,0:T(8,128)S(1)} collective-permute-done((f32[128,128]{1,0:T(8,128)S(1)}, f32[128,128]{1,0:T(8,128)S(1)}, u32[]{:S(2)}, u32[]{:S(2)}) %collective-permute-start.3) | collective-permute-done | bytes 65568 | tf_op jit(solution)/shard_map/ppermute | solution.py:300
  49.0 11.4 %all_to_all.20 = f32[16,32,128]{2,1,0:T(8,128)S(1)} all-to-all(f32[16,32,128]{2,1,0:T(8,128)S(1)} %shard_map.125), channel_id=1, replica_groups=mesh['y'=4,'h'=4,'l'=4,'core'=2,'fsdp'=4] {'y','l'}, dimensions={0} | all-to-all | bytes 524288 | tf_op jit(solution)/shard_map/all_to_all | solution.py:304
  60.4 1.0 shard_map.126
  61.4 11.8 %all_to_all.21.x_ref = f32[16,40,128]{2,1,0:T(8,128)S(1)} all-to-all(f32[16,40,128]{2,1,0:T(8,128)S(1)} %get-tuple-element.73), channel_id=1, replica_groups=mesh['y'=4,'h'=4,'l'=4,'core'=2,'fsdp'=4] {'y','l'}, dimensions={0} | all-to-all | bytes 655360 | tf_op jit(solution)/shard_map/all_to_all | solution.py:304
  73.3 6.8 %collective-permute-start.4 = (f32[136,128]{1,0:T(8,128)S(1)}, f32[136,128]{1,0:T(8,128)S(1)}, u32[]{:S(2)}, u32[]{:S(2)}) collective-permute-start(f32[136,128]{1,0:T(8,128)S(1)} %get-tuple-element.77.mine_ref), channel_id=1, source_target_pairs={{0,32},{4,100},{32,0},{36,68},{64,96},{68,36},{96,64},{100,4},{1,3... | collective-permute-start | bytes 208904 | tf_op jit(solution)/shard_map/ppermute | solution.py:300
  80.1 2.2 %shard_map.128 = (bf16[128,512]{1,0:T(8,128)(2,1)S(1)}, f32[128,512]{1,0:T(8,128)S(1)}, f32[128,512]{1,0:T(8,128)S(1)}, f32[3,128,512]{2,1,0:T(8,128)S(1)}, f32[...) custom-call(s32[1]{0:T(128)} %bitcast.1.core_ref, ...), custom_call_target="tpu_custom_call" | custom-call | tf_op jit(solution)/shard_map/pallas_call | solution.py:281
  82.3 1.2 collective-permute-done.4.near_ref
  83.5 10.5 %collective-permute-start.6 = (f32[3,128,512]{2,1,0:T(8,128)S(1)}, f32[3,128,512]{2,1,0:T(8,128)S(1)}, u32[]{:S(2)}, u32[]{:S(2)}) collective-permute-start(f32[3,128,512]{2,1,0:T(8,128)S(1)} %get-tuple-element.90), channel_id=1, source_target_pairs={{0,4},{4,0},{1,5},{5,1},{2,6},{6,2},{3,7},{7,3},{8,12},{12,8},{9,1... | collective-permute-start | bytes 2359304 | tf_op jit(solution)/shard_map/ppermute | solution.py:295
  94.0 4.1 %collective-permute-start.5 = (f32[136,128]{1,0:T(8,128)S(1)}, f32[136,128]{1,0:T(8,128)S(1)}, u32[]{:S(2)}, u32[]{:S(2)}) collective-permute-start(f32[136,128]{1,0:T(8,128)S(1)} %shard_map.129.mine_ref), channel_id=1, source_target_pairs={{0,96},{4,36},{32,64},{36,4},{64,32},{68,100},{96,0},{100,68},{1,9... | collective-permute-start | bytes 208904 | tf_op jit(solution)/shard_map/ppermute | solution.py:300
  98.0 0.7 shard_map.130
  98.8 4.7 %collective-permute-done.5.far_ref = f32[136,128]{1,0:T(8,128)S(1)} collective-permute-done((f32[136,128]{1,0:T(8,128)S(1)}, f32[136,128]{1,0:T(8,128)S(1)}, u32[]{:S(2)}, u32[]{:S(2)}) %collective-permute-start.5) | collective-permute-done | bytes 69664 | tf_op jit(solution)/shard_map/ppermute | solution.py:300
  103.4 0.7 shard_map.131
  104.2 3.5 %all-to-all-start.3 = ((f32[16,32,128]{2,1,0:T(8,128)}), f32[16,32,128]{2,1,0:T(8,128)S(1)}, u32[]{:S(2)}, u32[]{:S(2)}) async-start(f32[16,32,128]{2,1,0:T(8,128)} %get-tuple-element.102), calls=%async_computation.3 | async-start | bytes 524288 | tf_op jit(solution)/shard_map/all_to_all | solution.py:304
  107.7 0.1 shard_map.132
  107.8 8.8 %psum.7.squares_ref = f32[8,128]{1,0:T(8,128)S(1)} all-reduce(f32[8,128]{1,0:T(8,128)S(1)} %get-tuple-element.105), channel_id=1, replica_groups=mesh['y'=4,'h'=4,'l'=4,'core'=2,'fsdp'=4] {'fsdp'}, use_global_device_ids=true, to_apply=%region_0.0 | all-reduce | flops 1024 | bytes 8192 | tf_op jit(solution)/shard_map/psum | solution.py:377
  116.6 0.7 all-to-all-done.3
  117.3 4.3 %collective-permute-start.7 = (f32[528,128]{1,0:T(8,128)S(1)}, f32[528,128]{1,0:T(8,128)S(1)}, u32[]{:S(2)}, u32[]{:S(2)}) collective-permute-start(f32[528,128]{1,0:T(8,128)S(1)} %shard_map.133), channel_id=1, source_target_pairs={{0,4},{4,0},{1,5},{5,1},{2,6},{6,2},{3,7},{7,3},{8,12},{12,8},{9,1... | collective-permute-start | bytes 811016 | tf_op jit(solution)/shard_map/ppermute | solution.py:295
  121.6 1.2 collective-permute-done.7.far_ref
  122.8 1.2 shard_map.134
  (28 shorter events, 0.3 us)
Async XLA Ops:
  2.0 9.9 %collective-permute-start = (f32[4,128,128]{2,1,0:T(8,128)S(1)}, f32[4,128,128]{2,1,0:T(8,128)S(1)}, u32[]{:S(2)}, u32[]{:S(2)}) collective-permute-start(f32[4,128,128]{2,1,0:T(8,128)S(1)} %get-tuple-element.61), channel_id=1, source_target_pairs={{0,4},{4,0},{1,5},{5,1},{2,6},{6,2},{3,7},{7,3},{8,12},{12,8},{9,1... | collective-permute-start | bytes 786440 | tf_op jit(solution)/shard_map/ppermute | solution.py:295
  11.9 4.4 %copy-start.2 = (bf16[128,1024]{1,0:T(8,128)(2,1)S(1)}, bf16[128,1024]{1,0:T(8,128)(2,1)}, u32[]{:S(2)}) copy-start(bf16[128,1024]{1,0:T(8,128)(2,1)} %q_ref.3) | copy-start | bytes 786436
  11.9 4.4 %copy-start.3 = (bf16[128,1024]{1,0:T(8,128)(2,1)S(1)}, bf16[128,1024]{1,0:T(8,128)(2,1)}, u32[]{:S(2)}) copy-start(bf16[128,1024]{1,0:T(8,128)(2,1)} %g_ref.3) | copy-start | bytes 786436
  12.7 3.7 %copy-start = (bf16[128,1024]{1,0:T(8,128)(2,1)S(1)}, bf16[128,1024]{1,0:T(8,128)(2,1)}, u32[]{:S(2)}) copy-start(bf16[128,1024]{1,0:T(8,128)(2,1)} %k_ref.5) | copy-start | bytes 786436
  12.7 3.7 %copy-start.1 = (bf16[128,1024]{1,0:T(8,128)(2,1)S(1)}, bf16[128,1024]{1,0:T(8,128)(2,1)}, u32[]{:S(2)}) copy-start(bf16[128,1024]{1,0:T(8,128)(2,1)} %v_ref.5) | copy-start | bytes 786436
  12.7 13.6 %all-to-all-start = ((f32[16,32,128]{2,1,0:T(8,128)}), f32[16,32,128]{2,1,0:T(8,128)S(1)}, u32[]{:S(2)}, u32[]{:S(2)}) async-start(f32[16,32,128]{2,1,0:T(8,128)} %shard_map.120), calls=%async_computation | async-start | bytes 524288 | tf_op jit(solution)/shard_map/all_to_all | solution.py:304
  16.5 19.7 %collective-permute-start.2 = (f32[4,128,512]{2,1,0:T(8,128)S(1)}, f32[4,128,512]{2,1,0:T(8,128)S(1)}, u32[]{:S(2)}, u32[]{:S(2)}) collective-permute-start(f32[4,128,512]{2,1,0:T(8,128)S(1)} %shard_map.122), channel_id=1, source_target_pairs={{0,4},{4,0},{1,5},{5,1},{2,6},{6,2},{3,7},{7,3},{8,12},{12,8},{9,1... | collective-permute-start | bytes 3145736 | tf_op jit(solution)/shard_map/ppermute | solution.py:295
  26.3 0.7 copy-start.4
  27.0 12.1 %collective-permute-start.1 = (f32[128,128]{1,0:T(8,128)S(1)}, f32[128,128]{1,0:T(8,128)S(1)}, u32[]{:S(2)}, u32[]{:S(2)}) collective-permute-start(f32[128,128]{1,0:T(8,128)S(1)} %get-tuple-element.62.mine_ref), channel_id=1, source_target_pairs={{0,32},{4,100},{32,0},{36,68},{64,96},{68,36},{96,64},{100,4},{1,3... | collective-permute-start | bytes 196616 | tf_op jit(solution)/shard_map/ppermute | solution.py:300
  39.1 9.8 %copy-start.5 = (f32[16,32,128]{2,1,0:T(8,128)S(1)}, f32[16,32,128]{2,1,0:T(8,128)}, u32[]{:S(2)}) copy-start(f32[16,32,128]{2,1,0:T(8,128)} %copy-done.4) | copy-start | bytes 786436
  39.1 9.8 %collective-permute-start.3 = (f32[128,128]{1,0:T(8,128)S(1)}, f32[128,128]{1,0:T(8,128)S(1)}, u32[]{:S(2)}, u32[]{:S(2)}) collective-permute-start(f32[128,128]{1,0:T(8,128)S(1)} %shard_map.123.mine_ref), channel_id=1, source_target_pairs={{0,96},{4,36},{32,64},{36,4},{64,32},{68,100},{96,0},{100,68},{1,9... | collective-permute-start | bytes 196616 | tf_op jit(solution)/shard_map/ppermute | solution.py:300
  49.0 11.4 %copy-start.6 = (f32[1024]{0:T(1024)S(1)}, f32[1024]{0:T(1024)}, u32[]{:S(2)}) copy-start(f32[1024]{0:T(1024)} %param.12) | copy-start | bytes 12292
  73.2 6.8 %copy-start.7 = (f32[1024]{0:T(1024)S(1)}, f32[1024]{0:T(1024)}, u32[]{:S(2)}) copy-start(f32[1024]{0:T(1024)} %param.13) | copy-start | bytes 12292
  73.2 6.8 %copy-start.8 = (f32[2,1024]{1,0:T(2,128)S(1)}, f32[2,1024]{1,0:T(2,128)}, u32[]{:S(2)}) copy-start(f32[2,1024]{1,0:T(2,128)} %first_ref.1) | copy-start | bytes 24580
  73.2 6.9 %copy-start.9 = (f32[2,1024]{1,0:T(2,128)S(1)}, f32[2,1024]{1,0:T(2,128)}, u32[]{:S(2)}) copy-start(f32[2,1024]{1,0:T(2,128)} %second_ref.1) | copy-start | bytes 24580
  73.3 10.2 %collective-permute-start.4 = (f32[136,128]{1,0:T(8,128)S(1)}, f32[136,128]{1,0:T(8,128)S(1)}, u32[]{:S(2)}, u32[]{:S(2)}) collective-permute-start(f32[136,128]{1,0:T(8,128)S(1)} %get-tuple-element.77.mine_ref), channel_id=1, source_target_pairs={{0,32},{4,100},{32,0},{36,68},{64,96},{68,36},{96,64},{100,4},{1,3... | collective-permute-start | bytes 208904 | tf_op jit(solution)/shard_map/ppermute | solution.py:300
  83.5 14.6 %collective-permute-start.6 = (f32[3,128,512]{2,1,0:T(8,128)S(1)}, f32[3,128,512]{2,1,0:T(8,128)S(1)}, u32[]{:S(2)}, u32[]{:S(2)}) collective-permute-start(f32[3,128,512]{2,1,0:T(8,128)S(1)} %get-tuple-element.90), channel_id=1, source_target_pairs={{0,4},{4,0},{1,5},{5,1},{2,6},{6,2},{3,7},{7,3},{8,12},{12,8},{9,1... | collective-permute-start | bytes 2359304 | tf_op jit(solution)/shard_map/ppermute | solution.py:295
  94.0 9.5 %collective-permute-start.5 = (f32[136,128]{1,0:T(8,128)S(1)}, f32[136,128]{1,0:T(8,128)S(1)}, u32[]{:S(2)}, u32[]{:S(2)}) collective-permute-start(f32[136,128]{1,0:T(8,128)S(1)} %shard_map.129.mine_ref), channel_id=1, source_target_pairs={{0,96},{4,36},{32,64},{36,4},{64,32},{68,100},{96,0},{100,68},{1,9... | collective-permute-start | bytes 208904 | tf_op jit(solution)/shard_map/ppermute | solution.py:300
  104.2 13.1 %all-to-all-start.3 = ((f32[16,32,128]{2,1,0:T(8,128)}), f32[16,32,128]{2,1,0:T(8,128)S(1)}, u32[]{:S(2)}, u32[]{:S(2)}) async-start(f32[16,32,128]{2,1,0:T(8,128)} %get-tuple-element.102), calls=%async_computation.3 | async-start | bytes 524288 | tf_op jit(solution)/shard_map/all_to_all | solution.py:304
  117.3 5.5 %collective-permute-start.7 = (f32[528,128]{1,0:T(8,128)S(1)}, f32[528,128]{1,0:T(8,128)S(1)}, u32[]{:S(2)}, u32[]{:S(2)}) collective-permute-start(f32[528,128]{1,0:T(8,128)S(1)} %shard_map.133), channel_id=1, source_target_pairs={{0,4},{4,0},{1,5},{5,1},{2,6},{6,2},{3,7},{7,3},{8,12},{12,8},{9,1... | collective-permute-start | bytes 811016 | tf_op jit(solution)/shard_map/ppermute | solution.py:295

commit v5 on v4

--- a/solution.py
+++ b/solution.py
@@ -5,7 +5,6 @@
 from jax import lax
 from jax.experimental import pallas as pl
 from jax.experimental.pallas import tpu as pltpu
-from jax.sharding import Mesh
 from jax.sharding import PartitionSpec as P
 
 HEAD_DIM = 128
@@ -15,6 +14,8 @@
 CORES = 2
 GROUP = 4
 GRAD_ROWS = 8
+ORDER = [(0, 0), (0, 1), (0, 2), (0, 3), (1, 0), (1, 1), (1, 2), (1, 3), (2, 0), (2, 1), (2, 2), (2, 3), (3, 0), (3, 1), (3, 2), (3, 3)]
+SLOT = [[0, 1, 2, 3], [4, 5, 6, 7], [8, 9, 10, 11], [12, 13, 14, 15]]
 STEP_ROW = HALF * HEAD_DIM
 VMEM_LIMIT = 12 * 1024 * 1024
 
@@ -90,14 +91,38 @@
             loc_ref[b, :, there] = dot(w, v, 1, 0)
 
 
-def group_kernel(reverse, rows, x_ref, part_ref, send_ref):
+def place(at_ref):
+    h, core = at_ref[0] // CORES, at_ref[0] % CORES
+    return core, h, h ^ (1 + 2 * core), h ^ (3 - 2 * core)
+
+
+def is_split(core, group):
+    return core == 2
+
+
+def orders(reverse):
     order = list(reversed(range(GROUP))) if reverse else list(range(GROUP))
-    total = jnp.zeros((rows, HEAD_DIM), F32)
+    return order, order[2:] + order[:2]
+
+
+def group_kernel(reverse, rows, at_ref, x_ref, part_ref, send_ref):
+    core, h, _, _ = place(at_ref)
+    split = is_split(core, h)
+    order, turned = orders(reverse)
+    above = jnp.zeros((rows, HEAD_DIM), F32)
     for i, y in enumerate(order):
+        x = [x_ref[SLOT[y][l], :rows] for l in range(GROUP)]
+        part, total = {}, above
         for l in order:
-            part_ref[y * GROUP + l] = total
-            total = total + x_ref[y * GROUP + l, :rows]
-        send_ref[i * rows : (i + 1) * rows] = total
+            part[l] = total
+            total = total + x[l]
+        half = above
+        for k, l in enumerate(turned):
+            part_ref[SLOT[y][l]] = jnp.where(split, half, part[l])
+            half = half + x[l]
+            if k == 1:
+                send_ref[i * rows : (i + 1) * rows] = jnp.where(split, half, total)
+        above = total
     if x_ref.shape[1] > rows:
         grads = x_ref[0, rows:]
         for i in range(1, x_ref.shape[0]):
@@ -105,33 +130,38 @@
         send_ref[GROUP * rows :] = grads
 
 
-def for_group(reverse, rows, ref, i, group, dest):
+def up_to(rows, ref, i):
+    return ref[i * rows : (i + 1) * rows] if i >= 0 else jnp.zeros((rows, HEAD_DIM), F32)
+
+
+def for_group(reverse, rows, ref, i, core, group, dest):
     first = (group > dest) if reverse else (group < dest)
-    up_to = ref[i * rows : (i + 1) * rows]
-    above = ref[(i - 1) * rows : i * rows] if i else jnp.zeros((rows, HEAD_DIM), F32)
-    return jnp.where(first, up_to, above)
-
-
-def partners(at_ref):
-    h, core = at_ref[0] // CORES, at_ref[0] % CORES
-    return h, h ^ (1 + 2 * core), h ^ (3 - 2 * core)
+    with_this = jnp.logical_or(first, is_split(core, group))
+    return jnp.where(with_this, up_to(rows, ref, i), up_to(rows, ref, i - 1))
 
 
 def sum_kernel(reverse, rows, at_ref, mine_ref, near_ref, out_ref):
-    h, near, far = partners(at_ref)
+    core, h, near, far = place(at_ref)
+    to_split = is_split(core, far)
     for i in range(GROUP):
-        own = for_group(reverse, rows, mine_ref, i, h, far)
-        out_ref[i * rows : (i + 1) * rows] = own + for_group(reverse, rows, near_ref, i, near, far)
+        plain = up_to(rows, mine_ref, i) + up_to(rows, near_ref, i)
+        made = for_group(reverse, rows, mine_ref, i, core, h, far)
+        made = made + for_group(reverse, rows, near_ref, i, core, near, far)
+        out_ref[i * rows : (i + 1) * rows] = jnp.where(to_split, plain, made)
     if out_ref.shape[0] > GROUP * rows:
         out_ref[GROUP * rows :] = mine_ref[GROUP * rows :] + near_ref[GROUP * rows :]
 
 
 def offset_kernel(reverse, rows, at_ref, near_ref, far_ref, mine_ref, part_ref, out_ref, *grads_ref):
-    h, near, _ = partners(at_ref)
-    for i, y in enumerate(reversed(range(GROUP)) if reverse else range(GROUP)):
-        offset = for_group(reverse, rows, near_ref, i, near, h) + far_ref[i * rows : (i + 1) * rows]
-        for l in range(GROUP):
-            out_ref[y * GROUP + l] = part_ref[y * GROUP + l] + offset
+    core, h, near, _ = place(at_ref)
+    split = is_split(core, h)
+    order, turned = orders(reverse)
+    for i, y in enumerate(order):
+        offset = for_group(reverse, rows, near_ref, i, core, near, h) + up_to(rows, far_ref, i)
+        halves = [up_to(rows, near_ref, n) + up_to(rows, far_ref, n) for n in (i - 1, i)]
+        halves = [jnp.where(split, half, offset) for half in halves]
+        for k, l in enumerate(turned):
+            out_ref[SLOT[y][l]] = part_ref[SLOT[y][l]] + halves[k // 2]
     if grads_ref:
         grads_ref[0][...] = mine_ref[GROUP * rows :] + far_ref[GROUP * rows :]
 
@@ -290,21 +320,31 @@
 STATE = (HALF, HEAD_DIM, HEAD_DIM)
 
 
-def swap(array, axis="core", step=1):
+def swap(array, axis="seq"):
     n = lax.axis_size(axis)
-    return lax.ppermute(array, axis, [(i, i ^ step) for i in range(n)])
+    return lax.ppermute(array, axis, [(i, i ^ 1) for i in range(n)])
+
+
+def device(ring, y, h, l, core):
+    return (y * ring + (h * GROUP + l) % ring) * CORES + core
 
 
 def group_swap(array, steps):
-    pairs = [(h * CORES + c, (h ^ steps[c]) * CORES + c) for h in range(GROUP) for c in range(CORES)]
-    return lax.ppermute(array, ("h", "core"), pairs)
-
-
-def exchange(array, axis):
-    return lax.all_to_all(array, axis, 0, 0, tiled=True)
-
-
-NEAR = ("y", "l")
+    ring = lax.axis_size("seq") // (GROUP * CORES)
+    pairs = [
+        (device(ring, y, h, l, core), device(ring, y, h ^ steps[core], l, core))
+        for y in range(GROUP) for h in range(GROUP) for l in range(GROUP) for core in range(CORES)
+    ]
+    return lax.ppermute(array, "seq", pairs)
+
+
+def exchange(array):
+    ring = lax.axis_size("seq") // (GROUP * CORES)
+    groups = [
+        [device(ring, y, h, l, core) for y, l in ORDER]
+        for h in range(GROUP) for core in range(CORES)
+    ]
+    return lax.all_to_all(array, "seq", 0, 0, tiled=True, axis_index_groups=groups)
 
 
 def chip_scan(pay, reverse, beside_one, beside_two, given):
@@ -312,20 +352,23 @@
     rows = HALF * HEAD_DIM // members
     extra = pay.shape[1] - rows
     part = (members, rows, HEAD_DIM)
-    at_s = lax.axis_index(("h", "core")).astype(jnp.int32).reshape(1)
-    landed = exchange(pay, NEAR)
+    at = lax.axis_index("seq").astype(jnp.int32)
+    ring = lax.axis_size("seq") // (GROUP * CORES)
+    core = at % CORES
+    at_s = ((at // CORES + ring) % ring // GROUP * CORES + core).reshape(1)
+    landed = exchange(pay)
     if reverse:
         landed, given = lax.optimization_barrier((landed, given))
     sums_shape = (GROUP * rows + extra, HEAD_DIM)
     part_sums, send = call(
-        functools.partial(group_kernel, reverse, rows), [(part, F32), (sums_shape, F32)], landed, scalar=False
+        functools.partial(group_kernel, reverse, rows), [(part, F32), (sums_shape, F32)], at_s, landed
     )
     near, given = lax.optimization_barrier((group_swap(send, (1, 3)), beside_one(given)))
     (both,) = call(functools.partial(sum_kernel, reverse, rows), [(sums_shape, F32)], at_s, send, near)
     far, made = lax.optimization_barrier((group_swap(both, (3, 1)), beside_two(given)))
     outs = [(part, F32)] + ([((extra, HEAD_DIM), F32)] if extra else [])
     sums, *rest = call(functools.partial(offset_kernel, reverse, rows), outs, at_s, near, far, both, part_sums)
-    return exchange(sums, NEAR).reshape(STATE), rest, made
+    return exchange(sums).reshape(STATE), rest, made
 
 
 def per_device(queries, keys, values, grad_out, norm_gain, norm_bias, first_moment, second_moment):
@@ -333,7 +376,7 @@
     half = (rows, HALF_WIDTH)
     members = GROUP * GROUP
     slice_rows = HALF * HEAD_DIM // members
-    core_s = lax.axis_index("core").astype(jnp.int32).reshape(1)
+    core_s = (lax.axis_index("seq").astype(jnp.int32) % CORES).reshape(1)
     by_head = (HEADS_HERE, HEAD_DIM)
     gain, bias = norm_gain.reshape(by_head), norm_bias.reshape(by_head)
 
@@ -385,14 +428,10 @@
 
 
 def solution(mesh):
-    seq, fsdp = mesh.devices.shape
-    fine = Mesh(
-        mesh.devices.reshape(GROUP, seq // (GROUP * GROUP * CORES), GROUP, CORES, fsdp), ("y", "h", "l", "core", "fsdp")
-    )
-    big = P(("y", "h", "l", "core"), "fsdp")
+    big = P("seq", "fsdp")
     return jax.shard_map(
         per_device,
-        mesh=fine,
+        mesh=mesh,
         in_specs=(big, big, big, big, P("fsdp"), P("fsdp"), P(None, "fsdp"), P(None, "fsdp")),
         out_specs=(big, big, big, P("fsdp"), P("fsdp")),
         check_vma=False,

time: 125 us -> 124 us (level)
  no operation moved by 1% of the time
where the time goes in v5:
time: 124 us; the launch traced here: 123 us
  starting transfers between devices  60.2 us (49%)
  blocking collectives  32 us (26%)
  waiting for transfers between devices  20.7 us (17%)
  Pallas kernels  8.21 us (7%)
    ppermute x4, starting transfers between devices, group_swap(): return lax.ppermute(array, 'seq', pairs)  27.1 us
    ppermute x4, starting transfers between devices, swap(): return lax.ppermute(array, axis, [(i, i ^ 1) for i in range(n)])  25.9 us
    all_to_all x2, blocking collectives, exchange(): lax.all_to_all(array, 'seq', 0, 0, tiled=True, axis_index_groups=groups)  23.3 us
    ppermute x4, waiting for transfers between devices, group_swap(): return lax.ppermute(array, 'seq', pairs)  10.3 us
    psum x1, blocking collectives, per_device(): lax.psum(squares, 'fsdp')  8.77 us
    pallas_call x16, Pallas kernels, call(): pl.pallas_call(kernel, out_shape=[jax.ShapeDtypeStruct(s, d) for s, d in...  8.21 us
    all_to_all x2, waiting for transfers between devices, exchange(): lax.all_to_all(array, 'seq', 0, 0, tiled=True, axis_index_groups=groups)  8.16 us
    all_to_all x2, starting transfers between devices, exchange(): lax.all_to_all(array, 'seq', 0, 0, tiled=True, axis_index_groups=groups)  7.2 us
  transfers between devices with their start and end apart: 10, of which 8 were waited for; matrix products, arithmetic and copies ran while one was open for 0% of the time, Pallas kernels for 3%

profile of v5, /device:TPU:1, one launch (start us, length us, event | category | flops | bytes accessed | tf_op | source)
XLA Modules:
  0.0 123.2 jit_solution(8504560131837253397)
XLA Ops:
  0.6 1.1 pad_maximum_fusion.kv_ref
  1.7 0.3 shard_map.119
  2.0 8.8 %collective-permute-start = (f32[4,128,128]{2,1,0:T(8,128)S(1)}, f32[4,128,128]{2,1,0:T(8,128)S(1)}, u32[]{:S(2)}, u32[]{:S(2)}) collective-permute-start(f32[4,128,128]{2,1,0:T(8,128)S(1)} %get-tuple-element.61), channel_id=1, source_target_pairs={{0,4},{4,0},{8,12},{12,8},{16,20},{20,16},{24,28},{28,24},{32,36},... | collective-permute-start | bytes 786440 | tf_op jit(solution)/shard_map/ppermute | solution.py:325
  10.8 1.1 collective-permute-done.b_ref
  12.0 0.7 shard_map.120
  12.7 3.7 %all-to-all-start = ((f32[16,32,128]{2,1,0:T(8,128)}), f32[16,32,128]{2,1,0:T(8,128)S(1)}, u32[]{:S(2)}, u32[]{:S(2)}) async-start(f32[16,32,128]{2,1,0:T(8,128)} %shard_map.120), calls=%async_computation | async-start | bytes 524288 | tf_op jit(solution)/shard_map/all_to_all | solution.py:347
  16.4 0.1 shard_map.122
  16.5 2.3 %collective-permute-start.2 = (f32[4,128,512]{2,1,0:T(8,128)S(1)}, f32[4,128,512]{2,1,0:T(8,128)S(1)}, u32[]{:S(2)}, u32[]{:S(2)}) collective-permute-start(f32[4,128,512]{2,1,0:T(8,128)S(1)} %shard_map.122), channel_id=1, source_target_pairs={{0,4},{4,0},{8,12},{12,8},{16,20},{20,16},{24,28},{28,24},{32,36},... | collective-permute-start | bytes 3145736 | tf_op jit(solution)/shard_map/ppermute | solution.py:325
  18.8 7.5 %all-to-all-done.x_ref = f32[16,32,128]{2,1,0:T(8,128)S(1)} async-done(((f32[16,32,128]{2,1,0:T(8,128)}), f32[16,32,128]{2,1,0:T(8,128)S(1)}, u32[]{:S(2)}, u32[]{:S(2)}) %all-to-all-start) | async-done | bytes 262176 | tf_op jit(solution)/shard_map/all_to_all | solution.py:347
  26.4 9.2 %collective-permute-start.1 = (f32[128,128]{1,0:T(8,128)S(1)}, f32[128,128]{1,0:T(8,128)S(1)}, u32[]{:S(2)}, u32[]{:S(2)}) collective-permute-start(f32[128,128]{1,0:T(8,128)S(1)} %get-tuple-element.62.mine_ref), channel_id=1, source_target_pairs={{0,32},{4,100},{8,40},{12,108},{16,48},{20,116},{24,56},{28,124},{... | collective-permute-start | bytes 196616 | tf_op jit(solution)/shard_map/ppermute | solution.py:338
  35.5 2.9 %collective-permute-done.1.near_ref = f32[128,128]{1,0:T(8,128)S(1)} collective-permute-done((f32[128,128]{1,0:T(8,128)S(1)}, f32[128,128]{1,0:T(8,128)S(1)}, u32[]{:S(2)}, u32[]{:S(2)}) %collective-permute-start.1) | collective-permute-done | bytes 65568 | tf_op jit(solution)/shard_map/ppermute | solution.py:338
  38.5 7.1 %collective-permute-start.3 = (f32[128,128]{1,0:T(8,128)S(1)}, f32[128,128]{1,0:T(8,128)S(1)}, u32[]{:S(2)}, u32[]{:S(2)}) collective-permute-start(f32[128,128]{1,0:T(8,128)S(1)} %shard_map.123.mine_ref), channel_id=1, source_target_pairs={{0,96},{4,36},{8,104},{12,44},{16,112},{20,52},{24,120},{28,60},{3... | collective-permute-start | bytes 196616 | tf_op jit(solution)/shard_map/ppermute | solution.py:338
  45.5 1.0 shard_map.124
  46.6 1.6 %collective-permute-done.3.far_ref = f32[128,128]{1,0:T(8,128)S(1)} collective-permute-done((f32[128,128]{1,0:T(8,128)S(1)}, f32[128,128]{1,0:T(8,128)S(1)}, u32[]{:S(2)}, u32[]{:S(2)}) %collective-permute-start.3) | collective-permute-done | bytes 65568 | tf_op jit(solution)/shard_map/ppermute | solution.py:338
  48.2 11.4 %all_to_all.20 = f32[16,32,128]{2,1,0:T(8,128)S(1)} all-to-all(f32[16,32,128]{2,1,0:T(8,128)S(1)} %shard_map.125), channel_id=1, replica_groups={{0,8,16,24,128,136,144,152,256,264,272,280,384,392,400,408},{4,12,20,28..., dimensions={0} | all-to-all | bytes 524288 | tf_op jit(solution)/shard_map/all_to_all | solution.py:347
  59.6 1.0 shard_map.126
  60.6 11.8 %all_to_all.21.x_ref = f32[16,40,128]{2,1,0:T(8,128)S(1)} all-to-all(f32[16,40,128]{2,1,0:T(8,128)S(1)} %get-tuple-element.73), channel_id=1, replica_groups={{0,8,16,24,128,136,144,152,256,264,272,280,384,392,400,408},{4,12,20,28..., dimensions={0} | all-to-all | bytes 655360 | tf_op jit(solution)/shard_map/all_to_all | solution.py:347
  72.5 6.8 %collective-permute-start.4 = (f32[136,128]{1,0:T(8,128)S(1)}, f32[136,128]{1,0:T(8,128)S(1)}, u32[]{:S(2)}, u32[]{:S(2)}) collective-permute-start(f32[136,128]{1,0:T(8,128)S(1)} %get-tuple-element.77.mine_ref), channel_id=1, source_target_pairs={{0,32},{4,100},{8,40},{12,108},{16,48},{20,116},{24,56},{28,124},{... | collective-permute-start | bytes 208904 | tf_op jit(solution)/shard_map/ppermute | solution.py:338
  79.3 2.2 %shard_map.128 = (bf16[128,512]{1,0:T(8,128)(2,1)S(1)}, f32[128,512]{1,0:T(8,128)S(1)}, f32[128,512]{1,0:T(8,128)S(1)}, f32[3,128,512]{2,1,0:T(8,128)S(1)}, f32[...) custom-call(s32[1]{0:T(128)} %bitcast.1.core_ref, ...), custom_call_target="tpu_custom_call" | custom-call | tf_op jit(solution)/shard_map/pallas_call | solution.py:311
  81.5 1.2 collective-permute-done.4.near_ref
  82.7 10.5 %collective-permute-start.6 = (f32[3,128,512]{2,1,0:T(8,128)S(1)}, f32[3,128,512]{2,1,0:T(8,128)S(1)}, u32[]{:S(2)}, u32[]{:S(2)}) collective-permute-start(f32[3,128,512]{2,1,0:T(8,128)S(1)} %get-tuple-element.90), channel_id=1, source_target_pairs={{0,4},{4,0},{8,12},{12,8},{16,20},{20,16},{24,28},{28,24},{32,36},... | collective-permute-start | bytes 2359304 | tf_op jit(solution)/shard_map/ppermute | solution.py:325
  93.2 4.1 %collective-permute-start.5 = (f32[136,128]{1,0:T(8,128)S(1)}, f32[136,128]{1,0:T(8,128)S(1)}, u32[]{:S(2)}, u32[]{:S(2)}) collective-permute-start(f32[136,128]{1,0:T(8,128)S(1)} %shard_map.129.mine_ref), channel_id=1, source_target_pairs={{0,96},{4,36},{8,104},{12,44},{16,112},{20,52},{24,120},{28,60},{3... | collective-permute-start | bytes 208904 | tf_op jit(solution)/shard_map/ppermute | solution.py:338
  97.2 0.7 shard_map.130
  98.0 4.7 %collective-permute-done.5.far_ref = f32[136,128]{1,0:T(8,128)S(1)} collective-permute-done((f32[136,128]{1,0:T(8,128)S(1)}, f32[136,128]{1,0:T(8,128)S(1)}, u32[]{:S(2)}, u32[]{:S(2)}) %collective-permute-start.5) | collective-permute-done | bytes 69664 | tf_op jit(solution)/shard_map/ppermute | solution.py:338
  102.6 0.7 shard_map.131
  103.4 3.5 %all-to-all-start.3 = ((f32[16,32,128]{2,1,0:T(8,128)}), f32[16,32,128]{2,1,0:T(8,128)S(1)}, u32[]{:S(2)}, u32[]{:S(2)}) async-start(f32[16,32,128]{2,1,0:T(8,128)} %get-tuple-element.102), calls=%async_computation.3 | async-start | bytes 524288 | tf_op jit(solution)/shard_map/all_to_all | solution.py:347
  106.9 0.1 shard_map.132
  107.0 8.8 %psum.7.squares_ref = f32[8,128]{1,0:T(8,128)S(1)} all-reduce(f32[8,128]{1,0:T(8,128)S(1)} %get-tuple-element.105), channel_id=1, replica_groups=mesh['seq'=128,'fsdp'=4] {'fsdp'}, use_global_device_ids=true, to_apply=%region_0.1 | all-reduce | flops 1024 | bytes 8192 | tf_op jit(solution)/shard_map/psum | solution.py:420
  115.8 0.7 all-to-all-done.3
  116.5 4.3 %collective-permute-start.7 = (f32[528,128]{1,0:T(8,128)S(1)}, f32[528,128]{1,0:T(8,128)S(1)}, u32[]{:S(2)}, u32[]{:S(2)}) collective-permute-start(f32[528,128]{1,0:T(8,128)S(1)} %shard_map.133), channel_id=1, source_target_pairs={{0,4},{4,0},{8,12},{12,8},{16,20},{20,16},{24,28},{28,24},{32,36},... | collective-permute-start | bytes 811016 | tf_op jit(solution)/shard_map/ppermute | solution.py:325
  120.8 1.2 collective-permute-done.7.far_ref
  122.0 1.2 shard_map.134
  (24 shorter events, 0.2 us)
Async XLA Ops:
  2.0 9.9 %collective-permute-start = (f32[4,128,128]{2,1,0:T(8,128)S(1)}, f32[4,128,128]{2,1,0:T(8,128)S(1)}, u32[]{:S(2)}, u32[]{:S(2)}) collective-permute-start(f32[4,128,128]{2,1,0:T(8,128)S(1)} %get-tuple-element.61), channel_id=1, source_target_pairs={{0,4},{4,0},{8,12},{12,8},{16,20},{20,16},{24,28},{28,24},{32,36},... | collective-permute-start | bytes 786440 | tf_op jit(solution)/shard_map/ppermute | solution.py:325
  12.0 4.4 %copy-start.2 = (bf16[128,1024]{1,0:T(8,128)(2,1)S(1)}, bf16[128,1024]{1,0:T(8,128)(2,1)}, u32[]{:S(2)}) copy-start(bf16[128,1024]{1,0:T(8,128)(2,1)} %q_ref.3) | copy-start | bytes 786436
  12.0 4.4 %copy-start.3 = (bf16[128,1024]{1,0:T(8,128)(2,1)S(1)}, bf16[128,1024]{1,0:T(8,128)(2,1)}, u32[]{:S(2)}) copy-start(bf16[128,1024]{1,0:T(8,128)(2,1)} %g_ref.3) | copy-start | bytes 786436
  12.7 3.7 %copy-start = (bf16[128,1024]{1,0:T(8,128)(2,1)S(1)}, bf16[128,1024]{1,0:T(8,128)(2,1)}, u32[]{:S(2)}) copy-start(bf16[128,1024]{1,0:T(8,128)(2,1)} %k_ref.5) | copy-start | bytes 786436
  12.7 3.7 %copy-start.1 = (bf16[128,1024]{1,0:T(8,128)(2,1)S(1)}, bf16[128,1024]{1,0:T(8,128)(2,1)}, u32[]{:S(2)}) copy-start(bf16[128,1024]{1,0:T(8,128)(2,1)} %v_ref.5) | copy-start | bytes 786436
  12.7 13.6 %all-to-all-start = ((f32[16,32,128]{2,1,0:T(8,128)}), f32[16,32,128]{2,1,0:T(8,128)S(1)}, u32[]{:S(2)}, u32[]{:S(2)}) async-start(f32[16,32,128]{2,1,0:T(8,128)} %shard_map.120), calls=%async_computation | async-start | bytes 524288 | tf_op jit(solution)/shard_map/all_to_all | solution.py:347
  16.5 19.0 %collective-permute-start.2 = (f32[4,128,512]{2,1,0:T(8,128)S(1)}, f32[4,128,512]{2,1,0:T(8,128)S(1)}, u32[]{:S(2)}, u32[]{:S(2)}) collective-permute-start(f32[4,128,512]{2,1,0:T(8,128)S(1)} %shard_map.122), channel_id=1, source_target_pairs={{0,4},{4,0},{8,12},{12,8},{16,20},{20,16},{24,28},{28,24},{32,36},... | collective-permute-start | bytes 3145736 | tf_op jit(solution)/shard_map/ppermute | solution.py:325
  26.4 12.1 %collective-permute-start.1 = (f32[128,128]{1,0:T(8,128)S(1)}, f32[128,128]{1,0:T(8,128)S(1)}, u32[]{:S(2)}, u32[]{:S(2)}) collective-permute-start(f32[128,128]{1,0:T(8,128)S(1)} %get-tuple-element.62.mine_ref), channel_id=1, source_target_pairs={{0,32},{4,100},{8,40},{12,108},{16,48},{20,116},{24,56},{28,124},{... | collective-permute-start | bytes 196616 | tf_op jit(solution)/shard_map/ppermute | solution.py:338
  38.5 9.7 %collective-permute-start.3 = (f32[128,128]{1,0:T(8,128)S(1)}, f32[128,128]{1,0:T(8,128)S(1)}, u32[]{:S(2)}, u32[]{:S(2)}) collective-permute-start(f32[128,128]{1,0:T(8,128)S(1)} %shard_map.123.mine_ref), channel_id=1, source_target_pairs={{0,96},{4,36},{8,104},{12,44},{16,112},{20,52},{24,120},{28,60},{3... | collective-permute-start | bytes 196616 | tf_op jit(solution)/shard_map/ppermute | solution.py:338
  48.2 11.4 %copy-start.4 = (f32[1024]{0:T(1024)S(1)}, f32[1024]{0:T(1024)}, u32[]{:S(2)}) copy-start(f32[1024]{0:T(1024)} %param.12) | copy-start | bytes 12292
  72.4 6.8 %copy-start.5 = (f32[1024]{0:T(1024)S(1)}, f32[1024]{0:T(1024)}, u32[]{:S(2)}) copy-start(f32[1024]{0:T(1024)} %param.13) | copy-start | bytes 12292
  72.4 6.9 %copy-start.6 = (f32[2,1024]{1,0:T(2,128)S(1)}, f32[2,1024]{1,0:T(2,128)}, u32[]{:S(2)}) copy-start(f32[2,1024]{1,0:T(2,128)} %first_ref.1) | copy-start | bytes 24580
  72.4 6.9 %copy-start.7 = (f32[2,1024]{1,0:T(2,128)S(1)}, f32[2,1024]{1,0:T(2,128)}, u32[]{:S(2)}) copy-start(f32[2,1024]{1,0:T(2,128)} %second_ref.1) | copy-start | bytes 24580
  72.5 10.2 %collective-permute-start.4 = (f32[136,128]{1,0:T(8,128)S(1)}, f32[136,128]{1,0:T(8,128)S(1)}, u32[]{:S(2)}, u32[]{:S(2)}) collective-permute-start(f32[136,128]{1,0:T(8,128)S(1)} %get-tuple-element.77.mine_ref), channel_id=1, source_target_pairs={{0,32},{4,100},{8,40},{12,108},{16,48},{20,116},{24,56},{28,124},{... | collective-permute-start | bytes 208904 | tf_op jit(solution)/shard_map/ppermute | solution.py:338
  82.7 14.6 %collective-permute-start.6 = (f32[3,128,512]{2,1,0:T(8,128)S(1)}, f32[3,128,512]{2,1,0:T(8,128)S(1)}, u32[]{:S(2)}, u32[]{:S(2)}) collective-permute-start(f32[3,128,512]{2,1,0:T(8,128)S(1)} %get-tuple-element.90), channel_id=1, source_target_pairs={{0,4},{4,0},{8,12},{12,8},{16,20},{20,16},{24,28},{28,24},{32,36},... | collective-permute-start | bytes 2359304 | tf_op jit(solution)/shard_map/ppermute | solution.py:325
  93.2 9.5 %collective-permute-start.5 = (f32[136,128]{1,0:T(8,128)S(1)}, f32[136,128]{1,0:T(8,128)S(1)}, u32[]{:S(2)}, u32[]{:S(2)}) collective-permute-start(f32[136,128]{1,0:T(8,128)S(1)} %shard_map.129.mine_ref), channel_id=1, source_target_pairs={{0,96},{4,36},{8,104},{12,44},{16,112},{20,52},{24,120},{28,60},{3... | collective-permute-start | bytes 208904 | tf_op jit(solution)/shard_map/ppermute | solution.py:338
  103.4 13.1 %all-to-all-start.3 = ((f32[16,32,128]{2,1,0:T(8,128)}), f32[16,32,128]{2,1,0:T(8,128)S(1)}, u32[]{:S(2)}, u32[]{:S(2)}) async-start(f32[16,32,128]{2,1,0:T(8,128)} %get-tuple-element.102), calls=%async_computation.3 | async-start | bytes 524288 | tf_op jit(solution)/shard_map/all_to_all | solution.py:347
  116.5 5.5 %collective-permute-start.7 = (f32[528,128]{1,0:T(8,128)S(1)}, f32[528,128]{1,0:T(8,128)S(1)}, u32[]{:S(2)}, u32[]{:S(2)}) collective-permute-start(f32[528,128]{1,0:T(8,128)S(1)} %shard_map.133), channel_id=1, source_target_pairs={{0,4},{4,0},{8,12},{12,8},{16,20},{20,16},{24,28},{28,24},{32,36},... | collective-permute-start | bytes 811016 | tf_op jit(solution)/shard_map/ppermute | solution.py:325

commit v6 on v4

--- a/solution.py
+++ b/solution.py
@@ -74,7 +74,7 @@
         send_ref[i] = ref[:, at].astype(F32)
 
 
-def local_kernel(core_ref, q_ref, k_ref, v_ref, g_ref, recv_ref, in_ref, loc_ref, first_ref):
+def local_kernel(core_ref, q_ref, k_ref, v_ref, g_ref, recv_ref, in_ref, loc_ref, first_ref, bias_ref):
     core = core_ref[0]
     causal = causal_mask()
     at = half_at(core)
@@ -84,6 +84,8 @@
     for j in range(HALF):
         there = fixed(j)
         first_ref[j] = dot(in_ref[core, 1, :, there], in_ref[core, 2, :, there], 0, 0)
+        grad_f = in_ref[0, 3, :, there].astype(F32) + in_ref[1, 3, :, there].astype(F32)
+        bias_ref[j : j + 1] = jnp.sum(grad_f, axis=0, keepdims=True)
         for b in range(CORES):
             q, k, v = (in_ref[b, i, :, there] for i in range(3))
             w = jnp.where(causal, dot(q, k, 1, 1), 0.0).astype(BF16)
@@ -136,15 +138,15 @@
         grads_ref[0][...] = mine_ref[GROUP * rows :] + far_ref[GROUP * rows :]
 
 
-def norm_kernel(core_ref, in_ref, gain_ref, loc_ref, before_ref, first_ref, state_ref, dout_ref, pay_ref):
+def norm_kernel(core_ref, in_ref, gain_ref, loc_ref, before_ref, first_ref, bias_ref, state_ref, dout_ref, pay_ref):
     core = core_ref[0]
     slices, rows = pay_ref.shape[0] // HALF, pay_ref.shape[1] - GRAD_ROWS
-    gain_rows, bias_rows = [], []
+    gain_rows = []
     for j in range(HALF):
         there = fixed(j)
         gain = gain_ref[pl.ds(core * HALF + j, 1), :]
         before = before_ref[j]
-        pair, gain_row, bias_row = 0.0, 0.0, 0.0
+        pair, gain_row = 0.0, 0.0
         for b in range(CORES):
             state = jnp.where(core != b, before + first_ref[j], before).astype(BF16)
             state_ref[b, j] = state
@@ -163,12 +165,10 @@
             dout_ref[b, :, there] = dout
             pair = pair + dot(q, dout, 0, 0)
             gain_row = gain_row + jnp.sum(grad_f * normed, axis=0, keepdims=True)
-            bias_row = bias_row + jnp.sum(grad_f, axis=0, keepdims=True)
         for i in range(slices):
             pay_ref[j * slices + i, :rows] = pair[i * rows : (i + 1) * rows]
         gain_rows.append(gain_row)
-        bias_rows.append(bias_row)
-    grads = jnp.concatenate(gain_rows + bias_rows, axis=0)
+    grads = jnp.concatenate(gain_rows + [bias_ref[...]], axis=0)
     for s in range(pay_ref.shape[0]):
         pay_ref[s, rows:] = grads
 
@@ -343,7 +343,7 @@
 
     def local_part(recv):
         return call(
-            local_kernel, [((CORES, 4) + half, BF16), ((CORES,) + half, F32), (STATE, F32)],
+            local_kernel, [((CORES, 4) + half, BF16), ((CORES,) + half, F32), (STATE, F32), ((HALF, HEAD_DIM), F32)],
             core_s, queries, keys, values, grad_out, recv,
         )
 
@@ -361,13 +361,13 @@
 
     mine, send = call(pair_kernel, [(STATE, F32)] * 2, core_s, jnp.stack([keys, values]))
     (pay,) = call(add_kernel, [((members, slice_rows, HEAD_DIM), F32)], mine, swap(send), scalar=False)
-    before, _, (both, local, first_state) = chip_scan(pay, False, lambda recv: recv, local_part, share_inputs())
+    before, _, (both, local, first_state, bias_sums) = chip_scan(pay, False, lambda recv: recv, local_part, share_inputs())
 
     pay_shape = (members, slice_rows + GRAD_ROWS, HEAD_DIM)
     state, dout, pay = call(
         norm_kernel,
         [((CORES,) + STATE, BF16), ((CORES,) + half, BF16), (pay_shape, F32)],
-        core_s, both, gain, local, before, first_state,
+        core_s, both, gain, local, before, first_state, bias_sums,
     )
     after, (grads,), (grad_q, gk_own, gv_own, near, own, other, pack) = chip_scan(
         pay, True, lambda tied: near_grads(*tied), lambda tied: share_grads(*tied), (both, dout, state)

time: 125 us -> 125 us (level)
  no operation moved by 1% of the time
where the time goes in v6:
time: 125 us; the launch traced here: 124 us
  starting transfers between devices  60.3 us (48%)
  blocking collectives  32 us (26%)
  waiting for transfers between devices  20.8 us (17%)
  Pallas kernels  8.16 us (7%)
    ppermute x4, starting transfers between devices, group_swap(): return lax.ppermute(array, ('h', 'core'), pairs)  27.2 us
    ppermute x4, starting transfers between devices, swap(): return lax.ppermute(array, axis, [(i, i ^ step) for i in range(n)])  25.9 us
    all_to_all x2, blocking collectives, exchange(): return lax.all_to_all(array, axis, 0, 0, tiled=True)  23.3 us
    ppermute x4, waiting for transfers between devices, group_swap(): return lax.ppermute(array, ('h', 'core'), pairs)  10.3 us
    psum x1, blocking collectives, per_device(): lax.psum(squares, 'fsdp')  8.77 us
    all_to_all x2, waiting for transfers between devices, exchange(): return lax.all_to_all(array, axis, 0, 0, tiled=True)  8.21 us
    pallas_call x16, Pallas kernels, call(): pl.pallas_call(kernel, out_shape=[jax.ShapeDtypeStruct(s, d) for s, d in...  8.16 us
    all_to_all x2, starting transfers between devices, exchange(): return lax.all_to_all(array, axis, 0, 0, tiled=True)  7.2 us
  transfers between devices with their start and end apart: 10, of which 8 were waited for; matrix products, arithmetic and copies ran while one was open for 0% of the time, Pallas kernels for 3%

profile of v6, /device:TPU:1, one launch (start us, length us, event | category | flops | bytes accessed | tf_op | source)
XLA Modules:
  0.0 124.0 jit_solution(15927368562385783785)
XLA Ops:
  0.6 1.1 pad_maximum_fusion.kv_ref
  1.7 0.3 shard_map.119
  2.0 8.8 %collective-permute-start = (f32[4,128,128]{2,1,0:T(8,128)S(1)}, f32[4,128,128]{2,1,0:T(8,128)S(1)}, u32[]{:S(2)}, u32[]{:S(2)}) collective-permute-start(f32[4,128,128]{2,1,0:T(8,128)S(1)} %get-tuple-element.63), channel_id=1, source_target_pairs={{0,4},{4,0},{1,5},{5,1},{2,6},{6,2},{3,7},{7,3},{8,12},{12,8},{9,1... | collective-permute-start | bytes 786440 | tf_op jit(solution)/shard_map/ppermute | solution.py:295
  10.8 1.1 collective-permute-done.b_ref
  12.0 0.7 shard_map.120
  12.7 3.7 %all-to-all-start = ((f32[16,32,128]{2,1,0:T(8,128)}), f32[16,32,128]{2,1,0:T(8,128)S(1)}, u32[]{:S(2)}, u32[]{:S(2)}) async-start(f32[16,32,128]{2,1,0:T(8,128)} %shard_map.120), calls=%async_computation | async-start | bytes 524288 | tf_op jit(solution)/shard_map/all_to_all | solution.py:304
  16.5 2.3 %collective-permute-start.2 = (f32[4,128,512]{2,1,0:T(8,128)S(1)}, f32[4,128,512]{2,1,0:T(8,128)S(1)}, u32[]{:S(2)}, u32[]{:S(2)}) collective-permute-start(f32[4,128,512]{2,1,0:T(8,128)S(1)} %shard_map.122), channel_id=1, source_target_pairs={{0,4},{4,0},{1,5},{5,1},{2,6},{6,2},{3,7},{7,3},{8,12},{12,8},{9,1... | collective-permute-start | bytes 3145736 | tf_op jit(solution)/shard_map/ppermute | solution.py:295
  18.8 7.5 %all-to-all-done.x_ref = f32[16,32,128]{2,1,0:T(8,128)S(1)} async-done(((f32[16,32,128]{2,1,0:T(8,128)}), f32[16,32,128]{2,1,0:T(8,128)S(1)}, u32[]{:S(2)}, u32[]{:S(2)}) %all-to-all-start) | async-done | bytes 262176 | tf_op jit(solution)/shard_map/all_to_all | solution.py:304
  26.4 0.7 copy-done.4
  27.0 9.1 %collective-permute-start.1 = (f32[128,128]{1,0:T(8,128)S(1)}, f32[128,128]{1,0:T(8,128)S(1)}, u32[]{:S(2)}, u32[]{:S(2)}) collective-permute-start(f32[128,128]{1,0:T(8,128)S(1)} %get-tuple-element.64.mine_ref), channel_id=1, source_target_pairs={{0,32},{4,100},{32,0},{36,68},{64,96},{68,36},{96,64},{100,4},{1,3... | collective-permute-start | bytes 196616 | tf_op jit(solution)/shard_map/ppermute | solution.py:300
  36.2 2.9 %collective-permute-done.1.near_ref = f32[128,128]{1,0:T(8,128)S(1)} collective-permute-done((f32[128,128]{1,0:T(8,128)S(1)}, f32[128,128]{1,0:T(8,128)S(1)}, u32[]{:S(2)}, u32[]{:S(2)}) %collective-permute-start.1) | collective-permute-done | bytes 65568 | tf_op jit(solution)/shard_map/ppermute | solution.py:300
  39.1 7.2 %collective-permute-start.3 = (f32[128,128]{1,0:T(8,128)S(1)}, f32[128,128]{1,0:T(8,128)S(1)}, u32[]{:S(2)}, u32[]{:S(2)}) collective-permute-start(f32[128,128]{1,0:T(8,128)S(1)} %shard_map.123.mine_ref), channel_id=1, source_target_pairs={{0,96},{4,36},{32,64},{36,4},{64,32},{68,100},{96,0},{100,68},{1,9... | collective-permute-start | bytes 196616 | tf_op jit(solution)/shard_map/ppermute | solution.py:300
  46.3 1.0 shard_map.124
  47.4 1.6 %collective-permute-done.3.far_ref = f32[128,128]{1,0:T(8,128)S(1)} collective-permute-done((f32[128,128]{1,0:T(8,128)S(1)}, f32[128,128]{1,0:T(8,128)S(1)}, u32[]{:S(2)}, u32[]{:S(2)}) %collective-permute-start.3) | collective-permute-done | bytes 65568 | tf_op jit(solution)/shard_map/ppermute | solution.py:300
  49.0 11.4 %all_to_all.20 = f32[16,32,128]{2,1,0:T(8,128)S(1)} all-to-all(f32[16,32,128]{2,1,0:T(8,128)S(1)} %shard_map.125), channel_id=1, replica_groups=mesh['y'=4,'h'=4,'l'=4,'core'=2,'fsdp'=4] {'y','l'}, dimensions={0} | all-to-all | bytes 524288 | tf_op jit(solution)/shard_map/all_to_all | solution.py:304
  60.4 1.0 shard_map.126
  61.4 11.8 %all_to_all.21.x_ref = f32[16,40,128]{2,1,0:T(8,128)S(1)} all-to-all(f32[16,40,128]{2,1,0:T(8,128)S(1)} %get-tuple-element.77), channel_id=1, replica_groups=mesh['y'=4,'h'=4,'l'=4,'core'=2,'fsdp'=4] {'y','l'}, dimensions={0} | all-to-all | bytes 655360 | tf_op jit(solution)/shard_map/all_to_all | solution.py:304
  73.3 6.8 %collective-permute-start.4 = (f32[136,128]{1,0:T(8,128)S(1)}, f32[136,128]{1,0:T(8,128)S(1)}, u32[]{:S(2)}, u32[]{:S(2)}) collective-permute-start(f32[136,128]{1,0:T(8,128)S(1)} %get-tuple-element.81.mine_ref), channel_id=1, source_target_pairs={{0,32},{4,100},{32,0},{36,68},{64,96},{68,36},{96,64},{100,4},{1,3... | collective-permute-start | bytes 208904 | tf_op jit(solution)/shard_map/ppermute | solution.py:300
  80.1 2.2 %shard_map.128 = (bf16[128,512]{1,0:T(8,128)(2,1)S(1)}, f32[128,512]{1,0:T(8,128)S(1)}, f32[128,512]{1,0:T(8,128)S(1)}, f32[3,128,512]{2,1,0:T(8,128)S(1)}, f32[...) custom-call(s32[1]{0:T(128)} %bitcast.1.core_ref, ...), custom_call_target="tpu_custom_call" | custom-call | tf_op jit(solution)/shard_map/pallas_call | solution.py:281
  82.3 1.2 collective-permute-done.4.near_ref
  83.5 10.5 %collective-permute-start.6 = (f32[3,128,512]{2,1,0:T(8,128)S(1)}, f32[3,128,512]{2,1,0:T(8,128)S(1)}, u32[]{:S(2)}, u32[]{:S(2)}) collective-permute-start(f32[3,128,512]{2,1,0:T(8,128)S(1)} %get-tuple-element.94), channel_id=1, source_target_pairs={{0,4},{4,0},{1,5},{5,1},{2,6},{6,2},{3,7},{7,3},{8,12},{12,8},{9,1... | collective-permute-start | bytes 2359304 | tf_op jit(solution)/shard_map/ppermute | solution.py:295
  94.0 4.1 %collective-permute-start.5 = (f32[136,128]{1,0:T(8,128)S(1)}, f32[136,128]{1,0:T(8,128)S(1)}, u32[]{:S(2)}, u32[]{:S(2)}) collective-permute-start(f32[136,128]{1,0:T(8,128)S(1)} %shard_map.129.mine_ref), channel_id=1, source_target_pairs={{0,96},{4,36},{32,64},{36,4},{64,32},{68,100},{96,0},{100,68},{1,9... | collective-permute-start | bytes 208904 | tf_op jit(solution)/shard_map/ppermute | solution.py:300
  98.0 0.7 shard_map.130
  98.8 4.7 %collective-permute-done.5.far_ref = f32[136,128]{1,0:T(8,128)S(1)} collective-permute-done((f32[136,128]{1,0:T(8,128)S(1)}, f32[136,128]{1,0:T(8,128)S(1)}, u32[]{:S(2)}, u32[]{:S(2)}) %collective-permute-start.5) | collective-permute-done | bytes 69664 | tf_op jit(solution)/shard_map/ppermute | solution.py:300
  103.4 0.7 shard_map.131
  104.2 3.5 %all-to-all-start.3 = ((f32[16,32,128]{2,1,0:T(8,128)}), f32[16,32,128]{2,1,0:T(8,128)S(1)}, u32[]{:S(2)}, u32[]{:S(2)}) async-start(f32[16,32,128]{2,1,0:T(8,128)} %get-tuple-element.106), calls=%async_computation.3 | async-start | bytes 524288 | tf_op jit(solution)/shard_map/all_to_all | solution.py:304
  107.7 0.1 shard_map.132
  107.8 8.8 %psum.7.squares_ref = f32[8,128]{1,0:T(8,128)S(1)} all-reduce(f32[8,128]{1,0:T(8,128)S(1)} %get-tuple-element.109), channel_id=1, replica_groups=mesh['y'=4,'h'=4,'l'=4,'core'=2,'fsdp'=4] {'fsdp'}, use_global_device_ids=true, to_apply=%region_0.0 | all-reduce | flops 1024 | bytes 8192 | tf_op jit(solution)/shard_map/psum | solution.py:377
  116.6 0.7 all-to-all-done.3
  117.3 4.3 %collective-permute-start.7 = (f32[528,128]{1,0:T(8,128)S(1)}, f32[528,128]{1,0:T(8,128)S(1)}, u32[]{:S(2)}, u32[]{:S(2)}) collective-permute-start(f32[528,128]{1,0:T(8,128)S(1)} %shard_map.133), channel_id=1, source_target_pairs={{0,4},{4,0},{1,5},{5,1},{2,6},{6,2},{3,7},{7,3},{8,12},{12,8},{9,1... | collective-permute-start | bytes 811016 | tf_op jit(solution)/shard_map/ppermute | solution.py:295
  121.6 1.2 collective-permute-done.7.far_ref
  122.8 1.2 shard_map.134
  (28 shorter events, 0.3 us)
Async XLA Ops:
  2.0 9.9 %collective-permute-start = (f32[4,128,128]{2,1,0:T(8,128)S(1)}, f32[4,128,128]{2,1,0:T(8,128)S(1)}, u32[]{:S(2)}, u32[]{:S(2)}) collective-permute-start(f32[4,128,128]{2,1,0:T(8,128)S(1)} %get-tuple-element.63), channel_id=1, source_target_pairs={{0,4},{4,0},{1,5},{5,1},{2,6},{6,2},{3,7},{7,3},{8,12},{12,8},{9,1... | collective-permute-start | bytes 786440 | tf_op jit(solution)/shard_map/ppermute | solution.py:295
  11.9 4.4 %copy-start.2 = (bf16[128,1024]{1,0:T(8,128)(2,1)S(1)}, bf16[128,1024]{1,0:T(8,128)(2,1)}, u32[]{:S(2)}) copy-start(bf16[128,1024]{1,0:T(8,128)(2,1)} %q_ref.3) | copy-start | bytes 786436
  11.9 4.4 %copy-start.3 = (bf16[128,1024]{1,0:T(8,128)(2,1)S(1)}, bf16[128,1024]{1,0:T(8,128)(2,1)}, u32[]{:S(2)}) copy-start(bf16[128,1024]{1,0:T(8,128)(2,1)} %g_ref.3) | copy-start | bytes 786436
  12.7 3.7 %copy-start = (bf16[128,1024]{1,0:T(8,128)(2,1)S(1)}, bf16[128,1024]{1,0:T(8,128)(2,1)}, u32[]{:S(2)}) copy-start(bf16[128,1024]{1,0:T(8,128)(2,1)} %k_ref.5) | copy-start | bytes 786436
  12.7 3.7 %copy-start.1 = (bf16[128,1024]{1,0:T(8,128)(2,1)S(1)}, bf16[128,1024]{1,0:T(8,128)(2,1)}, u32[]{:S(2)}) copy-start(bf16[128,1024]{1,0:T(8,128)(2,1)} %v_ref.5) | copy-start | bytes 786436
  12.7 13.6 %all-to-all-start = ((f32[16,32,128]{2,1,0:T(8,128)}), f32[16,32,128]{2,1,0:T(8,128)S(1)}, u32[]{:S(2)}, u32[]{:S(2)}) async-start(f32[16,32,128]{2,1,0:T(8,128)} %shard_map.120), calls=%async_computation | async-start | bytes 524288 | tf_op jit(solution)/shard_map/all_to_all | solution.py:304
  16.5 19.7 %collective-permute-start.2 = (f32[4,128,512]{2,1,0:T(8,128)S(1)}, f32[4,128,512]{2,1,0:T(8,128)S(1)}, u32[]{:S(2)}, u32[]{:S(2)}) collective-permute-start(f32[4,128,512]{2,1,0:T(8,128)S(1)} %shard_map.122), channel_id=1, source_target_pairs={{0,4},{4,0},{1,5},{5,1},{2,6},{6,2},{3,7},{7,3},{8,12},{12,8},{9,1... | collective-permute-start | bytes 3145736 | tf_op jit(solution)/shard_map/ppermute | solution.py:295
  26.3 0.7 copy-start.4
  27.0 12.1 %collective-permute-start.1 = (f32[128,128]{1,0:T(8,128)S(1)}, f32[128,128]{1,0:T(8,128)S(1)}, u32[]{:S(2)}, u32[]{:S(2)}) collective-permute-start(f32[128,128]{1,0:T(8,128)S(1)} %get-tuple-element.64.mine_ref), channel_id=1, source_target_pairs={{0,32},{4,100},{32,0},{36,68},{64,96},{68,36},{96,64},{100,4},{1,3... | collective-permute-start | bytes 196616 | tf_op jit(solution)/shard_map/ppermute | solution.py:300
  39.1 9.8 %copy-start.5 = (f32[16,32,128]{2,1,0:T(8,128)S(1)}, f32[16,32,128]{2,1,0:T(8,128)}, u32[]{:S(2)}) copy-start(f32[16,32,128]{2,1,0:T(8,128)} %copy-done.4) | copy-start | bytes 786436
  39.1 9.8 %collective-permute-start.3 = (f32[128,128]{1,0:T(8,128)S(1)}, f32[128,128]{1,0:T(8,128)S(1)}, u32[]{:S(2)}, u32[]{:S(2)}) collective-permute-start(f32[128,128]{1,0:T(8,128)S(1)} %shard_map.123.mine_ref), channel_id=1, source_target_pairs={{0,96},{4,36},{32,64},{36,4},{64,32},{68,100},{96,0},{100,68},{1,9... | collective-permute-start | bytes 196616 | tf_op jit(solution)/shard_map/ppermute | solution.py:300
  49.0 11.4 %copy-start.6 = (f32[1024]{0:T(1024)S(1)}, f32[1024]{0:T(1024)}, u32[]{:S(2)}) copy-start(f32[1024]{0:T(1024)} %param.12) | copy-start | bytes 12292
  73.2 6.8 %copy-start.7 = (f32[1024]{0:T(1024)S(1)}, f32[1024]{0:T(1024)}, u32[]{:S(2)}) copy-start(f32[1024]{0:T(1024)} %param.13) | copy-start | bytes 12292
  73.2 6.8 %copy-start.8 = (f32[2,1024]{1,0:T(2,128)S(1)}, f32[2,1024]{1,0:T(2,128)}, u32[]{:S(2)}) copy-start(f32[2,1024]{1,0:T(2,128)} %first_ref.1) | copy-start | bytes 24580
  73.2 6.9 %copy-start.9 = (f32[2,1024]{1,0:T(2,128)S(1)}, f32[2,1024]{1,0:T(2,128)}, u32[]{:S(2)}) copy-start(f32[2,1024]{1,0:T(2,128)} %second_ref.1) | copy-start | bytes 24580
  73.3 10.2 %collective-permute-start.4 = (f32[136,128]{1,0:T(8,128)S(1)}, f32[136,128]{1,0:T(8,128)S(1)}, u32[]{:S(2)}, u32[]{:S(2)}) collective-permute-start(f32[136,128]{1,0:T(8,128)S(1)} %get-tuple-element.81.mine_ref), channel_id=1, source_target_pairs={{0,32},{4,100},{32,0},{36,68},{64,96},{68,36},{96,64},{100,4},{1,3... | collective-permute-start | bytes 208904 | tf_op jit(solution)/shard_map/ppermute | solution.py:300
  83.5 14.6 %collective-permute-start.6 = (f32[3,128,512]{2,1,0:T(8,128)S(1)}, f32[3,128,512]{2,1,0:T(8,128)S(1)}, u32[]{:S(2)}, u32[]{:S(2)}) collective-permute-start(f32[3,128,512]{2,1,0:T(8,128)S(1)} %get-tuple-element.94), channel_id=1, source_target_pairs={{0,4},{4,0},{1,5},{5,1},{2,6},{6,2},{3,7},{7,3},{8,12},{12,8},{9,1... | collective-permute-start | bytes 2359304 | tf_op jit(solution)/shard_map/ppermute | solution.py:295
  94.0 9.5 %collective-permute-start.5 = (f32[136,128]{1,0:T(8,128)S(1)}, f32[136,128]{1,0:T(8,128)S(1)}, u32[]{:S(2)}, u32[]{:S(2)}) collective-permute-start(f32[136,128]{1,0:T(8,128)S(1)} %shard_map.129.mine_ref), channel_id=1, source_target_pairs={{0,96},{4,36},{32,64},{36,4},{64,32},{68,100},{96,0},{100,68},{1,9... | collective-permute-start | bytes 208904 | tf_op jit(solution)/shard_map/ppermute | solution.py:300
  104.2 13.1 %all-to-all-start.3 = ((f32[16,32,128]{2,1,0:T(8,128)}), f32[16,32,128]{2,1,0:T(8,128)S(1)}, u32[]{:S(2)}, u32[]{:S(2)}) async-start(f32[16,32,128]{2,1,0:T(8,128)} %get-tuple-element.106), calls=%async_computation.3 | async-start | bytes 524288 | tf_op jit(solution)/shard_map/all_to_all | solution.py:304
  117.3 5.5 %collective-permute-start.7 = (f32[528,128]{1,0:T(8,128)S(1)}, f32[528,128]{1,0:T(8,128)S(1)}, u32[]{:S(2)}, u32[]{:S(2)}) collective-permute-start(f32[528,128]{1,0:T(8,128)S(1)} %shard_map.133), channel_id=1, source_target_pairs={{0,4},{4,0},{1,5},{5,1},{2,6},{6,2},{3,7},{7,3},{8,12},{12,8},{9,1... | collective-permute-start | bytes 811016 | tf_op jit(solution)/shard_map/ppermute | solution.py:295
